TPU v7x, 512 devices: a whole 4x4x16 slice. The times are simulated.
512 devices in a mesh: rep: 16 (over y, x), fsdp: 32 (over z, core).
Axes of the slice: x: 4, y: 4, z: 16, core: 2. Of those that a mesh axis runs over, the one named last changes fastest.
Arguments:
- partials: float32 [16, 32, 64, 4096], P('rep', 'fsdp'), may hold values from -6 to 6
- owner_blocks: int32 [32], replicated, may hold values from 1 to 512, 4096 in all
- momentum: float32 [16, 64, 16384], P('rep', None, 'fsdp'), may hold values from -6 to 6
- weights: float32 [64, 16384], P(None, 'fsdp'), may hold values from -6 to 6
- selected: int32 [16, 32, 16384], P(None, None, 'fsdp'), may hold values from 0 to 63, as said below
Outputs:
- new_momentum: float32 [16, 64, 16384], P('rep', None, 'fsdp')
- new_weights: float32 [64, 16384], P(None, 'fsdp')
Inputs may be any that keep to these rules, and one draw needn't show every extreme that they name: `owner_blocks`: counts of the 32 owners sum to 4096; the largest is exactly 512. `selected`: for each group and slot the 32 listed numbers are distinct; lists of slots that are not live are ignored.
All inputs are finite; a program needn't handle non-finite values.
Results may differ from a plain program's by a relative error of at most 0.00005.
Values sent between devices are 32-bit elements; how exact they have to be, the bound alone decides.
No kernel may reach another device: no remote copies, remote signals or barrier semaphores. Data moves between devices by JAX's collectives and lax.ppermute only.
A program may use at most 64 MiB of HBM per device.

v0:
```python
import jax
import jax.numpy as jnp
from jax import lax
from jax.sharding import PartitionSpec as P

BLOCK = 64


momentum_decay = 0.9
step_rate = 0.5


def dct_matrix():
    row_index = jnp.arange(BLOCK, dtype=jnp.int32)[:, None].astype(jnp.float32)
    column_index = jnp.arange(BLOCK, dtype=jnp.int32)[None, :].astype(jnp.float32)
    norm_factor = jnp.sqrt(jnp.where(row_index == 0.0, 1.0, 2.0) / BLOCK).astype(jnp.float32)
    return norm_factor * jnp.cos(jnp.pi * (2.0 * column_index + 1.0) * row_index / (2.0 * BLOCK))


def body(partials, owner_blocks, momentum, weights, selected):
    owners = lax.axis_size("fsdp")
    groups = lax.axis_size("rep")
    owner = lax.axis_index("fsdp")
    group_number = lax.axis_index("rep")
    partial_value = partials[0, 0]
    total_blocks = partial_value.shape[1]
    most = momentum.shape[2]
    starts = jnp.cumsum(owner_blocks) - owner_blocks
    slots = jnp.arange(most, dtype=jnp.int32)
    in_use = slots < owner_blocks[owner]
    all_use = (slots[None, :] < owner_blocks[:, None]).reshape(-1)
    source = jnp.clip(starts[:, None] + slots[None, :], 0, total_blocks - 1).reshape(-1)
    buffer = jnp.where(all_use[None, :], jnp.take(partial_value, source, axis=1), 0.0)
    summed = lax.psum_scatter(buffer, "fsdp", scatter_dimension=1, tiled=True)
    gradient = jnp.where(in_use[None, :], summed / owners, 0.0)
    accumulated = momentum_decay * momentum[0] + gradient
    dct_table = dct_matrix()
    coeffs = jnp.dot(dct_table, accumulated, precision=lax.Precision.HIGHEST)
    coef_numbers = jnp.arange(BLOCK, dtype=jnp.int32)
    own_lists = lax.dynamic_index_in_dim(selected, group_number, 0, keepdims=False)
    matches = own_lists[:, None, :] == coef_numbers[None, :, None]
    picked = jnp.sum(jnp.where(matches, coeffs[None, :, :], 0.0), axis=1)
    sparse = jnp.where(jnp.any(matches, axis=0), coeffs, 0.0)
    own_part = jnp.dot(dct_table.T, sparse, precision=lax.Precision.HIGHEST)
    new_momentum = jnp.where(in_use[None, :], accumulated - own_part, 0.0)[None]
    received = lax.all_gather(picked[None], "rep", axis=0, tiled=True)

    def add_group(member, partial_sum):
        values = lax.dynamic_index_in_dim(received, member, 0, keepdims=False)
        chosen = lax.dynamic_index_in_dim(selected, member, 0, keepdims=False)
        placed = chosen[:, None, :] == coef_numbers[None, :, None]
        return partial_sum + jnp.sum(jnp.where(placed, values[:, None, :], 0.0), axis=0)

    combined = lax.fori_loop(0, received.shape[0], add_group, jnp.zeros((BLOCK, most), jnp.float32))
    update = jnp.dot(dct_table.T, combined, precision=lax.Precision.HIGHEST) / groups
    new_weights = jnp.where(in_use[None, :], weights - step_rate * update, 0.0)
    return (new_momentum, new_weights)


def solution(mesh):
    placed = (
        P("rep", "fsdp", None, None),
        P(),
        P("rep", None, "fsdp"),
        P(None, "fsdp"),
        P(None, None, "fsdp"),
    )
    return jax.shard_map(
        body,
        mesh=mesh,
        in_specs=placed,
        out_specs=(P("rep", None, "fsdp"), P(None, "fsdp")),
        check_vma=False,
    )
```

profile of v0, /device:TPU:6, one launch (start us, length us, event | category | flops | bytes accessed | tf_op | source)
XLA Modules:
  0.0 303.1 jit_solution(11532232293556834928)
XLA Ops:
  9.8 1.8 copy.14
  11.6 54.4 %gather_fusion = f32[16384,64]{1,0:T(8,128)} fusion(f32[64,4096]{0,1:T(8,128)S(1)} %bitcast.36, s32[16384]{0:T(1024)S(1)} %broadcast_clamp_fusion), kind=kCustom, calls=%fused_computation | custom fusion | bytes 8454144 | tf_op jit(solution)/shard_map/jit(_take)/gather | solution.py:33
  66.0 6.8 %copy.15 = f32[16384,64]{0,1:T(8,128)} copy(f32[16384,64]{1,0:T(8,128)} %gather_fusion) | data formatting | bytes 8388608 | tf_op jit(solution)/shard_map/jit(_take)/gather | solution.py:33
  72.9 4.6 %select_bitcast_fusion = f32[64,16384]{1,0:T(8,128)} fusion(f32[16384,64]{0,1:T(8,128)} %copy.15, pred[16384]{0:T(1024)(128)(4,1)S(1)} %bitcast.41, pred[16384]{0:T(1024)(128)(4,1)S(1)} %compare_and_fusion), kind=kLoop, calls=%fused_computation.7 | loop fusion | flops 2097152 | bytes 8421376 | tf_op jit(solution)/shard_map/jit(_where)/select_n | solution.py:33
  79.5 0.9 dynamic-slice_bitcast_fusion.2
  80.3 115.6 %reduce-scatter.2.cloned.1.call-done = f32[64,512]{1,0:T(8,128)} async-done(((f32[64,16384]{1,0:T(8,128)}), f32[64,512]{1,0:T(8,128)}) %reduce-scatter.2.cloned.1.call-update) | async-done | bytes 131088 | tf_op jit(solution)/shard_map/reduce_scatter | solution.py:34
  195.9 1.3 fusion.12
  197.3 1.3 select_reduce_fusion.1
  199.2 2.1 fusion.4
  201.3 53.6 %all-gather.3.cloned.1.call-done = f32[512,512]{1,0:T(8,128)} async-done(((f32[32,512]{1,0:T(8,128)}), f32[512,512]{1,0:T(8,128)}) %all-gather.3.cloned.1.call-update) | async-done | bytes 1048592 | tf_op jit(solution)/shard_map/all_gather | solution.py:46
  254.9 40.2 %while.14 = (s32[]{:T(128)}, f32[64,512]{1,0:T(8,128)S(1)}, s32[16,32,512]{2,1,0:T(8,128)}, f32[16,32,512]{2,1,0:T(8,128)}, s32[]{:T(128)}, /*index=5*/s32[]{:T(128)}) while((s32[]{:T(128)}, f32[64,512]{1,0:T(8,128)S(1)}, s32[16,32,512]{2,1,0:T(8,128)}, f32[16,32,512]{2,1,0:T(8,128)}, s32[]{:T(128)}, /*index=5*/s32[]{:T(128)}) %tuple.45), condition=%wide.region_6.7_spmd.clone, body=%wide.region_4.6_spmd.clone.sunk | while | flops 3178499 | bytes 917591 | solution.py:54
  255.7 0.8 dynamic-slice_bitcast_fusion.6
  257.4 0.8 dynamic-slice_bitcast_fusion.5
  258.2 0.8 dynamic-slice_bitcast_fusion.6
  259.9 0.8 dynamic-slice_bitcast_fusion.5
  260.7 0.8 dynamic-slice_bitcast_fusion.6
  262.4 0.8 dynamic-slice_bitcast_fusion.5
  263.3 0.8 dynamic-slice_bitcast_fusion.6
  264.9 0.8 dynamic-slice_bitcast_fusion.5
  265.8 0.8 dynamic-slice_bitcast_fusion.6
  267.4 0.8 dynamic-slice_bitcast_fusion.5
  269.9 0.8 dynamic-slice_bitcast_fusion.5
  272.4 0.8 dynamic-slice_bitcast_fusion.5
  275.0 0.8 dynamic-slice_bitcast_fusion.5
  277.5 0.8 dynamic-slice_bitcast_fusion.5
  280.0 0.8 dynamic-slice_bitcast_fusion.5
  282.5 0.8 dynamic-slice_bitcast_fusion.5
  285.0 0.8 dynamic-slice_bitcast_fusion.5
  287.5 0.8 dynamic-slice_bitcast_fusion.5
  290.0 0.8 dynamic-slice_bitcast_fusion.5
  292.5 0.8 dynamic-slice_bitcast_fusion.5
  295.1 1.2 fusion.6
  (72 shorter events, 27.9 us)
Async XLA Ops:
  7.2 188.7 %reduce-scatter.2.cloned.1.call-start = ((), (), s32[]{:S(2)}) async-start(), calls=%async_computation.1 | async-start | bytes 4325376 | tf_op jit(solution)/shard_map/reduce_scatter | solution.py:34
  77.5 0.7 copy-start.2
  77.5 118.4 %copy-start = (f32[1,64,512]{2,1,0:T(8,128)S(1)}, f32[1,64,512]{2,1,0:T(8,128)}, u32[]{:S(2)}) copy-start(f32[1,64,512]{2,1,0:T(8,128)} %param.9) | copy-start | bytes 393220
  77.6 217.5 %copy-start.1 = (f32[64,512]{1,0:T(8,128)S(1)}, f32[64,512]{1,0:T(8,128)}, u32[]{:S(2)}) copy-start(f32[64,512]{1,0:T(8,128)} %param.10) | copy-start | bytes 393220
  77.6 177.3 %all-gather.3.cloned.1.call-start = ((), (), s32[]{:S(2)}) async-start(), calls=%async_computation.2 | async-start | bytes 1114112 | tf_op jit(solution)/shard_map/all_gather | solution.py:46
Sparse Core Ops, SparseCore 0:
  77.7 118.1 reduce-scatter.1
  199.5 55.3 all-gather.2
where the time goes:
time: 305 us; the launch traced here: 303 us
  waiting for transfers between devices  169 us (55%)
  local copies, waits for them, and re-layouts  93 us (30%)
  other arithmetic  21.6 us (7%)
  between operations  14.2 us (5%)
  matrix products  4.58 us (2%)
    reduce_scatter x1, waiting for transfers between devices, body(): summed = lax.psum_scatter(buffer, 'fsdp', scatter_dimension=1, tiled=True)  116 us
    gather x2, local copies, waits for them, and re-layouts, body(): jnp.take(partial_value, source, axis=1)  61.2 us
    all_gather x1, waiting for transfers between devices, body(): received = lax.all_gather(picked[None], 'rep', axis=0, tiled=True)  53.6 us
    broadcast_in_dim x16, local copies, waits for them, and re-layouts, add_group(): jnp.where(placed, values[:, None, :], 0.0)  13.6 us
    eq x16, local copies, waits for them, and re-layouts, add_group(): placed = chosen[:, None, :] == coef_numbers[None, :, None]  13.5 us
    reduce_sum x16, other arithmetic, add_group(): jnp.sum(jnp.where(placed, values[:, None, :], 0.0), axis=0)  12 us
  transfers between devices with their start and end apart: 2, of which 2 were waited for; matrix products, arithmetic and copies ran while one was open for 2% of the time, Pallas kernels for 0%

commit v1 on v0

v1 whole, which is shorter than its diff:
```python
import functools

import jax
import jax.numpy as jnp
import numpy as np
from jax import lax
from jax.experimental import pallas as pl
from jax.experimental.pallas import tpu as pltpu
from jax.sharding import Mesh, PartitionSpec as P

BLOCK = 64
K = 32
BLOCKS = 4096
MOST = 512
OWNERS = 32
GROUPS = 16
NEAR = 8
FAR = OWNERS // NEAR
ROWS = BLOCK // NEAR

REP = ("y", "x")
FSDP = ("zh", "zl", "core")

momentum_decay = 0.9
step_rate = 0.5


def dct_matrix():
    j = np.arange(BLOCK, dtype=np.float64)[:, None]
    v = np.arange(BLOCK, dtype=np.float64)[None, :]
    norm = np.sqrt(np.where(j == 0, 1.0, 2.0) / BLOCK)
    return (norm * np.cos(np.pi * (2 * v + 1) * j / (2 * BLOCK))).astype(np.float32)


def window_kernel(counts_ref, parts_ref, out_ref, total_ref):
    total_ref[:, :BLOCKS] = jnp.sum(parts_ref[...], axis=0)
    total_ref[:, BLOCKS:] = jnp.zeros((ROWS, MOST + 128), jnp.float32)
    lane = lax.broadcasted_iota(jnp.int32, (ROWS, 128), 1)
    start = jnp.int32(0)
    for i in range(OWNERS):
        base = pl.multiple_of((start // 128) * 128, 128)
        shift = start % 128
        tiles = [
            pltpu.roll(total_ref[:, pl.ds(base + 128 * t, 128)], (128 - shift) % 128, 1)
            for t in range(MOST // 128 + 1)
        ]
        for t in range(MOST // 128):
            out_ref[i, :, 128 * t : 128 * (t + 1)] = jnp.where(lane < 128 - shift, tiles[t], tiles[t + 1])
        start = start + counts_ref[i]


def owner_kernel(place_ref, parts_ref, momentum_ref, chosen_ref, table_ref, back_ref, momentum_out_ref, copies_ref):
    count = place_ref[1]
    live = lax.broadcasted_iota(jnp.int32, (BLOCK, MOST), 1) < count
    gradient = jnp.sum(parts_ref[...], axis=0) * (1.0 / OWNERS)
    accumulated = jnp.where(live, momentum_decay * momentum_ref[0] + gradient, 0.0)
    coeffs = jnp.dot(table_ref[...], accumulated, precision=lax.Precision.HIGHEST, preferred_element_type=jnp.float32)
    chosen = chosen_ref[0]
    bit = jnp.left_shift(jnp.int32(1), chosen & 31)
    low = jnp.sum(jnp.where(chosen < 32, bit, 0), axis=0, keepdims=True)
    high = jnp.sum(jnp.where(chosen < 32, 0, bit), axis=0, keepdims=True)
    number = lax.broadcasted_iota(jnp.int32, (32, MOST), 0)
    listed = jnp.concatenate(
        [jnp.right_shift(jnp.broadcast_to(word, (32, MOST)), number) & 1 for word in (low, high)], axis=0
    )
    sparse = jnp.where(listed != 0, coeffs, 0.0)
    own = jnp.dot(back_ref[...], sparse, precision=lax.Precision.HIGHEST, preferred_element_type=jnp.float32)
    momentum_out_ref[0] = jnp.where(live, accumulated - own, 0.0)
    for r in range(GROUPS):
        copies_ref[r] = own


def weights_kernel(place_ref, parts_ref, weights_ref, out_ref):
    live = lax.broadcasted_iota(jnp.int32, (BLOCK, MOST), 1) < place_ref[1]
    update = jnp.sum(parts_ref[...], axis=0) * (1.0 / GROUPS)
    out_ref[...] = jnp.where(live, weights_ref[...] - step_rate * update, 0.0)


def body(partials, owner_blocks, momentum, weights, selected):
    owner = lax.axis_index(FSDP)
    group = lax.axis_index(REP)
    place = jnp.stack([group, owner_blocks[owner]]).astype(jnp.int32)
    whole = pl.BlockSpec(memory_space=pltpu.VMEM)

    near = lax.all_to_all(partials.reshape(NEAR, ROWS, BLOCKS), ("zl", "core"), 0, 0, tiled=False)
    windows = pl.pallas_call(
        window_kernel,
        out_shape=jax.ShapeDtypeStruct((OWNERS, ROWS, MOST), jnp.float32),
        in_specs=[pl.BlockSpec(memory_space=pltpu.SMEM), whole],
        out_specs=whole,
        scratch_shapes=[pltpu.VMEM((ROWS, BLOCKS + MOST + 128), jnp.float32)],
        name="windows",
    )(owner_blocks, near)
    far = lax.all_to_all(windows, FSDP, 0, 0, tiled=False).reshape(FAR, BLOCK, MOST)

    table = dct_matrix()
    new_momentum, copies = pl.pallas_call(
        owner_kernel,
        out_shape=(
            jax.ShapeDtypeStruct((1, BLOCK, MOST), jnp.float32),
            jax.ShapeDtypeStruct((GROUPS, BLOCK, MOST), jnp.float32),
        ),
        grid_spec=pltpu.PrefetchScalarGridSpec(
            num_scalar_prefetch=1,
            grid=(1,),
            in_specs=[
                pl.BlockSpec((FAR, BLOCK, MOST), lambda i, place: (0, 0, 0)),
                pl.BlockSpec((1, BLOCK, MOST), lambda i, place: (0, 0, 0)),
                pl.BlockSpec((1, K, MOST), lambda i, place: (place[0], 0, 0)),
                pl.BlockSpec((BLOCK, BLOCK), lambda i, place: (0, 0)),
                pl.BlockSpec((BLOCK, BLOCK), lambda i, place: (0, 0)),
            ],
            out_specs=[
                pl.BlockSpec((1, BLOCK, MOST), lambda i, place: (0, 0, 0)),
                pl.BlockSpec((GROUPS, BLOCK, MOST), lambda i, place: (0, 0, 0)),
            ],
        ),
        name="owner_step",
    )(place, far, momentum, selected, jnp.asarray(table), jnp.asarray(table.T))
    everyone = lax.all_to_all(copies, REP, 0, 0, tiled=False)
    new_weights = pl.pallas_call(
        weights_kernel,
        out_shape=jax.ShapeDtypeStruct((BLOCK, MOST), jnp.float32),
        in_specs=[pl.BlockSpec(memory_space=pltpu.SMEM), whole, whole],
        out_specs=whole,
        name="weights_step",
    )(place, everyone, weights)
    return new_momentum, new_weights


def solution(mesh):
    fine = Mesh(mesh.devices.reshape(4, 4, FAR, NEAR // 2, 2), REP + FSDP)
    return jax.shard_map(
        body,
        mesh=fine,
        in_specs=(P(REP, FSDP, None, None), P(), P(REP, None, FSDP), P(None, FSDP), P(None, None, FSDP)),
        out_specs=(P(REP, None, FSDP), P(None, FSDP)),
        check_vma=False,
    )
```

time: 305 us -> 126 us (0.41)
  waiting for transfers between devices: 169 us -> 31.9 us
  local copies, waits for them, and re-layouts: 93 us -> 1.38 us
  blocking collectives: 0 us -> 66.1 us
  other arithmetic: 21.6 us -> 1.29 us
  starting transfers between devices: 0.08 us -> 13.7 us
  between operations: 14.2 us -> 0.67 us
  Pallas kernels: 0 us -> 8.81 us
  matrix products: 4.58 us -> 0 us
    reduce_scatter x1 -> x0, waiting for transfers between devices: 116 us -> none  [body(): summed = lax.psum_scatter(buffer, 'fsdp', scatter_dimension=1, tiled=True)]
    all_to_all x0 -> x2, blocking collectives: none -> 66.1 us  [the longest x1 33.5 us: body(): everyone = lax.all_to_all(copies, REP, 0, 0, tiled=False)]
    gather x2 -> x0, local copies, waits for them, and re-layouts: 61.2 us -> none  [body(): jnp.take(partial_value, source, axis=1)]
    all_gather x1 -> x0, waiting for transfers between devices: 53.6 us -> none  [body(): received = lax.all_gather(picked[None], 'rep', axis=0, tiled=True)]
    all_to_all x0 -> x1, waiting for transfers between devices: none -> 31.9 us  [body(): lax.all_to_all(windows, FSDP, 0, 0, tiled=False).reshape(FAR, BLOCK, MOST)]
    eq x17 -> x0, local copies, waits for them, and re-layouts: 14.4 us -> none  [the longest x16 13.5 us: add_group(): placed = chosen[:, None, :] == coef_numbers[None, :, None]]
    all_to_all x0 -> x1, starting transfers between devices: none -> 13.7 us  [body(): lax.all_to_all(windows, FSDP, 0, 0, tiled=False).reshape(FAR, BLOCK, MOST)]
    broadcast_in_dim x16 -> x0, local copies, waits for them, and re-layouts: 13.6 us -> none  [add_group(): jnp.where(placed, values[:, None, :], 0.0)]
  transfers between devices with their start and end apart: 2 -> 1, of which waited for: 2 -> 1; matrix products, arithmetic and copies ran while one was open for 2% -> 2% of each run, Pallas kernels for 0% -> 0%
where the time goes in v1:
time: 126 us; the launch traced here: 124 us
  blocking collectives  66.1 us (52%)
  waiting for transfers between devices  31.9 us (25%)
  starting transfers between devices  13.7 us (11%)
  Pallas kernels  8.81 us (7%)
  local copies, waits for them, and re-layouts  1.38 us (1%)
  other arithmetic  1.29 us (1%)
    all_to_all x1, blocking collectives, body(): everyone = lax.all_to_all(copies, REP, 0, 0, tiled=False)  33.5 us
    all_to_all x1, blocking collectives, body(): lax.all_to_all(partials.reshape(NEAR, ROWS, BLOCKS), ('zl', 'core'), 0, 0...  32.6 us
    all_to_all x1, waiting for transfers between devices, body(): lax.all_to_all(windows, FSDP, 0, 0, tiled=False).reshape(FAR, BLOCK, MOST)  31.9 us
    all_to_all x1, starting transfers between devices, body(): lax.all_to_all(windows, FSDP, 0, 0, tiled=False).reshape(FAR, BLOCK, MOST)  13.7 us
    pallas_call x1, Pallas kernels, body(): pl.pallas_call(owner_kernel, out_shape=(jax.ShapeDtypeStruct((1, BLOCK, M...  3.9 us
    pallas_call x1, Pallas kernels, body(): pl.pallas_call(window_kernel, out_shape=jax.ShapeDtypeStruct((OWNERS, ROW...  2.55 us
  transfers between devices with their start and end apart: 1, of which 1 were waited for; matrix products, arithmetic and copies ran while one was open for 2% of the time, Pallas kernels for 0%

profile of v1, /device:TPU:6, one launch (start us, length us, event | category | flops | bytes accessed | tf_op | source)
XLA Modules:
  0.0 123.8 jit_solution(17153086707441577962)
XLA Ops:
  0.6 0.0 copy-start.1
  0.6 32.6 %all_to_all.15.parts_ref = f32[8,8,4096]{2,1,0:T(8,128)} all-to-all(f32[8,8,4096]{2,1,0:T(8,128)} %bitcast.4), channel_id=1, replica_groups=mesh['y'=4,'x'=4,'zh'=4,'zl'=4,'core'=2] {'zl','core'}, dimensions={0} | all-to-all | bytes 2097152 | tf_op jit(solution)/shard_map/all_to_all | solution.py:85
  33.3 2.5 %windows.1 = f32[32,8,512]{2,1,0:T(8,128)} custom-call(s32[32]{0:T(128)} %counts_ref.1, f32[8,8,4096]{2,1,0:T(8,128)} %all_to_all.15.parts_ref), custom_call_target="tpu_custom_call" | custom-call | tf_op jit(solution)/shard_map/windows/pallas_call | solution.py:86
  35.8 13.7 %all-to-all-start.1 = ((f32[32,8,512]{2,1,0:T(8,128)}), f32[32,8,512]{2,1,0:T(8,128)S(1)}, u32[]{:S(2)}, u32[]{:S(2)}) async-start(f32[32,8,512]{2,1,0:T(8,128)} %windows.1), calls=%async_computation.1 | async-start | bytes 1048576 | tf_op jit(solution)/shard_map/all_to_all | solution.py:94
  49.5 0.0 copy-done.1
  49.5 0.6 dynamic_slice.3
  50.1 1.3 %pad_add_fusion.place_ref = s32[2]{0:T(128)} fusion(s32[1]{0:T(128)} %dynamic_slice.3, s32[1]{0:T(128)} %bitcast), kind=kLoop, calls=%fused_computation | loop fusion | flops 2 | bytes 16 | tf_op jit(solution)/shard_map/stack | solution.py:82
  51.4 31.9 %all-to-all-done.1 = f32[32,8,512]{2,1,0:T(8,128)S(1)} async-done(((f32[32,8,512]{2,1,0:T(8,128)}), f32[32,8,512]{2,1,0:T(8,128)S(1)}, u32[]{:S(2)}, u32[]{:S(2)}) %all-to-all-start.1) | async-done | bytes 524320 | tf_op jit(solution)/shard_map/all_to_all | solution.py:94
  83.3 0.0 copy-start
  83.3 0.8 copy-done
  84.1 3.9 %owner_step.1 = (f32[1,64,512]{2,1,0:T(8,128)}, f32[16,64,512]{2,1,0:T(8,128)}) custom-call(s32[2]{0:T(128)} %pad_add_fusion.place_ref, f32[4,64,512]{2,1,0:T(8,128)} %bitcast.3, f32[1,64,512]{2,1,0:T(8,128)} %momentum_ref.1, s32[16,32,512]{2,1,0:T(8,128)} %chosen_ref.1, f32[64,64]{1,0:T(8,128)} %constant.33.clone.table_ref, f32[64,64]{1,0:T(8,128)} %constant.34.clone.back_ref), custom_call_target="tpu_custom_call" | custom-call | tf_op jit(solution)/shard_map/owner_step/pallas_call | solution.py:97
  88.0 33.5 %all_to_all.16.parts_ref = f32[16,64,512]{2,1,0:T(8,128)} all-to-all(f32[16,64,512]{2,1,0:T(8,128)} %get-tuple-element.5), channel_id=1, replica_groups=mesh['y'=4,'x'=4,'zh'=4,'zl'=4,'core'=2] {'y','x'}, dimensions={0} | all-to-all | bytes 4194304 | tf_op jit(solution)/shard_map/all_to_all | solution.py:120
  121.4 2.4 %weights_step.1 = f32[64,512]{1,0:T(8,128)} custom-call(s32[2]{0:T(128)} %pad_add_fusion.place_ref, f32[16,64,512]{2,1,0:T(8,128)} %all_to_all.16.parts_ref, f32[64,512]{1,0:T(8,128)} %weights_ref.1), custom_call_target="tpu_custom_call" | custom-call | tf_op jit(solution)/shard_map/weights_step/pallas_call | solution.py:121
Async XLA Ops:
  0.6 48.9 %copy-start.1 = (s32[32]{0:T(128)S(1)}, s32[32]{0:T(128)}, u32[]{:S(2)}) copy-start(s32[32]{0:T(128)} %counts_ref.1) | copy-start | bytes 388
  35.8 47.5 %all-to-all-start.1 = ((f32[32,8,512]{2,1,0:T(8,128)}), f32[32,8,512]{2,1,0:T(8,128)S(1)}, u32[]{:S(2)}, u32[]{:S(2)}) async-start(f32[32,8,512]{2,1,0:T(8,128)} %windows.1), calls=%async_computation.1 | async-start | bytes 1048576 | tf_op jit(solution)/shard_map/all_to_all | solution.py:94
  83.3 0.8 copy-start

commit v2 on v1

--- a/solution.py
+++ b/solution.py
@@ -32,7 +32,7 @@
     return (norm * np.cos(np.pi * (2 * v + 1) * j / (2 * BLOCK))).astype(np.float32)
 
 
-def window_kernel(counts_ref, parts_ref, out_ref, total_ref):
+def window_kernel(place_ref, parts_ref, out_ref, total_ref):
     total_ref[:, :BLOCKS] = jnp.sum(parts_ref[...], axis=0)
     total_ref[:, BLOCKS:] = jnp.zeros((ROWS, MOST + 128), jnp.float32)
     lane = lax.broadcasted_iota(jnp.int32, (ROWS, 128), 1)
@@ -46,7 +46,7 @@
         ]
         for t in range(MOST // 128):
             out_ref[i, :, 128 * t : 128 * (t + 1)] = jnp.where(lane < 128 - shift, tiles[t], tiles[t + 1])
-        start = start + counts_ref[i]
+        start = start + place_ref[2 + i]
 
 
 def owner_kernel(place_ref, parts_ref, momentum_ref, chosen_ref, table_ref, back_ref, momentum_out_ref, copies_ref):
@@ -79,7 +79,7 @@
 def body(partials, owner_blocks, momentum, weights, selected):
     owner = lax.axis_index(FSDP)
     group = lax.axis_index(REP)
-    place = jnp.stack([group, owner_blocks[owner]]).astype(jnp.int32)
+    place = jnp.concatenate([jnp.stack([group, owner_blocks[owner]]).astype(jnp.int32), owner_blocks])
     whole = pl.BlockSpec(memory_space=pltpu.VMEM)
 
     near = lax.all_to_all(partials.reshape(NEAR, ROWS, BLOCKS), ("zl", "core"), 0, 0, tiled=False)
@@ -89,8 +89,9 @@
         in_specs=[pl.BlockSpec(memory_space=pltpu.SMEM), whole],
         out_specs=whole,
         scratch_shapes=[pltpu.VMEM((ROWS, BLOCKS + MOST + 128), jnp.float32)],
+        compiler_params=pltpu.CompilerParams(vmem_limit_bytes=8 << 20),
         name="windows",
-    )(owner_blocks, near)
+    )(place, near)
     far = lax.all_to_all(windows, FSDP, 0, 0, tiled=False).reshape(FAR, BLOCK, MOST)
 
     table = dct_matrix()
@@ -115,6 +116,7 @@
                 pl.BlockSpec((GROUPS, BLOCK, MOST), lambda i, place: (0, 0, 0)),
             ],
         ),
+        compiler_params=pltpu.CompilerParams(vmem_limit_bytes=16 << 20),
         name="owner_step",
     )(place, far, momentum, selected, jnp.asarray(table), jnp.asarray(table.T))
     everyone = lax.all_to_all(copies, REP, 0, 0, tiled=False)
@@ -123,6 +125,7 @@
         out_shape=jax.ShapeDtypeStruct((BLOCK, MOST), jnp.float32),
         in_specs=[pl.BlockSpec(memory_space=pltpu.SMEM), whole, whole],
         out_specs=whole,
+        compiler_params=pltpu.CompilerParams(vmem_limit_bytes=8 << 20),
         name="weights_step",
     )(place, everyone, weights)
     return new_momentum, new_weights

time: 126 us -> 120 us (0.952)
  blocking collectives: 66.1 us -> 79.9 us
  starting transfers between devices: 13.7 us -> 6.04 us
  waiting for transfers between devices: 31.9 us -> 25.3 us
  Pallas kernels: 8.81 us -> 4.29 us
    all_to_all x1, blocking collectives: 32.6 us -> 46.6 us  [body(): lax.all_to_all(windows, FSDP, 0, 0, tiled=False).reshape(FAR, BLOCK, MOST)]
    all_to_all x1, starting transfers between devices: 13.7 us -> 6.04 us  [body(): lax.all_to_all(partials.reshape(NEAR, ROWS, BLOCKS), ('zl', 'core'), 0, 0...]
    all_to_all x1, waiting for transfers between devices: 31.9 us -> 25.3 us  [body(): lax.all_to_all(partials.reshape(NEAR, ROWS, BLOCKS), ('zl', 'core'), 0, 0...]
    pallas_call x1, Pallas kernels: 3.9 us -> 1.95 us  [body(): pl.pallas_call(owner_kernel, out_shape=(jax.ShapeDtypeStruct((1, BLOCK, M...]
    pallas_call x1, Pallas kernels: 2.55 us -> 1.04 us  [body(): pl.pallas_call(window_kernel, out_shape=jax.ShapeDtypeStruct((OWNERS, ROW...]
    another operation x1 -> x0, other arithmetic: 1.29 us -> none  [body(): place = jnp.stack([group, owner_blocks[owner]]).astype(jnp.int32)]
  transfers between devices with their start and end apart: 1 -> 1, of which waited for: 1 -> 1; matrix products, arithmetic and copies ran while one was open for 2% -> 1% of each run, Pallas kernels for 0% -> 0%
where the time goes in v2:
time: 120 us; the launch traced here: 118 us
  blocking collectives  79.9 us (67%)
  waiting for transfers between devices  25.3 us (21%)
  starting transfers between devices  6.04 us (5%)
  Pallas kernels  4.29 us (4%)
    all_to_all x1, blocking collectives, body(): lax.all_to_all(windows, FSDP, 0, 0, tiled=False).reshape(FAR, BLOCK, MOST)  46.6 us
    all_to_all x1, blocking collectives, body(): everyone = lax.all_to_all(copies, REP, 0, 0, tiled=False)  33.3 us
    all_to_all x1, waiting for transfers between devices, body(): lax.all_to_all(partials.reshape(NEAR, ROWS, BLOCKS), ('zl', 'core'), 0, 0...  25.3 us
    all_to_all x1, starting transfers between devices, body(): lax.all_to_all(partials.reshape(NEAR, ROWS, BLOCKS), ('zl', 'core'), 0, 0...  6.04 us
  transfers between devices with their start and end apart: 1, of which 1 were waited for; matrix products, arithmetic and copies ran while one was open for 1% of the time, Pallas kernels for 0%

profile of v2, /device:TPU:6, one launch (start us, length us, event | category | flops | bytes accessed | tf_op | source)
XLA Modules:
  0.0 117.6 jit_solution(5805263828560756149)
XLA Ops:
  0.6 0.0 copy-start.5
  0.6 0.0 copy-start
  0.7 0.0 copy-start.2
  0.7 0.0 copy-start.3
  0.7 0.0 copy-start.4
  0.7 6.0 %all-to-all-start = ((f32[8,8,4096]{2,1,0:T(8,128)}), f32[8,8,4096]{2,1,0:T(8,128)S(1)}, u32[]{:S(2)}, u32[]{:S(2)}) async-start(f32[8,8,4096]{2,1,0:T(8,128)} %bitcast.4), calls=%async_computation | async-start | bytes 2097152 | tf_op jit(solution)/shard_map/all_to_all | solution.py:85
  6.7 0.0 copy-done.5
  6.7 0.6 dynamic_slice.3
  7.3 0.7 pad_add_fusion.place_ref
  8.0 25.3 %all-to-all-done.parts_ref = f32[8,8,4096]{2,1,0:T(8,128)S(1)} async-done(((f32[8,8,4096]{2,1,0:T(8,128)}), f32[8,8,4096]{2,1,0:T(8,128)S(1)}, u32[]{:S(2)}, u32[]{:S(2)}) %all-to-all-start) | async-done | bytes 1048608 | tf_op jit(solution)/shard_map/all_to_all | solution.py:85
  33.3 1.0 windows.1
  34.4 46.6 %all_to_all.15 = f32[32,8,512]{2,1,0:T(8,128)S(1)} all-to-all(f32[32,8,512]{2,1,0:T(8,128)S(1)} %windows.1), channel_id=1, replica_groups=mesh['y'=4,'x'=4,'zh'=4,'zl'=4,'core'=2] {'zh','zl','core'}, dimensions={0} | all-to-all | bytes 1048576 | tf_op jit(solution)/shard_map/all_to_all | solution.py:95
  81.0 0.0 copy-done
  81.0 0.0 copy-done.2
  81.0 0.0 copy-done.3
  81.0 0.0 copy-done.4
  81.0 1.9 %owner_step.1 = (f32[1,64,512]{2,1,0:T(8,128)}, f32[16,64,512]{2,1,0:T(8,128)S(1)}) custom-call(s32[34]{0:T(128)S(1)} %pad_add_fusion.place_ref, f32[4,64,512]{2,1,0:T(8,128)S(1)} %bitcast.3, f32[1,64,512]{2,1,0:T(8,128)S(1)} %copy-done.2, s32[16,32,512]{2,1,0:T(8,128)S(1)} %copy-done, f32[64,64]{1,0:T(8,128)S(1)} %copy-done.4, f32[64,64]{1,0:T(8,128)S(1)} %copy-done.3), custom_call_target="tpu_custom_call" | custom-call | tf_op jit(solution)/shard_map/owner_step/pallas_call | solution.py:98
  83.0 0.0 copy-start.1
  83.0 33.3 %all_to_all.16.parts_ref = f32[16,64,512]{2,1,0:T(8,128)S(1)} all-to-all(f32[16,64,512]{2,1,0:T(8,128)S(1)} %get-tuple-element.5), channel_id=1, replica_groups=mesh['y'=4,'x'=4,'zh'=4,'zl'=4,'core'=2] {'y','x'}, dimensions={0} | all-to-all | bytes 4194304 | tf_op jit(solution)/shard_map/all_to_all | solution.py:122
  116.3 0.0 copy-done.1
  116.3 1.3 %weights_step.1 = f32[64,512]{1,0:T(8,128)} custom-call(s32[34]{0:T(128)S(1)} %pad_add_fusion.place_ref, f32[16,64,512]{2,1,0:T(8,128)S(1)} %all_to_all.16.parts_ref, f32[64,512]{1,0:T(8,128)S(1)} %copy-done.1), custom_call_target="tpu_custom_call" | custom-call | tf_op jit(solution)/shard_map/weights_step/pallas_call | solution.py:123
Async XLA Ops:
  0.6 6.1 %copy-start.5 = (s32[32]{0:T(128)S(1)}, s32[32]{0:T(128)}, u32[]{:S(2)}) copy-start(s32[32]{0:T(128)} %param.8) | copy-start | bytes 388
  0.6 80.4 %copy-start = (s32[16,32,512]{2,1,0:T(8,128)S(1)}, s32[16,32,512]{2,1,0:T(8,128)}, u32[]{:S(2)}) copy-start(s32[16,32,512]{2,1,0:T(8,128)} %chosen_ref.1) | copy-start | bytes 3145732
  0.7 80.3 %copy-start.2 = (f32[1,64,512]{2,1,0:T(8,128)S(1)}, f32[1,64,512]{2,1,0:T(8,128)}, u32[]{:S(2)}) copy-start(f32[1,64,512]{2,1,0:T(8,128)} %momentum_ref.1) | copy-start | bytes 393220
  0.7 80.3 %copy-start.3 = (f32[64,64]{1,0:T(8,128)S(1)}, f32[64,64]{1,0:T(8,128)}, u32[]{:S(2)}) copy-start(f32[64,64]{1,0:T(8,128)} %constant.34.clone.back_ref) | copy-start | bytes 49156
  0.7 80.3 %copy-start.4 = (f32[64,64]{1,0:T(8,128)S(1)}, f32[64,64]{1,0:T(8,128)}, u32[]{:S(2)}) copy-start(f32[64,64]{1,0:T(8,128)} %constant.33.clone.table_ref) | copy-start | bytes 49156
  0.7 32.6 %all-to-all-start = ((f32[8,8,4096]{2,1,0:T(8,128)}), f32[8,8,4096]{2,1,0:T(8,128)S(1)}, u32[]{:S(2)}, u32[]{:S(2)}) async-start(f32[8,8,4096]{2,1,0:T(8,128)} %bitcast.4), calls=%async_computation | async-start | bytes 2097152 | tf_op jit(solution)/shard_map/all_to_all | solution.py:85
  83.0 33.3 %copy-start.1 = (f32[64,512]{1,0:T(8,128)S(1)}, f32[64,512]{1,0:T(8,128)}, u32[]{:S(2)}) copy-start(f32[64,512]{1,0:T(8,128)} %weights_ref.1) | copy-start | bytes 393220

commit v3 on v2

--- a/solution.py
+++ b/solution.py
@@ -15,6 +15,8 @@
 OWNERS = 32
 GROUPS = 16
 NEAR = 8
+CHIPS = NEAR // 2
+SIDE = 4
 FAR = OWNERS // NEAR
 ROWS = BLOCK // NEAR
 
@@ -30,6 +32,10 @@
     v = np.arange(BLOCK, dtype=np.float64)[None, :]
     norm = np.sqrt(np.where(j == 0, 1.0, 2.0) / BLOCK)
     return (norm * np.cos(np.pi * (2 * v + 1) * j / (2 * BLOCK))).astype(np.float32)
+
+
+def add_cores_kernel(parts_ref, out_ref):
+    out_ref[...] = parts_ref[0] + parts_ref[1]
 
 
 def window_kernel(place_ref, parts_ref, out_ref, total_ref):
@@ -52,7 +58,8 @@
 def owner_kernel(place_ref, parts_ref, momentum_ref, chosen_ref, table_ref, back_ref, momentum_out_ref, copies_ref):
     count = place_ref[1]
     live = lax.broadcasted_iota(jnp.int32, (BLOCK, MOST), 1) < count
-    gradient = jnp.sum(parts_ref[...], axis=0) * (1.0 / OWNERS)
+    added = jnp.sum(parts_ref[...], axis=0)
+    gradient = jnp.concatenate([added[b, c] for c in range(2) for b in range(CHIPS)], axis=0) * (1.0 / OWNERS)
     accumulated = jnp.where(live, momentum_decay * momentum_ref[0] + gradient, 0.0)
     coeffs = jnp.dot(table_ref[...], accumulated, precision=lax.Precision.HIGHEST, preferred_element_type=jnp.float32)
     chosen = chosen_ref[0]
@@ -66,8 +73,14 @@
     sparse = jnp.where(listed != 0, coeffs, 0.0)
     own = jnp.dot(back_ref[...], sparse, precision=lax.Precision.HIGHEST, preferred_element_type=jnp.float32)
     momentum_out_ref[0] = jnp.where(live, accumulated - own, 0.0)
-    for r in range(GROUPS):
+    for r in range(SIDE):
         copies_ref[r] = own
+
+
+def add_row_kernel(parts_ref, copies_ref):
+    added = jnp.sum(parts_ref[...], axis=0)
+    for r in range(SIDE):
+        copies_ref[r] = added
 
 
 def weights_kernel(place_ref, parts_ref, weights_ref, out_ref):
@@ -82,7 +95,16 @@
     place = jnp.concatenate([jnp.stack([group, owner_blocks[owner]]).astype(jnp.int32), owner_blocks])
     whole = pl.BlockSpec(memory_space=pltpu.VMEM)
 
-    near = lax.all_to_all(partials.reshape(NEAR, ROWS, BLOCKS), ("zl", "core"), 0, 0, tiled=False)
+    halves = lax.all_to_all(partials.reshape(2, BLOCK // 2, BLOCKS), "core", 0, 0, tiled=False)
+    half = pl.pallas_call(
+        add_cores_kernel,
+        out_shape=jax.ShapeDtypeStruct((BLOCK // 2, BLOCKS), jnp.float32),
+        in_specs=[whole],
+        out_specs=whole,
+        compiler_params=pltpu.CompilerParams(vmem_limit_bytes=8 << 20),
+        name="add_cores",
+    )(halves)
+    near = lax.all_to_all(half.reshape(CHIPS, ROWS, BLOCKS), "zl", 0, 0, tiled=False)
     windows = pl.pallas_call(
         window_kernel,
         out_shape=jax.ShapeDtypeStruct((OWNERS, ROWS, MOST), jnp.float32),
@@ -92,20 +114,20 @@
         compiler_params=pltpu.CompilerParams(vmem_limit_bytes=8 << 20),
         name="windows",
     )(place, near)
-    far = lax.all_to_all(windows, FSDP, 0, 0, tiled=False).reshape(FAR, BLOCK, MOST)
+    far = lax.all_to_all(windows, FSDP, 0, 0, tiled=False).reshape(FAR, CHIPS, 2, ROWS, MOST)
 
     table = dct_matrix()
     new_momentum, copies = pl.pallas_call(
         owner_kernel,
         out_shape=(
             jax.ShapeDtypeStruct((1, BLOCK, MOST), jnp.float32),
-            jax.ShapeDtypeStruct((GROUPS, BLOCK, MOST), jnp.float32),
+            jax.ShapeDtypeStruct((SIDE, BLOCK, MOST), jnp.float32),
         ),
         grid_spec=pltpu.PrefetchScalarGridSpec(
             num_scalar_prefetch=1,
             grid=(1,),
             in_specs=[
-                pl.BlockSpec((FAR, BLOCK, MOST), lambda i, place: (0, 0, 0)),
+                pl.BlockSpec((FAR, CHIPS, 2, ROWS, MOST), lambda i, place: (0, 0, 0, 0, 0)),
                 pl.BlockSpec((1, BLOCK, MOST), lambda i, place: (0, 0, 0)),
                 pl.BlockSpec((1, K, MOST), lambda i, place: (place[0], 0, 0)),
                 pl.BlockSpec((BLOCK, BLOCK), lambda i, place: (0, 0)),
@@ -113,13 +135,22 @@
             ],
             out_specs=[
                 pl.BlockSpec((1, BLOCK, MOST), lambda i, place: (0, 0, 0)),
-                pl.BlockSpec((GROUPS, BLOCK, MOST), lambda i, place: (0, 0, 0)),
+                pl.BlockSpec((SIDE, BLOCK, MOST), lambda i, place: (0, 0, 0)),
             ],
         ),
         compiler_params=pltpu.CompilerParams(vmem_limit_bytes=16 << 20),
         name="owner_step",
     )(place, far, momentum, selected, jnp.asarray(table), jnp.asarray(table.T))
-    everyone = lax.all_to_all(copies, REP, 0, 0, tiled=False)
+    row = lax.all_to_all(copies, "x", 0, 0, tiled=False)
+    copies = pl.pallas_call(
+        add_row_kernel,
+        out_shape=jax.ShapeDtypeStruct((SIDE, BLOCK, MOST), jnp.float32),
+        in_specs=[whole],
+        out_specs=whole,
+        compiler_params=pltpu.CompilerParams(vmem_limit_bytes=8 << 20),
+        name="add_row",
+    )(row)
+    everyone = lax.all_to_all(copies, "y", 0, 0, tiled=False)
     new_weights = pl.pallas_call(
         weights_kernel,
         out_shape=jax.ShapeDtypeStruct((BLOCK, MOST), jnp.float32),
@@ -132,7 +163,7 @@
 
 
 def solution(mesh):
-    fine = Mesh(mesh.devices.reshape(4, 4, FAR, NEAR // 2, 2), REP + FSDP)
+    fine = Mesh(mesh.devices.reshape(SIDE, SIDE, FAR, CHIPS, 2), REP + FSDP)
     return jax.shard_map(
         body,
         mesh=fine,

time: 120 us -> 105 us (0.88); the launches traced: 118 us -> 104 us
  waiting for transfers between devices: 25.3 us -> 12.8 us
  blocking collectives: 79.9 us -> 77.5 us
    all_to_all x1, waiting for transfers between devices: 25.3 us -> 12.8 us  [body(): lax.all_to_all(half.reshape(CHIPS, ROWS, BLOCKS), 'zl', 0, 0, tiled=False)]
    all_to_all x2 -> x4, blocking collectives: 79.9 us -> 77.5 us  [the longest x1 47 us: body(): lax.all_to_all(windows, FSDP, 0, 0, tiled=False)]
where the time goes in v3:
time: 105 us; the launch traced here: 104 us
  blocking collectives  77.5 us (74%)
  waiting for transfers between devices  12.8 us (12%)
  starting transfers between devices  5.89 us (6%)
  Pallas kernels  4.93 us (5%)
  local copies, waits for them, and re-layouts  1.27 us (1%)
    all_to_all x1, blocking collectives, body(): lax.all_to_all(windows, FSDP, 0, 0, tiled=False)  47 us
    all_to_all x1, waiting for transfers between devices, body(): lax.all_to_all(half.reshape(CHIPS, ROWS, BLOCKS), 'zl', 0, 0, tiled=False)  12.8 us
    all_to_all x1, blocking collectives, body(): everyone = lax.all_to_all(copies, 'y', 0, 0, tiled=False)  12.6 us
    all_to_all x1, blocking collectives, body(): row = lax.all_to_all(copies, 'x', 0, 0, tiled=False)  12.2 us
    all_to_all x1, starting transfers between devices, body(): lax.all_to_all(half.reshape(CHIPS, ROWS, BLOCKS), 'zl', 0, 0, tiled=False)  5.89 us
    all_to_all x1, blocking collectives, body(): lax.all_to_all(partials.reshape(2, BLOCK // 2, BLOCKS), 'core', 0, 0, til...  5.69 us
  transfers between devices with their start and end apart: 1, of which 1 were waited for; matrix products, arithmetic and copies ran while one was open for 1% of the time, Pallas kernels for 0%

profile of v3, /device:TPU:6, one launch (start us, length us, event | category | flops | bytes accessed | tf_op | source)
XLA Modules:
  0.0 103.8 jit_solution(3203943794120423791)
XLA Ops:
  0.6 5.7 %all_to_all.25.parts_ref = f32[2,32,4096]{2,1,0:T(8,128)S(1)} all-to-all(f32[2,32,4096]{2,1,0:T(8,128)} %bitcast.5), channel_id=1, replica_groups=mesh['y'=4,'x'=4,'zh'=4,'zl'=4,'core'=2] {'core'}, dimensions={0} | all-to-all | bytes 2097152 | tf_op jit(solution)/shard_map/all_to_all | solution.py:98
  6.3 0.9 add_cores.1
  7.2 5.9 %all-to-all-start.1 = ((f32[4,8,4096]{2,1,0:T(8,128)}), f32[4,8,4096]{2,1,0:T(8,128)S(1)}, u32[]{:S(2)}, u32[]{:S(2)}) async-start(f32[4,8,4096]{2,1,0:T(8,128)} %bitcast.2), calls=%async_computation.1 | async-start | bytes 1048576 | tf_op jit(solution)/shard_map/all_to_all | solution.py:107
  13.1 0.0 copy-start.5
  13.1 0.7 copy-done.5
  13.7 0.6 dynamic_slice.3
  14.3 0.7 pad_add_fusion.place_ref
  15.0 0.0 copy-start
  15.0 12.8 %all-to-all-done.1.parts_ref = f32[4,8,4096]{2,1,0:T(8,128)S(1)} async-done(((f32[4,8,4096]{2,1,0:T(8,128)}), f32[4,8,4096]{2,1,0:T(8,128)S(1)}, u32[]{:S(2)}, u32[]{:S(2)}) %all-to-all-start.1) | async-done | bytes 524320 | tf_op jit(solution)/shard_map/all_to_all | solution.py:107
  27.9 1.0 windows.1
  28.9 0.0 copy-start.2
  28.9 0.0 copy-start.3
  28.9 0.0 copy-start.4
  28.9 47.0 %all_to_all.26 = f32[32,8,512]{2,1,0:T(8,128)S(1)} all-to-all(f32[32,8,512]{2,1,0:T(8,128)S(1)} %windows.1), channel_id=1, replica_groups=mesh['y'=4,'x'=4,'zh'=4,'zl'=4,'core'=2] {'zh','zl','core'}, dimensions={0} | all-to-all | bytes 1048576 | tf_op jit(solution)/shard_map/all_to_all | solution.py:117
  75.9 0.0 copy-done
  75.9 0.0 copy-done.2
  75.9 0.0 copy-done.3
  75.9 0.0 copy-done.4
  76.0 1.8 %owner_step.1 = (f32[1,64,512]{2,1,0:T(8,128)}, f32[4,64,512]{2,1,0:T(8,128)S(1)}) custom-call(s32[34]{0:T(128)S(1)} %pad_add_fusion.place_ref, f32[4,4,2,8,512]{4,3,2,1,0:T(8,128)S(1)} %bitcast.4, f32[1,64,512]{2,1,0:T(8,128)S(1)} %copy-done.2, s32[16,32,512]{2,1,0:T(8,128)S(1)} %copy-done, f32[64,64]{1,0:T(8,128)S(1)} %copy-done.4, f32[64,64]{1,0:T(8,128)S(1)} %copy-done.3), custom_call_target="tpu_custom_call" | custom-call | tf_op jit(solution)/shard_map/owner_step/pallas_call | solution.py:120
  77.7 12.2 %all_to_all.27.parts_ref = f32[4,64,512]{2,1,0:T(8,128)S(1)} all-to-all(f32[4,64,512]{2,1,0:T(8,128)S(1)} %get-tuple-element.5), channel_id=1, replica_groups=mesh['y'=4,'x'=4,'zh'=4,'zl'=4,'core'=2] {'x'}, dimensions={0} | all-to-all | bytes 1048576 | tf_op jit(solution)/shard_map/all_to_all | solution.py:144
  89.9 0.0 copy-start.1
  89.9 12.6 %all_to_all.28.parts_ref = f32[4,64,512]{2,1,0:T(8,128)S(1)} all-to-all(f32[4,64,512]{2,1,0:T(8,128)S(1)} %add_row.1), channel_id=1, replica_groups=mesh['y'=4,'x'=4,'zh'=4,'zl'=4,'core'=2] {'y'}, dimensions={0} | all-to-all | bytes 1048576 | tf_op jit(solution)/shard_map/all_to_all | solution.py:153
  102.6 0.0 copy-done.1
  102.6 1.2 %weights_step.1 = f32[64,512]{1,0:T(8,128)} custom-call(s32[34]{0:T(128)S(1)} %pad_add_fusion.place_ref, f32[4,64,512]{2,1,0:T(8,128)S(1)} %all_to_all.28.parts_ref, f32[64,512]{1,0:T(8,128)S(1)} %copy-done.1), custom_call_target="tpu_custom_call" | custom-call | tf_op jit(solution)/shard_map/weights_step/pallas_call | solution.py:154
  (1 shorter events, 0.0 us)
Async XLA Ops:
  7.2 20.7 %all-to-all-start.1 = ((f32[4,8,4096]{2,1,0:T(8,128)}), f32[4,8,4096]{2,1,0:T(8,128)S(1)}, u32[]{:S(2)}, u32[]{:S(2)}) async-start(f32[4,8,4096]{2,1,0:T(8,128)} %bitcast.2), calls=%async_computation.1 | async-start | bytes 1048576 | tf_op jit(solution)/shard_map/all_to_all | solution.py:107
  13.1 0.7 copy-start.5
  15.0 60.9 %copy-start = (s32[16,32,512]{2,1,0:T(8,128)S(1)}, s32[16,32,512]{2,1,0:T(8,128)}, u32[]{:S(2)}) copy-start(s32[16,32,512]{2,1,0:T(8,128)} %chosen_ref.1) | copy-start | bytes 3145732
  28.9 47.0 %copy-start.2 = (f32[1,64,512]{2,1,0:T(8,128)S(1)}, f32[1,64,512]{2,1,0:T(8,128)}, u32[]{:S(2)}) copy-start(f32[1,64,512]{2,1,0:T(8,128)} %momentum_ref.1) | copy-start | bytes 393220
  28.9 47.0 %copy-start.3 = (f32[64,64]{1,0:T(8,128)S(1)}, f32[64,64]{1,0:T(8,128)}, u32[]{:S(2)}) copy-start(f32[64,64]{1,0:T(8,128)} %constant.34.clone.back_ref) | copy-start | bytes 49156
  28.9 47.0 %copy-start.4 = (f32[64,64]{1,0:T(8,128)S(1)}, f32[64,64]{1,0:T(8,128)}, u32[]{:S(2)}) copy-start(f32[64,64]{1,0:T(8,128)} %constant.33.clone.table_ref) | copy-start | bytes 49156
  89.9 12.6 %copy-start.1 = (f32[64,512]{1,0:T(8,128)S(1)}, f32[64,512]{1,0:T(8,128)}, u32[]{:S(2)}) copy-start(f32[64,512]{1,0:T(8,128)} %weights_ref.1) | copy-start | bytes 393220

commit v4 on v3

--- a/solution.py
+++ b/solution.py
@@ -17,6 +17,7 @@
 NEAR = 8
 CHIPS = NEAR // 2
 SIDE = 4
+WIDTHS = (1536, 2048, 4096)
 FAR = OWNERS // NEAR
 ROWS = BLOCK // NEAR
 
@@ -38,12 +39,37 @@
     out_ref[...] = parts_ref[0] + parts_ref[1]
 
 
-def window_kernel(place_ref, parts_ref, out_ref, total_ref):
+def plan_kernel(where_ref, counts_ref, plan_ref):
+    plan_ref[0] = where_ref[0]
+    plan_ref[1] = counts_ref[where_ref[1]]
+    start = jnp.int32(0)
+    reach = jnp.int32(0)
+    first = jnp.int32(0)
+    for i in range(OWNERS):
+        if i % NEAR == 0:
+            first = start - start % 128
+        plan_ref[3 + i] = start
+        start = start + counts_ref[i]
+        reach = jnp.maximum(reach, start - first)
+    plan_ref[2] = sum((reach > width).astype(jnp.int32) for width in WIDTHS[:-1])
+
+
+def spread_kernel(width, plan_ref, parts_ref, out_ref, total_ref):
     total_ref[:, :BLOCKS] = jnp.sum(parts_ref[...], axis=0)
-    total_ref[:, BLOCKS:] = jnp.zeros((ROWS, MOST + 128), jnp.float32)
+    total_ref[:, BLOCKS:] = jnp.zeros((ROWS, width), jnp.float32)
+    for a in range(FAR):
+        base = pl.multiple_of((plan_ref[3 + NEAR * a] // 128) * 128, 128)
+        out_ref[a] = total_ref[:, pl.ds(base, width)]
+
+
+def window_kernel(width, plan_ref, far_ref, parts_ref, out_ref, total_ref):
+    total_ref[:, :width] = jnp.sum(parts_ref[...], axis=0)
+    total_ref[:, width:] = jnp.zeros((ROWS, MOST + 128), jnp.float32)
     lane = lax.broadcasted_iota(jnp.int32, (ROWS, 128), 1)
-    start = jnp.int32(0)
-    for i in range(OWNERS):
+    owner = far_ref[0] * NEAR
+    first = (plan_ref[3 + owner] // 128) * 128
+    for i in range(NEAR):
+        start = plan_ref[3 + owner + i] - first
         base = pl.multiple_of((start // 128) * 128, 128)
         shift = start % 128
         tiles = [
@@ -52,14 +78,37 @@
         ]
         for t in range(MOST // 128):
             out_ref[i, :, 128 * t : 128 * (t + 1)] = jnp.where(lane < 128 - shift, tiles[t], tiles[t + 1])
-        start = start + place_ref[2 + i]
+
+
+def deliver(width, plan, far, near):
+    smem = pl.BlockSpec(memory_space=pltpu.SMEM)
+    whole = pl.BlockSpec(memory_space=pltpu.VMEM)
+    small = pltpu.CompilerParams(vmem_limit_bytes=8 << 20)
+    spread = pl.pallas_call(
+        functools.partial(spread_kernel, width),
+        out_shape=jax.ShapeDtypeStruct((FAR, ROWS, width), jnp.float32),
+        in_specs=[smem, whole],
+        out_specs=whole,
+        scratch_shapes=[pltpu.VMEM((ROWS, BLOCKS + width), jnp.float32)],
+        compiler_params=small,
+        name=f"spread_{width}",
+    )(plan, near)
+    met = lax.all_to_all(spread, "zh", 0, 0, tiled=False)
+    return pl.pallas_call(
+        functools.partial(window_kernel, width),
+        out_shape=jax.ShapeDtypeStruct((NEAR, ROWS, MOST), jnp.float32),
+        in_specs=[smem, smem, whole],
+        out_specs=whole,
+        scratch_shapes=[pltpu.VMEM((ROWS, width + MOST + 128), jnp.float32)],
+        compiler_params=small,
+        name=f"windows_{width}",
+    )(plan, far, met)
 
 
 def owner_kernel(place_ref, parts_ref, momentum_ref, chosen_ref, table_ref, back_ref, momentum_out_ref, copies_ref):
     count = place_ref[1]
     live = lax.broadcasted_iota(jnp.int32, (BLOCK, MOST), 1) < count
-    added = jnp.sum(parts_ref[...], axis=0)
-    gradient = jnp.concatenate([added[b, c] for c in range(2) for b in range(CHIPS)], axis=0) * (1.0 / OWNERS)
+    gradient = jnp.concatenate([parts_ref[b, c] for c in range(2) for b in range(CHIPS)], axis=0) * (1.0 / OWNERS)
     accumulated = jnp.where(live, momentum_decay * momentum_ref[0] + gradient, 0.0)
     coeffs = jnp.dot(table_ref[...], accumulated, precision=lax.Precision.HIGHEST, preferred_element_type=jnp.float32)
     chosen = chosen_ref[0]
@@ -92,7 +141,15 @@
 def body(partials, owner_blocks, momentum, weights, selected):
     owner = lax.axis_index(FSDP)
     group = lax.axis_index(REP)
-    place = jnp.concatenate([jnp.stack([group, owner_blocks[owner]]).astype(jnp.int32), owner_blocks])
+    far = lax.axis_index("zh").reshape(1)
+    smem = pl.BlockSpec(memory_space=pltpu.SMEM)
+    place = pl.pallas_call(
+        plan_kernel,
+        out_shape=jax.ShapeDtypeStruct((3 + OWNERS,), jnp.int32),
+        in_specs=[smem, smem],
+        out_specs=smem,
+        name="plan",
+    )(jnp.stack([group, owner]).astype(jnp.int32), owner_blocks)
     whole = pl.BlockSpec(memory_space=pltpu.VMEM)
 
     halves = lax.all_to_all(partials.reshape(2, BLOCK // 2, BLOCKS), "core", 0, 0, tiled=False)
@@ -105,16 +162,8 @@
         name="add_cores",
     )(halves)
     near = lax.all_to_all(half.reshape(CHIPS, ROWS, BLOCKS), "zl", 0, 0, tiled=False)
-    windows = pl.pallas_call(
-        window_kernel,
-        out_shape=jax.ShapeDtypeStruct((OWNERS, ROWS, MOST), jnp.float32),
-        in_specs=[pl.BlockSpec(memory_space=pltpu.SMEM), whole],
-        out_specs=whole,
-        scratch_shapes=[pltpu.VMEM((ROWS, BLOCKS + MOST + 128), jnp.float32)],
-        compiler_params=pltpu.CompilerParams(vmem_limit_bytes=8 << 20),
-        name="windows",
-    )(place, near)
-    far = lax.all_to_all(windows, FSDP, 0, 0, tiled=False).reshape(FAR, CHIPS, 2, ROWS, MOST)
+    windows = lax.switch(place[2], [functools.partial(deliver, width) for width in WIDTHS], place, far, near)
+    blocks = lax.all_to_all(windows, ("zl", "core"), 0, 0, tiled=False).reshape(CHIPS, 2, ROWS, MOST)
 
     table = dct_matrix()
     new_momentum, copies = pl.pallas_call(
@@ -127,7 +176,7 @@
             num_scalar_prefetch=1,
             grid=(1,),
             in_specs=[
-                pl.BlockSpec((FAR, CHIPS, 2, ROWS, MOST), lambda i, place: (0, 0, 0, 0, 0)),
+                pl.BlockSpec((CHIPS, 2, ROWS, MOST), lambda i, place: (0, 0, 0, 0)),
                 pl.BlockSpec((1, BLOCK, MOST), lambda i, place: (0, 0, 0)),
                 pl.BlockSpec((1, K, MOST), lambda i, place: (place[0], 0, 0)),
                 pl.BlockSpec((BLOCK, BLOCK), lambda i, place: (0, 0)),
@@ -140,7 +189,7 @@
         ),
         compiler_params=pltpu.CompilerParams(vmem_limit_bytes=16 << 20),
         name="owner_step",
-    )(place, far, momentum, selected, jnp.asarray(table), jnp.asarray(table.T))
+    )(place, blocks, momentum, selected, jnp.asarray(table), jnp.asarray(table.T))
     row = lax.all_to_all(copies, "x", 0, 0, tiled=False)
     copies = pl.pallas_call(
         add_row_kernel,

time: 105 us -> 98.5 us (0.938)
  blocking collectives: 77.5 us -> 70.8 us
  Pallas kernels: 4.93 us -> 6.52 us
  waiting for transfers between devices: 12.8 us -> 11.6 us
    all_to_all x1 -> x2, blocking collectives: 47 us -> 40.9 us  [the longest x1 31 us: deliver(): met = lax.all_to_all(spread, 'zh', 0, 0, tiled=False)]
    pallas_call x1 -> x3, Pallas kernels: 1.03 us -> 2.64 us  [the longest x1 1.33 us: body(): pl.pallas_call(plan_kernel, out_shape=jax.ShapeDtypeStruct((3 + OWNERS,),...]
    all_to_all x1, waiting for transfers between devices: 12.8 us -> 11.6 us  [body(): lax.all_to_all(half.reshape(CHIPS, ROWS, BLOCKS), 'zl', 0, 0, tiled=False)]
  transfers between devices with their start and end apart: 1 -> 1, of which waited for: 1 -> 1; matrix products, arithmetic and copies ran while one was open for 1% -> 1% of each run, Pallas kernels for 0% -> 1%
where the time goes in v4:
time: 98.5 us; the launch traced here: 97.4 us
  blocking collectives  70.8 us (72%)
  waiting for transfers between devices  11.6 us (12%)
  Pallas kernels  6.52 us (7%)
  starting transfers between devices  5.89 us (6%)
  between operations  1.35 us (1%)
    all_to_all x1, blocking collectives, deliver(): met = lax.all_to_all(spread, 'zh', 0, 0, tiled=False)  31 us
    all_to_all x1, blocking collectives, body(): everyone = lax.all_to_all(copies, 'y', 0, 0, tiled=False)  12.5 us
    all_to_all x1, blocking collectives, body(): row = lax.all_to_all(copies, 'x', 0, 0, tiled=False)  11.7 us
    all_to_all x1, waiting for transfers between devices, body(): lax.all_to_all(half.reshape(CHIPS, ROWS, BLOCKS), 'zl', 0, 0, tiled=False)  11.6 us
    all_to_all x1, blocking collectives, body(): lax.all_to_all(windows, ('zl', 'core'), 0, 0, tiled=False)  9.9 us
    all_to_all x1, starting transfers between devices, body(): lax.all_to_all(half.reshape(CHIPS, ROWS, BLOCKS), 'zl', 0, 0, tiled=False)  5.89 us
    all_to_all x1, blocking collectives, body(): lax.all_to_all(partials.reshape(2, BLOCK // 2, BLOCKS), 'core', 0, 0, til...  5.69 us
  transfers between devices with their start and end apart: 1, of which 1 were waited for; matrix products, arithmetic and copies ran while one was open for 1% of the time, Pallas kernels for 1%

profile of v4, /device:TPU:6, one launch (start us, length us, event | category | flops | bytes accessed | tf_op | source)
XLA Modules:
  0.0 97.4 jit_solution(5198336849597110338)
XLA Ops:
  0.6 5.7 %all_to_all.40.parts_ref = f32[2,32,4096]{2,1,0:T(8,128)S(1)} all-to-all(f32[2,32,4096]{2,1,0:T(8,128)} %bitcast.8), channel_id=1, replica_groups=mesh['y'=4,'x'=4,'zh'=4,'zl'=4,'core'=2] {'core'}, dimensions={0} | all-to-all | bytes 2097152 | tf_op jit(solution)/shard_map/all_to_all | solution.py:155
  6.3 0.9 add_cores.1
  7.2 5.9 %all-to-all-start.4 = ((f32[4,8,4096]{2,1,0:T(8,128)}), f32[4,8,4096]{2,1,0:T(8,128)S(1)}, u32[]{:S(2)}, u32[]{:S(2)}) async-start(f32[4,8,4096]{2,1,0:T(8,128)} %bitcast.4), calls=%async_computation.4 | async-start | bytes 1048576 | tf_op jit(solution)/shard_map/all_to_all | solution.py:164
  13.1 0.6 pad_add_fusion.where_ref
  13.7 1.3 %plan.1.place_ref = s32[35]{0:T(128)S(1)} custom-call(s32[2]{0:T(128)} %pad_add_fusion.where_ref, s32[32]{0:T(128)} %counts_ref.1), custom_call_target="tpu_custom_call" | custom-call | tf_op jit(solution)/shard_map/plan/pallas_call | solution.py:146
  15.0 0.6 slice.3
  16.2 11.6 %all-to-all-done.4 = f32[4,8,4096]{2,1,0:T(8,128)S(1)} async-done(((f32[4,8,4096]{2,1,0:T(8,128)}), f32[4,8,4096]{2,1,0:T(8,128)S(1)}, u32[]{:S(2)}, u32[]{:S(2)}) %all-to-all-start.4) | async-done | bytes 524320 | tf_op jit(solution)/shard_map/all_to_all | solution.py:164
  27.9 0.0 copy-start
  27.9 32.3 %conditional.1 = (f32[8,8,512]{2,1,0:T(8,128)S(1)}) conditional(s32[]{:T(128)} %bitcast.2, (s32[35]{0:T(128)S(1)}, f32[4,8,4096]{2,1,0:T(8,128)S(1)}, s32[1]{0:T(128)}) %tuple.17, (s32[35]{0:T(128)S(1)}, f32[4,8,4096]{2,1,0:T(8,128)S(1)}, s32[1]{0:T(128)}) %tuple.17, (s32[35]{0:T(128)S(1)}, f32[4,8,4096]{2,1,0:T(8,128)S(1)}, ...), branch_computations={%region_0.0_spmd, %region_1.0_spmd, %region_2.0_spmd} | conditional | bytes 1048584 | solution.py:165
  27.9 0.6 spread_2048.1
  28.5 31.0 %all_to_all.38.parts_ref = f32[4,8,2048]{2,1,0:T(8,128)S(1)} all-to-all(f32[4,8,2048]{2,1,0:T(8,128)S(1)} %spread_2048.1), channel_id=1, replica_groups=mesh['y'=4,'x'=4,'zh'=4,'zl'=4,'core'=2] {'zh'}, dimensions={0} | all-to-all | bytes 524288 | tf_op jit(solution)/shard_map/cond/branch_1_fun/all_to_all | solution.py:96
  59.5 0.7 windows_2048.1
  60.2 0.0 copy-start.1
  60.2 0.0 copy-start.3
  60.2 0.0 copy-start.4
  60.2 9.9 %all_to_all.41 = f32[8,8,512]{2,1,0:T(8,128)S(1)} all-to-all(f32[8,8,512]{2,1,0:T(8,128)S(1)} %get-tuple-element.37), channel_id=1, replica_groups=mesh['y'=4,'x'=4,'zh'=4,'zl'=4,'core'=2] {'zl','core'}, dimensions={0} | all-to-all | bytes 262144 | tf_op jit(solution)/shard_map/all_to_all | solution.py:166
  70.1 0.0 copy-done
  70.1 0.0 copy-done.1
  70.2 0.0 copy-done.3
  70.2 0.0 copy-done.4
  70.2 1.8 %owner_step.1 = (f32[1,64,512]{2,1,0:T(8,128)}, f32[4,64,512]{2,1,0:T(8,128)S(1)}) custom-call(s32[35]{0:T(128)S(1)} %plan.1.place_ref, f32[4,2,8,512]{3,2,1,0:T(8,128)S(1)} %bitcast.7, f32[1,64,512]{2,1,0:T(8,128)S(1)} %copy-done.1, s32[16,32,512]{2,1,0:T(8,128)S(1)} %copy-done, f32[64,64]{1,0:T(8,128)S(1)} %copy-done.4, f32[64,64]{1,0:T(8,128)S(1)} %copy-done.3), custom_call_target="tpu_custom_call" | custom-call | tf_op jit(solution)/shard_map/owner_step/pallas_call | solution.py:169
  71.9 11.7 %all_to_all.42.parts_ref = f32[4,64,512]{2,1,0:T(8,128)S(1)} all-to-all(f32[4,64,512]{2,1,0:T(8,128)S(1)} %get-tuple-element.36), channel_id=1, replica_groups=mesh['y'=4,'x'=4,'zh'=4,'zl'=4,'core'=2] {'x'}, dimensions={0} | all-to-all | bytes 1048576 | tf_op jit(solution)/shard_map/all_to_all | solution.py:193
  83.6 0.0 copy-start.2
  83.6 12.5 %all_to_all.43.parts_ref = f32[4,64,512]{2,1,0:T(8,128)S(1)} all-to-all(f32[4,64,512]{2,1,0:T(8,128)S(1)} %add_row.1), channel_id=1, replica_groups=mesh['y'=4,'x'=4,'zh'=4,'zl'=4,'core'=2] {'y'}, dimensions={0} | all-to-all | bytes 1048576 | tf_op jit(solution)/shard_map/all_to_all | solution.py:202
  96.1 0.0 copy-done.2
  96.1 1.2 %weights_step.1 = f32[64,512]{1,0:T(8,128)} custom-call(s32[35]{0:T(128)S(1)} %plan.1.place_ref, f32[4,64,512]{2,1,0:T(8,128)S(1)} %all_to_all.43.parts_ref, f32[64,512]{1,0:T(8,128)S(1)} %copy-done.2), custom_call_target="tpu_custom_call" | custom-call | tf_op jit(solution)/shard_map/weights_step/pallas_call | solution.py:203
  (1 shorter events, 0.0 us)
Async XLA Ops:
  7.2 20.7 %all-to-all-start.4 = ((f32[4,8,4096]{2,1,0:T(8,128)}), f32[4,8,4096]{2,1,0:T(8,128)S(1)}, u32[]{:S(2)}, u32[]{:S(2)}) async-start(f32[4,8,4096]{2,1,0:T(8,128)} %bitcast.4), calls=%async_computation.4 | async-start | bytes 1048576 | tf_op jit(solution)/shard_map/all_to_all | solution.py:164
  27.9 42.3 %copy-start = (s32[16,32,512]{2,1,0:T(8,128)S(1)}, s32[16,32,512]{2,1,0:T(8,128)}, u32[]{:S(2)}) copy-start(s32[16,32,512]{2,1,0:T(8,128)} %chosen_ref.1) | copy-start | bytes 3145732
  60.2 9.9 %copy-start.1 = (f32[1,64,512]{2,1,0:T(8,128)S(1)}, f32[1,64,512]{2,1,0:T(8,128)}, u32[]{:S(2)}) copy-start(f32[1,64,512]{2,1,0:T(8,128)} %momentum_ref.1) | copy-start | bytes 393220
  60.2 9.9 %copy-start.3 = (f32[64,64]{1,0:T(8,128)S(1)}, f32[64,64]{1,0:T(8,128)}, u32[]{:S(2)}) copy-start(f32[64,64]{1,0:T(8,128)} %constant.35.clone.back_ref) | copy-start | bytes 49156
  60.2 9.9 %copy-start.4 = (f32[64,64]{1,0:T(8,128)S(1)}, f32[64,64]{1,0:T(8,128)}, u32[]{:S(2)}) copy-start(f32[64,64]{1,0:T(8,128)} %constant.34.clone.table_ref) | copy-start | bytes 49156
  83.6 12.5 %copy-start.2 = (f32[64,512]{1,0:T(8,128)S(1)}, f32[64,512]{1,0:T(8,128)}, u32[]{:S(2)}) copy-start(f32[64,512]{1,0:T(8,128)} %weights_ref.1) | copy-start | bytes 393220

commit v5 on v4

--- a/solution.py
+++ b/solution.py
@@ -35,11 +35,30 @@
     return (norm * np.cos(np.pi * (2 * v + 1) * j / (2 * BLOCK))).astype(np.float32)
 
 
-def add_cores_kernel(parts_ref, out_ref):
+def near_groups():
+    return [
+        [(CHIPS * a + b + 2 * core) % (OWNERS // 2) * 2 + core for b in range(CHIPS)]
+        for a in range(FAR)
+        for core in range(2)
+    ]
+
+
+def rep_groups(turn):
+    groups = []
+    for core in range(2):
+        for z in range(OWNERS // 2):
+            for i in range(SIDE):
+                line = [(i * SIDE + k if core == turn else k * SIDE + i) for k in range(SIDE)]
+                groups.append([rep * OWNERS + 2 * z + core for rep in line])
+    return groups
+
+
+def add_cores_kernel(plan_ref, parts_ref, out_ref):
+    del plan_ref
     out_ref[...] = parts_ref[0] + parts_ref[1]
 
 
-def plan_kernel(where_ref, counts_ref, plan_ref):
+def plan_kernel(where_ref, counts_ref, plan_ref, branch_ref):
     plan_ref[0] = where_ref[0]
     plan_ref[1] = counts_ref[where_ref[1]]
     start = jnp.int32(0)
@@ -48,17 +67,17 @@
     for i in range(OWNERS):
         if i % NEAR == 0:
             first = start - start % 128
-        plan_ref[3 + i] = start
+        plan_ref[2 + i] = start
         start = start + counts_ref[i]
         reach = jnp.maximum(reach, start - first)
-    plan_ref[2] = sum((reach > width).astype(jnp.int32) for width in WIDTHS[:-1])
+    branch_ref[0] = sum((reach > width).astype(jnp.int32) for width in WIDTHS[:-1])
 
 
 def spread_kernel(width, plan_ref, parts_ref, out_ref, total_ref):
     total_ref[:, :BLOCKS] = jnp.sum(parts_ref[...], axis=0)
     total_ref[:, BLOCKS:] = jnp.zeros((ROWS, width), jnp.float32)
     for a in range(FAR):
-        base = pl.multiple_of((plan_ref[3 + NEAR * a] // 128) * 128, 128)
+        base = pl.multiple_of((plan_ref[2 + NEAR * a] // 128) * 128, 128)
         out_ref[a] = total_ref[:, pl.ds(base, width)]
 
 
@@ -67,9 +86,9 @@
     total_ref[:, width:] = jnp.zeros((ROWS, MOST + 128), jnp.float32)
     lane = lax.broadcasted_iota(jnp.int32, (ROWS, 128), 1)
     owner = far_ref[0] * NEAR
-    first = (plan_ref[3 + owner] // 128) * 128
+    first = (plan_ref[2 + owner] // 128) * 128
     for i in range(NEAR):
-        start = plan_ref[3 + owner + i] - first
+        start = plan_ref[2 + owner + i] - first
         base = pl.multiple_of((start // 128) * 128, 128)
         shift = start % 128
         tiles = [
@@ -108,7 +127,7 @@
 def owner_kernel(place_ref, parts_ref, momentum_ref, chosen_ref, table_ref, back_ref, momentum_out_ref, copies_ref):
     count = place_ref[1]
     live = lax.broadcasted_iota(jnp.int32, (BLOCK, MOST), 1) < count
-    gradient = jnp.concatenate([parts_ref[b, c] for c in range(2) for b in range(CHIPS)], axis=0) * (1.0 / OWNERS)
+    gradient = jnp.concatenate([parts_ref[(b + 2 * c) % CHIPS, c] for c in range(2) for b in range(CHIPS)], axis=0) * (1.0 / OWNERS)
     accumulated = jnp.where(live, momentum_decay * momentum_ref[0] + gradient, 0.0)
     coeffs = jnp.dot(table_ref[...], accumulated, precision=lax.Precision.HIGHEST, preferred_element_type=jnp.float32)
     chosen = chosen_ref[0]
@@ -143,11 +162,12 @@
     group = lax.axis_index(REP)
     far = lax.axis_index("zh").reshape(1)
     smem = pl.BlockSpec(memory_space=pltpu.SMEM)
-    place = pl.pallas_call(
+    place, branch = pl.pallas_call(
         plan_kernel,
-        out_shape=jax.ShapeDtypeStruct((3 + OWNERS,), jnp.int32),
+        out_shape=(jax.ShapeDtypeStruct((2 + OWNERS,), jnp.int32), jax.ShapeDtypeStruct((1,), jnp.int32)),
         in_specs=[smem, smem],
-        out_specs=smem,
+        out_specs=(smem, smem),
+        compiler_params=pltpu.CompilerParams(vmem_limit_bytes=1 << 20),
         name="plan",
     )(jnp.stack([group, owner]).astype(jnp.int32), owner_blocks)
     whole = pl.BlockSpec(memory_space=pltpu.VMEM)
@@ -156,13 +176,13 @@
     half = pl.pallas_call(
         add_cores_kernel,
         out_shape=jax.ShapeDtypeStruct((BLOCK // 2, BLOCKS), jnp.float32),
-        in_specs=[whole],
+        in_specs=[pl.BlockSpec(memory_space=pl.ANY), whole],
         out_specs=whole,
         compiler_params=pltpu.CompilerParams(vmem_limit_bytes=8 << 20),
         name="add_cores",
-    )(halves)
-    near = lax.all_to_all(half.reshape(CHIPS, ROWS, BLOCKS), "zl", 0, 0, tiled=False)
-    windows = lax.switch(place[2], [functools.partial(deliver, width) for width in WIDTHS], place, far, near)
+    )(place, halves)
+    near = lax.all_to_all(half.reshape(CHIPS, ROWS, BLOCKS), FSDP, 0, 0, axis_index_groups=near_groups(), tiled=False)
+    windows = lax.switch(branch[0], [functools.partial(deliver, width) for width in WIDTHS], place, far, near)
     blocks = lax.all_to_all(windows, ("zl", "core"), 0, 0, tiled=False).reshape(CHIPS, 2, ROWS, MOST)
 
     table = dct_matrix()
@@ -190,7 +210,7 @@
         compiler_params=pltpu.CompilerParams(vmem_limit_bytes=16 << 20),
         name="owner_step",
     )(place, blocks, momentum, selected, jnp.asarray(table), jnp.asarray(table.T))
-    row = lax.all_to_all(copies, "x", 0, 0, tiled=False)
+    row = lax.all_to_all(copies, REP + FSDP, 0, 0, axis_index_groups=rep_groups(0), tiled=False)
     copies = pl.pallas_call(
         add_row_kernel,
         out_shape=jax.ShapeDtypeStruct((SIDE, BLOCK, MOST), jnp.float32),
@@ -199,7 +219,7 @@
         compiler_params=pltpu.CompilerParams(vmem_limit_bytes=8 << 20),
         name="add_row",
     )(row)
-    everyone = lax.all_to_all(copies, "y", 0, 0, tiled=False)
+    everyone = lax.all_to_all(copies, REP + FSDP, 0, 0, axis_index_groups=rep_groups(1), tiled=False)
     new_weights = pl.pallas_call(
         weights_kernel,
         out_shape=jax.ShapeDtypeStruct((BLOCK, MOST), jnp.float32),

time: 98.5 us -> 92.9 us (0.943)
  blocking collectives: 70.8 us -> 65.4 us
  starting transfers between devices: 5.89 us -> 9.48 us
  waiting for transfers between devices: 11.6 us -> 8.49 us
    all_to_all x3 -> x2, blocking collectives: 29.8 us -> 23.1 us  [the longest x1 12.5 us: body(): lax.all_to_all(copies, REP + FSDP, 0, 0, axis_index_groups=rep_groups(1),...]
    all_to_all x1, blocking collectives: 9.9 us -> 14.5 us  [body(): lax.all_to_all(windows, ('zl', 'core'), 0, 0, tiled=False)]
    all_to_all x1 -> x2, starting transfers between devices: 5.89 us -> 9.48 us  [the longest x1 5.89 us: body(): lax.all_to_all(half.reshape(CHIPS, ROWS, BLOCKS), FSDP, 0, 0, axis_index_...]
    all_to_all x1, blocking collectives: 31 us -> 27.9 us  [deliver(): met = lax.all_to_all(spread, 'zh', 0, 0, tiled=False)]
    all_to_all x1 -> x2, waiting for transfers between devices: 11.6 us -> 8.49 us  [the longest x1 8.23 us: body(): lax.all_to_all(half.reshape(CHIPS, ROWS, BLOCKS), FSDP, 0, 0, axis_index_...]
  transfers between devices with their start and end apart: 1 -> 2, of which waited for: 1 -> 2; matrix products, arithmetic and copies ran while one was open for 1% -> 0% of each run, Pallas kernels for 1% -> 1%
where the time goes in v5:
time: 92.9 us; the launch traced here: 91.8 us
  blocking collectives  65.4 us (70%)
  starting transfers between devices  9.48 us (10%)
  waiting for transfers between devices  8.49 us (9%)
  Pallas kernels  6.36 us (7%)
  between operations  1.38 us (1%)
    all_to_all x1, blocking collectives, deliver(): met = lax.all_to_all(spread, 'zh', 0, 0, tiled=False)  27.9 us
    all_to_all x1, blocking collectives, body(): lax.all_to_all(windows, ('zl', 'core'), 0, 0, tiled=False)  14.5 us
    all_to_all x1, blocking collectives, body(): lax.all_to_all(copies, REP + FSDP, 0, 0, axis_index_groups=rep_groups(1),...  12.5 us
    all_to_all x1, blocking collectives, body(): lax.all_to_all(copies, REP + FSDP, 0, 0, axis_index_groups=rep_groups(0),...  10.6 us
    all_to_all x1, waiting for transfers between devices, body(): lax.all_to_all(half.reshape(CHIPS, ROWS, BLOCKS), FSDP, 0, 0, axis_index_...  8.23 us
    all_to_all x1, starting transfers between devices, body(): lax.all_to_all(half.reshape(CHIPS, ROWS, BLOCKS), FSDP, 0, 0, axis_index_...  5.89 us
    all_to_all x1, starting transfers between devices, body(): lax.all_to_all(partials.reshape(2, BLOCK // 2, BLOCKS), 'core', 0, 0, til...  3.59 us
  transfers between devices with their start and end apart: 2, of which 2 were waited for; matrix products, arithmetic and copies ran while one was open for 0% of the time, Pallas kernels for 1%

profile of v5, /device:TPU:6, one launch (start us, length us, event | category | flops | bytes accessed | tf_op | source)
XLA Modules:
  0.0 91.8 jit_solution(11360596035555257965)
XLA Ops:
  0.6 3.6 %all-to-all-start.3 = ((f32[2,32,4096]{2,1,0:T(8,128)}), f32[2,32,4096]{2,1,0:T(8,128)S(1)}, u32[]{:S(2)}, u32[]{:S(2)}) async-start(f32[2,32,4096]{2,1,0:T(8,128)} %bitcast.8), calls=%async_computation.3 | async-start | bytes 2097152 | tf_op jit(solution)/shard_map/all_to_all | solution.py:175
  4.2 0.0 copy-start.5
  4.2 0.1 pad_add_fusion.where_ref
  4.3 0.6 copy-done.5
  4.9 1.2 %plan.1 = (s32[34]{0:T(128)S(1)}, s32[1]{0:T(128)}) custom-call(s32[2]{0:T(128)S(1)} %pad_add_fusion.where_ref, s32[32]{0:T(128)S(1)} %copy-done.5), custom_call_target="tpu_custom_call" | custom-call | tf_op jit(solution)/shard_map/plan/pallas_call | solution.py:165
  6.1 0.3 all-to-all-done.3.parts_ref
  6.3 0.8 add_cores.1
  7.2 5.9 %all-to-all-start.4 = ((f32[4,8,4096]{2,1,0:T(8,128)}), f32[4,8,4096]{2,1,0:T(8,128)S(1)}, u32[]{:S(2)}, u32[]{:S(2)}) async-start(f32[4,8,4096]{2,1,0:T(8,128)} %bitcast.4), calls=%async_computation.4 | async-start | bytes 1048576 | tf_op jit(solution)/shard_map/all_to_all | solution.py:184
  13.7 8.2 %all-to-all-done.4 = f32[4,8,4096]{2,1,0:T(8,128)S(1)} async-done(((f32[4,8,4096]{2,1,0:T(8,128)}), f32[4,8,4096]{2,1,0:T(8,128)S(1)}, u32[]{:S(2)}, u32[]{:S(2)}) %all-to-all-start.4) | async-done | bytes 524320 | tf_op jit(solution)/shard_map/all_to_all | solution.py:184
  22.0 0.0 copy-start
  22.0 29.2 %conditional.1 = (f32[8,8,512]{2,1,0:T(8,128)S(1)}) conditional(s32[]{:T(128)} %bitcast.2, (s32[34]{0:T(128)S(1)}, f32[4,8,4096]{2,1,0:T(8,128)S(1)}, s32[1]{0:T(128)}) %tuple.17, (s32[34]{0:T(128)S(1)}, f32[4,8,4096]{2,1,0:T(8,128)S(1)}, s32[1]{0:T(128)}) %tuple.17, (s32[34]{0:T(128)S(1)}, f32[4,8,4096]{2,1,0:T(8,128)S(1)}, ...), branch_computations={%region_0.0_spmd, %region_1.0_spmd, %region_2.0_spmd} | conditional | bytes 1048584 | solution.py:185
  22.0 0.6 spread_1536.1
  22.6 27.9 %all_to_all.37.parts_ref = f32[4,8,1536]{2,1,0:T(8,128)S(1)} all-to-all(f32[4,8,1536]{2,1,0:T(8,128)S(1)} %spread_1536.1), channel_id=1, replica_groups=mesh['y'=4,'x'=4,'zh'=4,'zl'=4,'core'=2] {'zh'}, dimensions={0} | all-to-all | bytes 393216 | tf_op jit(solution)/shard_map/cond/branch_0_fun/all_to_all | solution.py:115
  50.4 0.7 windows_1536.1
  51.1 0.0 copy-start.1
  51.2 0.0 copy-start.3
  51.2 0.0 copy-start.4
  51.2 14.5 %all_to_all.40 = f32[8,8,512]{2,1,0:T(8,128)S(1)} all-to-all(f32[8,8,512]{2,1,0:T(8,128)S(1)} %get-tuple-element.41), channel_id=1, replica_groups=mesh['y'=4,'x'=4,'zh'=4,'zl'=4,'core'=2] {'zl','core'}, dimensions={0} | all-to-all | bytes 262144 | tf_op jit(solution)/shard_map/all_to_all | solution.py:186
  65.7 0.0 copy-done
  65.7 0.0 copy-done.1
  65.7 0.0 copy-done.3
  65.7 0.0 copy-done.4
  65.7 1.8 %owner_step.1 = (f32[1,64,512]{2,1,0:T(8,128)}, f32[4,64,512]{2,1,0:T(8,128)S(1)}) custom-call(s32[34]{0:T(128)S(1)} %get-tuple-element.37.plan_ref.place_ref, f32[4,2,8,512]{3,2,1,0:T(8,128)S(1)} %bitcast.7, f32[1,64,512]{2,1,0:T(8,128)S(1)} %copy-done.1, s32[16,32,512]{2,1,0:T(8,128)S(1)} %copy-done, f32[64,64]{1,0:T(8,128)S(1)} %copy-done.4, ...), custom_call_target="tpu_custom_call" | custom-call | tf_op jit(solution)/shard_map/owner_step/pallas_call | solution.py:189
  67.5 10.6 %all_to_all.41.parts_ref = f32[4,64,512]{2,1,0:T(8,128)S(1)} all-to-all(f32[4,64,512]{2,1,0:T(8,128)S(1)} %get-tuple-element.40), channel_id=1, replica_groups={{0,32,64,96},{128,160,192,224},{256,288,320,352},{384,416,448,480},{2,3..., dimensions={0} | all-to-all | bytes 1048576 | tf_op jit(solution)/shard_map/all_to_all | solution.py:213
  78.1 0.0 copy-start.2
  78.1 12.5 %all_to_all.42.parts_ref = f32[4,64,512]{2,1,0:T(8,128)S(1)} all-to-all(f32[4,64,512]{2,1,0:T(8,128)S(1)} %add_row.1), channel_id=1, replica_groups={{0,128,256,384},{32,160,288,416},{64,192,320,448},{96,224,352,480},{2,1..., dimensions={0} | all-to-all | bytes 1048576 | tf_op jit(solution)/shard_map/all_to_all | solution.py:222
  90.6 0.0 copy-done.2
  90.6 1.2 %weights_step.1 = f32[64,512]{1,0:T(8,128)} custom-call(s32[34]{0:T(128)S(1)} %get-tuple-element.37.plan_ref.place_ref, f32[4,64,512]{2,1,0:T(8,128)S(1)} %all_to_all.42.parts_ref, f32[64,512]{1,0:T(8,128)S(1)} %copy-done.2), custom_call_target="tpu_custom_call" | custom-call | tf_op jit(solution)/shard_map/weights_step/pallas_call | solution.py:223
  (1 shorter events, 0.0 us)
Async XLA Ops:
  0.6 5.7 %all-to-all-start.3 = ((f32[2,32,4096]{2,1,0:T(8,128)}), f32[2,32,4096]{2,1,0:T(8,128)S(1)}, u32[]{:S(2)}, u32[]{:S(2)}) async-start(f32[2,32,4096]{2,1,0:T(8,128)} %bitcast.8), calls=%async_computation.3 | async-start | bytes 2097152 | tf_op jit(solution)/shard_map/all_to_all | solution.py:175
  4.2 0.7 copy-start.5
  7.2 14.8 %all-to-all-start.4 = ((f32[4,8,4096]{2,1,0:T(8,128)}), f32[4,8,4096]{2,1,0:T(8,128)S(1)}, u32[]{:S(2)}, u32[]{:S(2)}) async-start(f32[4,8,4096]{2,1,0:T(8,128)} %bitcast.4), calls=%async_computation.4 | async-start | bytes 1048576 | tf_op jit(solution)/shard_map/all_to_all | solution.py:184
  22.0 43.7 %copy-start = (s32[16,32,512]{2,1,0:T(8,128)S(1)}, s32[16,32,512]{2,1,0:T(8,128)}, u32[]{:S(2)}) copy-start(s32[16,32,512]{2,1,0:T(8,128)} %chosen_ref.1) | copy-start | bytes 3145732
  51.1 14.5 %copy-start.1 = (f32[1,64,512]{2,1,0:T(8,128)S(1)}, f32[1,64,512]{2,1,0:T(8,128)}, u32[]{:S(2)}) copy-start(f32[1,64,512]{2,1,0:T(8,128)} %momentum_ref.1) | copy-start | bytes 393220
  51.2 14.5 %copy-start.3 = (f32[64,64]{1,0:T(8,128)S(1)}, f32[64,64]{1,0:T(8,128)}, u32[]{:S(2)}) copy-start(f32[64,64]{1,0:T(8,128)} %constant.35.clone.back_ref) | copy-start | bytes 49156
  51.2 14.5 %copy-start.4 = (f32[64,64]{1,0:T(8,128)S(1)}, f32[64,64]{1,0:T(8,128)}, u32[]{:S(2)}) copy-start(f32[64,64]{1,0:T(8,128)} %constant.34.clone.table_ref) | copy-start | bytes 49156
  78.1 12.5 %copy-start.2 = (f32[64,512]{1,0:T(8,128)S(1)}, f32[64,512]{1,0:T(8,128)}, u32[]{:S(2)}) copy-start(f32[64,512]{1,0:T(8,128)} %weights_ref.1) | copy-start | bytes 393220

commit v6 on v5

--- a/solution.py
+++ b/solution.py
@@ -17,7 +17,7 @@
 NEAR = 8
 CHIPS = NEAR // 2
 SIDE = 4
-WIDTHS = (1536, 2048, 4096)
+WIDTHS = (1280, 1408, 1536, 1664, 1792, 2048, 2560, 4096)
 FAR = OWNERS // NEAR
 ROWS = BLOCK // NEAR
 
@@ -35,10 +35,11 @@
     return (norm * np.cos(np.pi * (2 * v + 1) * j / (2 * BLOCK))).astype(np.float32)
 
 
-def near_groups():
+def near_hop(hop, mirrored):
+    chips = OWNERS // 2
     return [
-        [(CHIPS * a + b + 2 * core) % (OWNERS // 2) * 2 + core for b in range(CHIPS)]
-        for a in range(FAR)
+        (2 * z + core, (z + (-hop if mirrored and core else hop)) % chips * 2 + core)
+        for z in range(chips)
         for core in range(2)
     ]
 
@@ -53,9 +54,12 @@
     return groups
 
 
-def add_cores_kernel(plan_ref, parts_ref, out_ref):
+def add_cores_kernel(plan_ref, parts_ref, *tile_refs):
     del plan_ref
-    out_ref[...] = parts_ref[0] + parts_ref[1]
+    place = lax.axis_index("zl")
+    for k, tile_ref in enumerate(tile_refs):
+        rows = pl.ds(pl.multiple_of((place + k) % CHIPS * ROWS, ROWS), ROWS)
+        tile_ref[...] = parts_ref[0, rows, :] + parts_ref[1, rows, :]
 
 
 def plan_kernel(where_ref, counts_ref, plan_ref, branch_ref):
@@ -73,8 +77,8 @@
     branch_ref[0] = sum((reach > width).astype(jnp.int32) for width in WIDTHS[:-1])
 
 
-def spread_kernel(width, plan_ref, parts_ref, out_ref, total_ref):
-    total_ref[:, :BLOCKS] = jnp.sum(parts_ref[...], axis=0)
+def spread_kernel(width, plan_ref, own_ref, next_ref, across_ref, before_ref, out_ref, total_ref):
+    total_ref[:, :BLOCKS] = (own_ref[...] + next_ref[...]) + (across_ref[...] + before_ref[...])
     total_ref[:, BLOCKS:] = jnp.zeros((ROWS, width), jnp.float32)
     for a in range(FAR):
         base = pl.multiple_of((plan_ref[2 + NEAR * a] // 128) * 128, 128)
@@ -99,19 +103,19 @@
             out_ref[i, :, 128 * t : 128 * (t + 1)] = jnp.where(lane < 128 - shift, tiles[t], tiles[t + 1])
 
 
-def deliver(width, plan, far, near):
+def deliver(width, plan, far, *near):
     smem = pl.BlockSpec(memory_space=pltpu.SMEM)
     whole = pl.BlockSpec(memory_space=pltpu.VMEM)
     small = pltpu.CompilerParams(vmem_limit_bytes=8 << 20)
     spread = pl.pallas_call(
         functools.partial(spread_kernel, width),
         out_shape=jax.ShapeDtypeStruct((FAR, ROWS, width), jnp.float32),
-        in_specs=[smem, whole],
+        in_specs=[smem] + [whole] * CHIPS,
         out_specs=whole,
         scratch_shapes=[pltpu.VMEM((ROWS, BLOCKS + width), jnp.float32)],
         compiler_params=small,
         name=f"spread_{width}",
-    )(plan, near)
+    )(plan, *near)
     met = lax.all_to_all(spread, "zh", 0, 0, tiled=False)
     return pl.pallas_call(
         functools.partial(window_kernel, width),
@@ -127,7 +131,7 @@
 def owner_kernel(place_ref, parts_ref, momentum_ref, chosen_ref, table_ref, back_ref, momentum_out_ref, copies_ref):
     count = place_ref[1]
     live = lax.broadcasted_iota(jnp.int32, (BLOCK, MOST), 1) < count
-    gradient = jnp.concatenate([parts_ref[(b + 2 * c) % CHIPS, c] for c in range(2) for b in range(CHIPS)], axis=0) * (1.0 / OWNERS)
+    gradient = jnp.concatenate([parts_ref[b, c] for c in range(2) for b in range(CHIPS)], axis=0) * (1.0 / OWNERS)
     accumulated = jnp.where(live, momentum_decay * momentum_ref[0] + gradient, 0.0)
     coeffs = jnp.dot(table_ref[...], accumulated, precision=lax.Precision.HIGHEST, preferred_element_type=jnp.float32)
     chosen = chosen_ref[0]
@@ -173,16 +177,19 @@
     whole = pl.BlockSpec(memory_space=pltpu.VMEM)
 
     halves = lax.all_to_all(partials.reshape(2, BLOCK // 2, BLOCKS), "core", 0, 0, tiled=False)
-    half = pl.pallas_call(
+    tiles = pl.pallas_call(
         add_cores_kernel,
-        out_shape=jax.ShapeDtypeStruct((BLOCK // 2, BLOCKS), jnp.float32),
+        out_shape=[jax.ShapeDtypeStruct((ROWS, BLOCKS), jnp.float32)] * CHIPS,
         in_specs=[pl.BlockSpec(memory_space=pl.ANY), whole],
-        out_specs=whole,
+        out_specs=[whole] * CHIPS,
         compiler_params=pltpu.CompilerParams(vmem_limit_bytes=8 << 20),
         name="add_cores",
     )(place, halves)
-    near = lax.all_to_all(half.reshape(CHIPS, ROWS, BLOCKS), FSDP, 0, 0, axis_index_groups=near_groups(), tiled=False)
-    windows = lax.switch(branch[0], [functools.partial(deliver, width) for width in WIDTHS], place, far, near)
+    across = lax.ppermute(tiles[2], FSDP, near_hop(-2, True))
+    following = lax.ppermute(tiles[1], FSDP, near_hop(1, False))
+    before = lax.ppermute(tiles[3], FSDP, near_hop(-1, False))
+    near = (tiles[0], following, across, before)
+    windows = lax.switch(branch[0], [functools.partial(deliver, width) for width in WIDTHS], place, far, *near)
     blocks = lax.all_to_all(windows, ("zl", "core"), 0, 0, tiled=False).reshape(CHIPS, 2, ROWS, MOST)
 
     table = dct_matrix()

time: 92.9 us -> 95 us (1.023)
  starting transfers between devices: 9.48 us -> 21.3 us
  waiting for transfers between devices: 8.49 us -> 3.54 us
  blocking collectives: 65.4 us -> 61.4 us
    ppermute x0 -> x3, starting transfers between devices: none -> 17.7 us  [the longest x1 10.9 us: body(): across = lax.ppermute(tiles[2], FSDP, near_hop(-2, True))]
    all_to_all x1 -> x0, waiting for transfers between devices: 8.23 us -> none  [body(): lax.all_to_all(half.reshape(CHIPS, ROWS, BLOCKS), FSDP, 0, 0, axis_index_...]
    all_to_all x1 -> x0, starting transfers between devices: 5.89 us -> none  [body(): lax.all_to_all(half.reshape(CHIPS, ROWS, BLOCKS), FSDP, 0, 0, axis_index_...]
    ppermute x0 -> x3, waiting for transfers between devices: none -> 3.28 us  [the longest x1 2.12 us: body(): before = lax.ppermute(tiles[3], FSDP, near_hop(-1, False))]
    all_to_all x1, blocking collectives: 14.5 us -> 11.5 us  [body(): lax.all_to_all(windows, ('zl', 'core'), 0, 0, tiled=False)]
    all_to_all x1, blocking collectives: 27.9 us -> 26.9 us  [deliver(): met = lax.all_to_all(spread, 'zh', 0, 0, tiled=False)]
  transfers between devices with their start and end apart: 2 -> 4, of which waited for: 2 -> 3; matrix products, arithmetic and copies ran while one was open for 0% -> 0% of each run, Pallas kernels for 1% -> 1%
where the time goes in v6:
time: 95 us; the launch traced here: 93.9 us
  blocking collectives  61.4 us (65%)
  starting transfers between devices  21.3 us (22%)
  Pallas kernels  5.57 us (6%)
  waiting for transfers between devices  3.54 us (4%)
  between operations  1.41 us (1%)
    all_to_all x1, blocking collectives, deliver(): met = lax.all_to_all(spread, 'zh', 0, 0, tiled=False)  26.9 us
    all_to_all x1, blocking collectives, body(): lax.all_to_all(copies, REP + FSDP, 0, 0, axis_index_groups=rep_groups(1),...  12.5 us
    all_to_all x1, blocking collectives, body(): lax.all_to_all(windows, ('zl', 'core'), 0, 0, tiled=False)  11.5 us
    ppermute x1, starting transfers between devices, body(): across = lax.ppermute(tiles[2], FSDP, near_hop(-2, True))  10.9 us
    all_to_all x1, blocking collectives, body(): lax.all_to_all(copies, REP + FSDP, 0, 0, axis_index_groups=rep_groups(0),...  10.6 us
    ppermute x1, starting transfers between devices, body(): following = lax.ppermute(tiles[1], FSDP, near_hop(1, False))  3.83 us
    all_to_all x1, starting transfers between devices, body(): lax.all_to_all(partials.reshape(2, BLOCK // 2, BLOCKS), 'core', 0, 0, til...  3.59 us
    ppermute x1, starting transfers between devices, body(): before = lax.ppermute(tiles[3], FSDP, near_hop(-1, False))  2.92 us
  transfers between devices with their start and end apart: 4, of which 3 were waited for; matrix products, arithmetic and copies ran while one was open for 0% of the time, Pallas kernels for 1%

profile of v6, /device:TPU:6, one launch (start us, length us, event | category | flops | bytes accessed | tf_op | source)
XLA Modules:
  0.0 93.9 jit_solution(2421481134343666222)
XLA Ops:
  0.6 3.6 %all-to-all-start.8 = ((f32[2,32,4096]{2,1,0:T(8,128)}), f32[2,32,4096]{2,1,0:T(8,128)S(1)}, u32[]{:S(2)}, u32[]{:S(2)}) async-start(f32[2,32,4096]{2,1,0:T(8,128)} %bitcast.7), calls=%async_computation.8 | async-start | bytes 2097152 | tf_op jit(solution)/shard_map/all_to_all | solution.py:179
  4.2 0.0 copy-start.5
  4.2 0.1 pad_add_fusion.where_ref
  4.3 0.6 copy-done.5
  4.9 1.2 %plan.1 = (s32[34]{0:T(128)S(1)}, s32[1]{0:T(128)}) custom-call(s32[2]{0:T(128)S(1)} %pad_add_fusion.where_ref, s32[32]{0:T(128)S(1)} %copy-done.5), custom_call_target="tpu_custom_call" | custom-call | tf_op jit(solution)/shard_map/plan/pallas_call | solution.py:169
  6.1 0.3 all-to-all-done.8.parts_ref
  6.3 0.1 add_cores.1
  6.4 3.8 %collective-permute-start = (f32[8,4096]{1,0:T(8,128)S(1)}, f32[8,4096]{1,0:T(8,128)S(1)}, u32[]{:S(2)}, u32[]{:S(2)}) collective-permute-start(f32[8,4096]{1,0:T(8,128)S(1)} %get-tuple-element.166), channel_id=1, source_target_pairs={{0,2},{1,3},{2,4},{3,5},{4,6},{5,7},{6,8},{7,9},{8,10},{9,11},{10,... | collective-permute-start | bytes 393224 | tf_op jit(solution)/shard_map/ppermute | solution.py:189
  10.2 10.9 %collective-permute-start.1 = (f32[8,4096]{1,0:T(8,128)S(1)}, f32[8,4096]{1,0:T(8,128)S(1)}, u32[]{:S(2)}, u32[]{:S(2)}) collective-permute-start(f32[8,4096]{1,0:T(8,128)S(1)} %get-tuple-element.167), channel_id=1, source_target_pairs={{0,28},{1,5},{2,30},{3,7},{4,0},{5,9},{6,2},{7,11},{8,4},{9,13},{1... | collective-permute-start | bytes 393224 | tf_op jit(solution)/shard_map/ppermute | solution.py:188
  21.2 2.9 %collective-permute-start.2 = (f32[8,4096]{1,0:T(8,128)S(1)}, f32[8,4096]{1,0:T(8,128)S(1)}, u32[]{:S(2)}, u32[]{:S(2)}) collective-permute-start(f32[8,4096]{1,0:T(8,128)S(1)} %get-tuple-element.168), channel_id=1, source_target_pairs={{0,30},{1,31},{2,0},{3,1},{4,2},{5,3},{6,4},{7,5},{8,6},{9,7},{10,... | collective-permute-start | bytes 393224 | tf_op jit(solution)/shard_map/ppermute | solution.py:190
  24.8 0.0 collective-permute-done
  24.8 1.2 %collective-permute-done.1 = f32[8,4096]{1,0:T(8,128)S(1)} collective-permute-done((f32[8,4096]{1,0:T(8,128)S(1)}, f32[8,4096]{1,0:T(8,128)S(1)}, u32[]{:S(2)}, u32[]{:S(2)}) %collective-permute-start.1) | collective-permute-done | bytes 131104 | tf_op jit(solution)/shard_map/ppermute | solution.py:188
  25.9 2.1 %collective-permute-done.2 = f32[8,4096]{1,0:T(8,128)S(1)} collective-permute-done((f32[8,4096]{1,0:T(8,128)S(1)}, f32[8,4096]{1,0:T(8,128)S(1)}, u32[]{:S(2)}, u32[]{:S(2)}) %collective-permute-start.2) | collective-permute-done | bytes 131104 | tf_op jit(solution)/shard_map/ppermute | solution.py:190
  28.0 0.0 copy-start
  28.0 28.2 %conditional.1 = (f32[8,8,512]{2,1,0:T(8,128)S(1)}) conditional(s32[]{:T(128)} %bitcast.2, (s32[34]{0:T(128)S(1)}, f32[8,4096]{1,0:T(8,128)S(1)}, f32[8,4096]{1,0:T(8,128)S(1)}, f32[8,4096]{1,0:T(8,128)S(1)}, f32[8,4096]{1,0:T(8,128)S(1)}, /*index=5*/s32[1]{0:T(128)}) %tuple.32, (s32[34]{0:T(128)S(1)}, ...), branch_computations={%region_0.0_spmd, %region_1.0_spmd, %region_2.0_spmd, %region_3.0_... | conditional | bytes 1048584 | solution.py:192
  28.0 0.6 spread_2048.1
  28.6 26.9 %all_to_all.57.parts_ref = f32[4,8,2048]{2,1,0:T(8,128)S(1)} all-to-all(f32[4,8,2048]{2,1,0:T(8,128)S(1)} %spread_2048.1), channel_id=1, replica_groups=mesh['y'=4,'x'=4,'zh'=4,'zl'=4,'core'=2] {'zh'}, dimensions={0} | all-to-all | bytes 524288 | tf_op jit(solution)/shard_map/cond/branch_5_fun/all_to_all | solution.py:119
  55.5 0.7 windows_2048.1
  56.3 0.0 copy-start.1
  56.3 0.0 copy-start.3
  56.3 0.0 copy-start.4
  56.3 11.5 %all_to_all.60 = f32[8,8,512]{2,1,0:T(8,128)S(1)} all-to-all(f32[8,8,512]{2,1,0:T(8,128)S(1)} %get-tuple-element.171), channel_id=1, replica_groups=mesh['y'=4,'x'=4,'zh'=4,'zl'=4,'core'=2] {'zl','core'}, dimensions={0} | all-to-all | bytes 262144 | tf_op jit(solution)/shard_map/all_to_all | solution.py:193
  67.8 0.0 copy-done
  67.8 0.0 copy-done.1
  67.8 0.0 copy-done.3
  67.8 0.0 copy-done.4
  67.8 1.8 %owner_step.1 = (f32[1,64,512]{2,1,0:T(8,128)}, f32[4,64,512]{2,1,0:T(8,128)S(1)}) custom-call(s32[34]{0:T(128)S(1)} %get-tuple-element.163.plan_ref.place_ref, f32[4,2,8,512]{3,2,1,0:T(8,128)S(1)} %bitcast.6, f32[1,64,512]{2,1,0:T(8,128)S(1)} %copy-done.1, s32[16,32,512]{2,1,0:T(8,128)S(1)} %copy-done, f32[64,64]{1,0:T(8,128)S(1)} %copy-done.4, ...), custom_call_target="tpu_custom_call" | custom-call | tf_op jit(solution)/shard_map/owner_step/pallas_call | solution.py:196
  69.6 10.6 %all_to_all.61.parts_ref = f32[4,64,512]{2,1,0:T(8,128)S(1)} all-to-all(f32[4,64,512]{2,1,0:T(8,128)S(1)} %get-tuple-element.170), channel_id=1, replica_groups={{0,32,64,96},{128,160,192,224},{256,288,320,352},{384,416,448,480},{2,3..., dimensions={0} | all-to-all | bytes 1048576 | tf_op jit(solution)/shard_map/all_to_all | solution.py:220
  80.2 0.0 copy-start.2
  80.2 12.5 %all_to_all.62.parts_ref = f32[4,64,512]{2,1,0:T(8,128)S(1)} all-to-all(f32[4,64,512]{2,1,0:T(8,128)S(1)} %add_row.1), channel_id=1, replica_groups={{0,128,256,384},{32,160,288,416},{64,192,320,448},{96,224,352,480},{2,1..., dimensions={0} | all-to-all | bytes 1048576 | tf_op jit(solution)/shard_map/all_to_all | solution.py:229
  92.7 0.0 copy-done.2
  92.7 1.2 %weights_step.1 = f32[64,512]{1,0:T(8,128)} custom-call(s32[34]{0:T(128)S(1)} %get-tuple-element.163.plan_ref.place_ref, f32[4,64,512]{2,1,0:T(8,128)S(1)} %all_to_all.62.parts_ref, f32[64,512]{1,0:T(8,128)S(1)} %copy-done.2), custom_call_target="tpu_custom_call" | custom-call | tf_op jit(solution)/shard_map/weights_step/pallas_call | solution.py:230
  (1 shorter events, 0.0 us)
Async XLA Ops:
  0.6 5.7 %all-to-all-start.8 = ((f32[2,32,4096]{2,1,0:T(8,128)}), f32[2,32,4096]{2,1,0:T(8,128)S(1)}, u32[]{:S(2)}, u32[]{:S(2)}) async-start(f32[2,32,4096]{2,1,0:T(8,128)} %bitcast.7), calls=%async_computation.8 | async-start | bytes 2097152 | tf_op jit(solution)/shard_map/all_to_all | solution.py:179
  4.2 0.7 copy-start.5
  6.4 18.4 %collective-permute-start = (f32[8,4096]{1,0:T(8,128)S(1)}, f32[8,4096]{1,0:T(8,128)S(1)}, u32[]{:S(2)}, u32[]{:S(2)}) collective-permute-start(f32[8,4096]{1,0:T(8,128)S(1)} %get-tuple-element.166), channel_id=1, source_target_pairs={{0,2},{1,3},{2,4},{3,5},{4,6},{5,7},{6,8},{7,9},{8,10},{9,11},{10,... | collective-permute-start | bytes 393224 | tf_op jit(solution)/shard_map/ppermute | solution.py:189
  10.2 15.7 %collective-permute-start.1 = (f32[8,4096]{1,0:T(8,128)S(1)}, f32[8,4096]{1,0:T(8,128)S(1)}, u32[]{:S(2)}, u32[]{:S(2)}) collective-permute-start(f32[8,4096]{1,0:T(8,128)S(1)} %get-tuple-element.167), channel_id=1, source_target_pairs={{0,28},{1,5},{2,30},{3,7},{4,0},{5,9},{6,2},{7,11},{8,4},{9,13},{1... | collective-permute-start | bytes 393224 | tf_op jit(solution)/shard_map/ppermute | solution.py:188
  21.2 6.9 %collective-permute-start.2 = (f32[8,4096]{1,0:T(8,128)S(1)}, f32[8,4096]{1,0:T(8,128)S(1)}, u32[]{:S(2)}, u32[]{:S(2)}) collective-permute-start(f32[8,4096]{1,0:T(8,128)S(1)} %get-tuple-element.168), channel_id=1, source_target_pairs={{0,30},{1,31},{2,0},{3,1},{4,2},{5,3},{6,4},{7,5},{8,6},{9,7},{10,... | collective-permute-start | bytes 393224 | tf_op jit(solution)/shard_map/ppermute | solution.py:190
  28.0 39.8 %copy-start = (s32[16,32,512]{2,1,0:T(8,128)S(1)}, s32[16,32,512]{2,1,0:T(8,128)}, u32[]{:S(2)}) copy-start(s32[16,32,512]{2,1,0:T(8,128)} %chosen_ref.1) | copy-start | bytes 3145732
  56.3 11.5 %copy-start.1 = (f32[1,64,512]{2,1,0:T(8,128)S(1)}, f32[1,64,512]{2,1,0:T(8,128)}, u32[]{:S(2)}) copy-start(f32[1,64,512]{2,1,0:T(8,128)} %momentum_ref.1) | copy-start | bytes 393220
  56.3 11.5 %copy-start.3 = (f32[64,64]{1,0:T(8,128)S(1)}, f32[64,64]{1,0:T(8,128)}, u32[]{:S(2)}) copy-start(f32[64,64]{1,0:T(8,128)} %constant.36.clone.back_ref) | copy-start | bytes 49156
  56.3 11.5 %copy-start.4 = (f32[64,64]{1,0:T(8,128)S(1)}, f32[64,64]{1,0:T(8,128)}, u32[]{:S(2)}) copy-start(f32[64,64]{1,0:T(8,128)} %constant.35.clone.table_ref) | copy-start | bytes 49156
  80.2 12.5 %copy-start.2 = (f32[64,512]{1,0:T(8,128)S(1)}, f32[64,512]{1,0:T(8,128)}, u32[]{:S(2)}) copy-start(f32[64,512]{1,0:T(8,128)} %weights_ref.1) | copy-start | bytes 393220

commit v7 on v6

--- a/solution.py
+++ b/solution.py
@@ -35,13 +35,17 @@
     return (norm * np.cos(np.pi * (2 * v + 1) * j / (2 * BLOCK))).astype(np.float32)
 
 
-def near_hop(hop, mirrored):
+def near_pairs(kind):
     chips = OWNERS // 2
-    return [
-        (2 * z + core, (z + (-hop if mirrored and core else hop)) % chips * 2 + core)
-        for z in range(chips)
-        for core in range(2)
-    ]
+    pairs = []
+    for z in range(chips):
+        for core in range(2):
+            if kind == 2:
+                hop = 2 if (z + 2 * core) % CHIPS < 2 else -2
+            else:
+                hop = 1 if (z + core + kind) % 2 == 0 else -1
+            pairs.append((2 * z + core, (z + hop) % chips * 2 + core))
+    return pairs
 
 
 def rep_groups(turn):
@@ -57,8 +61,9 @@
 def add_cores_kernel(plan_ref, parts_ref, *tile_refs):
     del plan_ref
     place = lax.axis_index("zl")
-    for k, tile_ref in enumerate(tile_refs):
-        rows = pl.ds(pl.multiple_of((place + k) % CHIPS * ROWS, ROWS), ROWS)
+    up = 1 + 2 * ((place + lax.axis_index("core")) % 2)
+    for hop, tile_ref in zip((0, up, 4 - up, 2), tile_refs):
+        rows = pl.ds(pl.multiple_of((place + hop) % CHIPS * ROWS, ROWS), ROWS)
         tile_ref[...] = parts_ref[0, rows, :] + parts_ref[1, rows, :]
 
 
@@ -77,8 +82,9 @@
     branch_ref[0] = sum((reach > width).astype(jnp.int32) for width in WIDTHS[:-1])
 
 
-def spread_kernel(width, plan_ref, own_ref, next_ref, across_ref, before_ref, out_ref, total_ref):
-    total_ref[:, :BLOCKS] = (own_ref[...] + next_ref[...]) + (across_ref[...] + before_ref[...])
+def spread_kernel(width, plan_ref, after_ref, own_ref, next_ref, other_ref, across_ref, out_ref, total_ref):
+    del after_ref
+    total_ref[:, :BLOCKS] = (own_ref[...] + next_ref[...]) + (other_ref[...] + across_ref[...])
     total_ref[:, BLOCKS:] = jnp.zeros((ROWS, width), jnp.float32)
     for a in range(FAR):
         base = pl.multiple_of((plan_ref[2 + NEAR * a] // 128) * 128, 128)
@@ -103,19 +109,19 @@
             out_ref[i, :, 128 * t : 128 * (t + 1)] = jnp.where(lane < 128 - shift, tiles[t], tiles[t + 1])
 
 
-def deliver(width, plan, far, *near):
+def deliver(width, plan, far, after, *near):
     smem = pl.BlockSpec(memory_space=pltpu.SMEM)
     whole = pl.BlockSpec(memory_space=pltpu.VMEM)
     small = pltpu.CompilerParams(vmem_limit_bytes=8 << 20)
     spread = pl.pallas_call(
         functools.partial(spread_kernel, width),
         out_shape=jax.ShapeDtypeStruct((FAR, ROWS, width), jnp.float32),
-        in_specs=[smem] + [whole] * CHIPS,
+        in_specs=[smem, pl.BlockSpec(memory_space=pl.ANY)] + [whole] * CHIPS,
         out_specs=whole,
         scratch_shapes=[pltpu.VMEM((ROWS, BLOCKS + width), jnp.float32)],
         compiler_params=small,
         name=f"spread_{width}",
-    )(plan, *near)
+    )(plan, after, *near)
     met = lax.all_to_all(spread, "zh", 0, 0, tiled=False)
     return pl.pallas_call(
         functools.partial(window_kernel, width),
@@ -128,12 +134,13 @@
     )(plan, far, met)
 
 
-def owner_kernel(place_ref, parts_ref, momentum_ref, chosen_ref, table_ref, back_ref, momentum_out_ref, copies_ref):
-    count = place_ref[1]
-    live = lax.broadcasted_iota(jnp.int32, (BLOCK, MOST), 1) < count
-    gradient = jnp.concatenate([parts_ref[b, c] for c in range(2) for b in range(CHIPS)], axis=0) * (1.0 / OWNERS)
-    accumulated = jnp.where(live, momentum_decay * momentum_ref[0] + gradient, 0.0)
-    coeffs = jnp.dot(table_ref[...], accumulated, precision=lax.Precision.HIGHEST, preferred_element_type=jnp.float32)
+def prepare_kernel(place_ref, after_ref, momentum_ref, chosen_ref, table_ref, decayed_ref, listed_ref, sparse_ref, live_ref):
+    del after_ref
+    live = lax.broadcasted_iota(jnp.int32, (BLOCK, MOST), 1) < place_ref[1]
+    decayed = jnp.where(live, momentum_decay * momentum_ref[0], 0.0)
+    decayed_ref[...] = decayed
+    live_ref[...] = live[:8].astype(jnp.float32)
+    coeffs = jnp.dot(table_ref[...], decayed, precision=lax.Precision.HIGHEST, preferred_element_type=jnp.float32)
     chosen = chosen_ref[0]
     bit = jnp.left_shift(jnp.int32(1), chosen & 31)
     low = jnp.sum(jnp.where(chosen < 32, bit, 0), axis=0, keepdims=True)
@@ -142,9 +149,17 @@
     listed = jnp.concatenate(
         [jnp.right_shift(jnp.broadcast_to(word, (32, MOST)), number) & 1 for word in (low, high)], axis=0
     )
-    sparse = jnp.where(listed != 0, coeffs, 0.0)
+    listed_ref[...] = listed
+    sparse_ref[...] = jnp.where(listed != 0, coeffs, 0.0)
+
+
+def owner_kernel(parts_ref, decayed_ref, listed_ref, sparse_ref, live_ref, table_ref, back_ref, left_ref, copies_ref):
+    gathered = jnp.concatenate([parts_ref[b, c] for c in range(2) for b in range(CHIPS)], axis=0)
+    gradient = jnp.where(live_ref[:1, :] != 0, gathered * (1.0 / OWNERS), 0.0)
+    coeffs = jnp.dot(table_ref[...], gradient, precision=lax.Precision.HIGHEST, preferred_element_type=jnp.float32)
+    sparse = sparse_ref[...] + jnp.where(listed_ref[...] != 0, coeffs, 0.0)
     own = jnp.dot(back_ref[...], sparse, precision=lax.Precision.HIGHEST, preferred_element_type=jnp.float32)
-    momentum_out_ref[0] = jnp.where(live, accumulated - own, 0.0)
+    left_ref[...] = decayed_ref[...] + gradient - own
     for r in range(SIDE):
         copies_ref[r] = own
 
@@ -155,10 +170,10 @@
         copies_ref[r] = added
 
 
-def weights_kernel(place_ref, parts_ref, weights_ref, out_ref):
-    live = lax.broadcasted_iota(jnp.int32, (BLOCK, MOST), 1) < place_ref[1]
+def last_kernel(live_ref, left_ref, parts_ref, weights_ref, momentum_out_ref, out_ref):
+    momentum_out_ref[0] = left_ref[...]
     update = jnp.sum(parts_ref[...], axis=0) * (1.0 / GROUPS)
-    out_ref[...] = jnp.where(live, weights_ref[...] - step_rate * update, 0.0)
+    out_ref[...] = jnp.where(live_ref[:1, :] != 0, weights_ref[...] - step_rate * update, 0.0)
 
 
 def body(partials, owner_blocks, momentum, weights, selected):
@@ -175,6 +190,7 @@
         name="plan",
     )(jnp.stack([group, owner]).astype(jnp.int32), owner_blocks)
     whole = pl.BlockSpec(memory_space=pltpu.VMEM)
+    small = pltpu.CompilerParams(vmem_limit_bytes=8 << 20)
 
     halves = lax.all_to_all(partials.reshape(2, BLOCK // 2, BLOCKS), "core", 0, 0, tiled=False)
     tiles = pl.pallas_call(
@@ -185,38 +201,37 @@
         compiler_params=pltpu.CompilerParams(vmem_limit_bytes=8 << 20),
         name="add_cores",
     )(place, halves)
-    across = lax.ppermute(tiles[2], FSDP, near_hop(-2, True))
-    following = lax.ppermute(tiles[1], FSDP, near_hop(1, False))
-    before = lax.ppermute(tiles[3], FSDP, near_hop(-1, False))
-    near = (tiles[0], following, across, before)
-    windows = lax.switch(branch[0], [functools.partial(deliver, width) for width in WIDTHS], place, far, *near)
-    blocks = lax.all_to_all(windows, ("zl", "core"), 0, 0, tiled=False).reshape(CHIPS, 2, ROWS, MOST)
-
-    table = dct_matrix()
-    new_momentum, copies = pl.pallas_call(
-        owner_kernel,
-        out_shape=(
-            jax.ShapeDtypeStruct((1, BLOCK, MOST), jnp.float32),
-            jax.ShapeDtypeStruct((SIDE, BLOCK, MOST), jnp.float32),
-        ),
+    table, back = jnp.asarray(dct_matrix()), jnp.asarray(dct_matrix().T)
+    square = jax.ShapeDtypeStruct((BLOCK, MOST), jnp.float32)
+    decayed, listed, sparse, live = pl.pallas_call(
+        prepare_kernel,
+        out_shape=(square, jax.ShapeDtypeStruct((BLOCK, MOST), jnp.int32), square, jax.ShapeDtypeStruct((8, MOST), jnp.float32)),
         grid_spec=pltpu.PrefetchScalarGridSpec(
             num_scalar_prefetch=1,
             grid=(1,),
             in_specs=[
-                pl.BlockSpec((CHIPS, 2, ROWS, MOST), lambda i, place: (0, 0, 0, 0)),
+                pl.BlockSpec(memory_space=pl.ANY),
                 pl.BlockSpec((1, BLOCK, MOST), lambda i, place: (0, 0, 0)),
                 pl.BlockSpec((1, K, MOST), lambda i, place: (place[0], 0, 0)),
                 pl.BlockSpec((BLOCK, BLOCK), lambda i, place: (0, 0)),
-                pl.BlockSpec((BLOCK, BLOCK), lambda i, place: (0, 0)),
             ],
-            out_specs=[
-                pl.BlockSpec((1, BLOCK, MOST), lambda i, place: (0, 0, 0)),
-                pl.BlockSpec((SIDE, BLOCK, MOST), lambda i, place: (0, 0, 0)),
-            ],
+            out_specs=[pl.BlockSpec((BLOCK, MOST), lambda i, place: (0, 0))] * 3 + [pl.BlockSpec((8, MOST), lambda i, place: (0, 0))],
         ),
-        compiler_params=pltpu.CompilerParams(vmem_limit_bytes=16 << 20),
+        compiler_params=small,
+        name="prepare",
+    )(place, tiles[0], momentum, selected, table)
+    near = [tiles[0]] + [lax.ppermute(tiles[1 + kind], FSDP, near_pairs(kind)) for kind in range(3)]
+    windows = lax.switch(branch[0], [functools.partial(deliver, width) for width in WIDTHS], place, far, sparse, *near)
+    blocks = lax.all_to_all(windows, ("zl", "core"), 0, 0, tiled=False).reshape(CHIPS, 2, ROWS, MOST)
+
+    left, copies = pl.pallas_call(
+        owner_kernel,
+        out_shape=(square, jax.ShapeDtypeStruct((SIDE, BLOCK, MOST), jnp.float32)),
+        in_specs=[whole] * 7,
+        out_specs=(whole, whole),
+        compiler_params=small,
         name="owner_step",
-    )(place, blocks, momentum, selected, jnp.asarray(table), jnp.asarray(table.T))
+    )(blocks, decayed, listed, sparse, live, table, back)
     row = lax.all_to_all(copies, REP + FSDP, 0, 0, axis_index_groups=rep_groups(0), tiled=False)
     copies = pl.pallas_call(
         add_row_kernel,
@@ -227,14 +242,14 @@
         name="add_row",
     )(row)
     everyone = lax.all_to_all(copies, REP + FSDP, 0, 0, axis_index_groups=rep_groups(1), tiled=False)
-    new_weights = pl.pallas_call(
-        weights_kernel,
-        out_shape=jax.ShapeDtypeStruct((BLOCK, MOST), jnp.float32),
-        in_specs=[pl.BlockSpec(memory_space=pltpu.SMEM), whole, whole],
-        out_specs=whole,
-        compiler_params=pltpu.CompilerParams(vmem_limit_bytes=8 << 20),
+    new_momentum, new_weights = pl.pallas_call(
+        last_kernel,
+        out_shape=(jax.ShapeDtypeStruct((1, BLOCK, MOST), jnp.float32), square),
+        in_specs=[whole] * 4,
+        out_specs=(whole, whole),
+        compiler_params=small,
         name="weights_step",
-    )(place, everyone, weights)
+    )(live, left, everyone, weights)
     return new_momentum, new_weights
 
 

time: 95 us -> 91.3 us (0.961)
  blocking collectives: 61.4 us -> 58.8 us
  waiting for transfers between devices: 3.54 us -> 5.15 us
  starting transfers between devices: 21.3 us -> 20 us
    all_to_all x1, blocking collectives: 26.9 us -> 24.5 us  [deliver(): met = lax.all_to_all(spread, 'zh', 0, 0, tiled=False)]
    ppermute x3, starting transfers between devices: 17.7 us -> 16.2 us  [body(): lax.ppermute(tiles[1 + kind], FSDP, near_pairs(kind))]
    ppermute x3, waiting for transfers between devices: 3.28 us -> 4.33 us  [body(): lax.ppermute(tiles[1 + kind], FSDP, near_pairs(kind))]
    pallas_call x2 -> x3, Pallas kernels: 2.99 us -> 2.08 us  [the longest x1 0.8 us: body(): pl.pallas_call(prepare_kernel, out_shape=(square, jax.ShapeDtypeStruct((B...]
  transfers between devices with their start and end apart: 4 -> 4, of which waited for: 3 -> 2; matrix products, arithmetic and copies ran while one was open for 0% -> 0% of each run, Pallas kernels for 1% -> 2%
where the time goes in v7:
time: 91.3 us; the launch traced here: 90.1 us
  blocking collectives  58.8 us (64%)
  starting transfers between devices  20 us (22%)
  waiting for transfers between devices  5.15 us (6%)
  Pallas kernels  4.65 us (5%)
  between operations  1.45 us (2%)
    all_to_all x1, blocking collectives, deliver(): met = lax.all_to_all(spread, 'zh', 0, 0, tiled=False)  24.5 us
    ppermute x3, starting transfers between devices, body(): lax.ppermute(tiles[1 + kind], FSDP, near_pairs(kind))  16.2 us
    all_to_all x1, blocking collectives, body(): lax.all_to_all(copies, REP + FSDP, 0, 0, axis_index_groups=rep_groups(1),...  12.5 us
    all_to_all x1, blocking collectives, body(): lax.all_to_all(windows, ('zl', 'core'), 0, 0, tiled=False)  11.2 us
    all_to_all x1, blocking collectives, body(): lax.all_to_all(copies, REP + FSDP, 0, 0, axis_index_groups=rep_groups(0),...  10.6 us
    ppermute x3, waiting for transfers between devices, body(): lax.ppermute(tiles[1 + kind], FSDP, near_pairs(kind))  4.33 us
    all_to_all x1, starting transfers between devices, body(): lax.all_to_all(partials.reshape(2, BLOCK // 2, BLOCKS), 'core', 0, 0, til...  3.72 us
  transfers between devices with their start and end apart: 4, of which 2 were waited for; matrix products, arithmetic and copies ran while one was open for 0% of the time, Pallas kernels for 2%

profile of v7, /device:TPU:6, one launch (start us, length us, event | category | flops | bytes accessed | tf_op | source)
XLA Modules:
  0.0 90.1 jit_solution(8280712119618211278)
XLA Ops:
  0.6 0.0 copy-start.5
  0.6 0.0 copy-start.1
  0.7 3.7 %all-to-all-start.8 = ((f32[2,32,4096]{2,1,0:T(8,128)}), f32[2,32,4096]{2,1,0:T(8,128)S(1)}, u32[]{:S(2)}, u32[]{:S(2)}) async-start(f32[2,32,4096]{2,1,0:T(8,128)} %bitcast.7), calls=%async_computation.8 | async-start | bytes 2097152 | tf_op jit(solution)/shard_map/all_to_all | solution.py:195
  4.4 0.0 copy-start
  4.4 0.1 pad_add_fusion.where_ref
  4.5 0.0 copy-done.5
  4.5 1.2 %plan.1 = (s32[34]{0:T(128)S(1)}, s32[1]{0:T(128)}) custom-call(s32[2]{0:T(128)S(1)} %pad_add_fusion.where_ref, s32[32]{0:T(128)S(1)} %copy-done.5), custom_call_target="tpu_custom_call" | custom-call | tf_op jit(solution)/shard_map/plan/pallas_call | solution.py:184
  5.7 0.8 all-to-all-done.8.parts_ref
  6.5 0.1 add_cores.1
  6.5 3.8 %collective-permute-start = (f32[8,4096]{1,0:T(8,128)S(1)}, f32[8,4096]{1,0:T(8,128)S(1)}, u32[]{:S(2)}, u32[]{:S(2)}) collective-permute-start(f32[8,4096]{1,0:T(8,128)S(1)} %get-tuple-element.196), channel_id=1, source_target_pairs={{0,2},{1,31},{2,0},{3,5},{4,6},{5,3},{6,4},{7,9},{8,10},{9,7},{10,... | collective-permute-start | bytes 393224 | tf_op jit(solution)/shard_map/ppermute | solution.py:223
  10.4 10.5 %collective-permute-start.1 = (f32[8,4096]{1,0:T(8,128)S(1)}, f32[8,4096]{1,0:T(8,128)S(1)}, u32[]{:S(2)}, u32[]{:S(2)}) collective-permute-start(f32[8,4096]{1,0:T(8,128)S(1)} %get-tuple-element.197), channel_id=1, source_target_pairs={{0,30},{1,3},{2,4},{3,1},{4,2},{5,7},{6,8},{7,5},{8,6},{9,11},{10,... | collective-permute-start | bytes 393224 | tf_op jit(solution)/shard_map/ppermute | solution.py:223
  20.9 1.9 %collective-permute-start.2 = (f32[8,4096]{1,0:T(8,128)S(1)}, f32[8,4096]{1,0:T(8,128)S(1)}, u32[]{:S(2)}, u32[]{:S(2)}) collective-permute-start(f32[8,4096]{1,0:T(8,128)S(1)} %get-tuple-element.198), channel_id=1, source_target_pairs={{0,4},{1,29},{2,6},{3,31},{4,0},{5,9},{6,2},{7,11},{8,12},{9,5},{1... | collective-permute-start | bytes 393224 | tf_op jit(solution)/shard_map/ppermute | solution.py:223
  23.5 0.0 copy-done.1
  23.5 0.0 copy-done
  23.5 0.0 copy-done.3
  23.5 0.8 prepare.1
  24.3 0.0 collective-permute-done
  24.3 0.0 collective-permute-done.1
  24.3 4.3 %collective-permute-done.2 = f32[8,4096]{1,0:T(8,128)S(1)} collective-permute-done((f32[8,4096]{1,0:T(8,128)S(1)}, f32[8,4096]{1,0:T(8,128)S(1)}, u32[]{:S(2)}, u32[]{:S(2)}) %collective-permute-start.2) | collective-permute-done | bytes 131104 | tf_op jit(solution)/shard_map/ppermute | solution.py:223
  28.6 25.8 %conditional.1 = (f32[8,8,512]{2,1,0:T(8,128)S(1)}) conditional(s32[]{:T(128)} %bitcast.3, (s32[34]{0:T(128)S(1)}, f32[64,512]{1,0:T(8,128)S(1)}, f32[8,4096]{1,0:T(8,128)S(1)}, f32[8,4096]{1,0:T(8,128)S(1)}, f32[8,4096]{1,0:T(8,128)S(1)}, /*index=5*/f32[8,4096]{1,0:T(8,128)S(1)}, s32[1]{0:T(128)}) %tuple.31, ...), branch_computations={%region_0.0_spmd, %region_1.0_spmd, %region_2.0_spmd, %region_3.0_... | conditional | bytes 1048584 | solution.py:224
  28.6 0.6 spread_1664.1
  29.2 24.5 %all_to_all.55.parts_ref = f32[4,8,1664]{2,1,0:T(8,128)S(1)} all-to-all(f32[4,8,1664]{2,1,0:T(8,128)S(1)} %spread_1664.1), channel_id=1, replica_groups=mesh['y'=4,'x'=4,'zh'=4,'zl'=4,'core'=2] {'zh'}, dimensions={0} | all-to-all | bytes 425984 | tf_op jit(solution)/shard_map/cond/branch_3_fun/all_to_all | solution.py:125
  53.8 0.7 windows_1664.1
  54.5 0.0 copy-start.4
  54.5 11.2 %all_to_all.60 = f32[8,8,512]{2,1,0:T(8,128)S(1)} all-to-all(f32[8,8,512]{2,1,0:T(8,128)S(1)} %get-tuple-element.203), channel_id=1, replica_groups=mesh['y'=4,'x'=4,'zh'=4,'zl'=4,'core'=2] {'zl','core'}, dimensions={0} | all-to-all | bytes 262144 | tf_op jit(solution)/shard_map/all_to_all | solution.py:225
  65.7 0.0 copy-done.4
  65.7 0.5 owner_step.1
  66.2 10.6 %all_to_all.61.parts_ref = f32[4,64,512]{2,1,0:T(8,128)S(1)} all-to-all(f32[4,64,512]{2,1,0:T(8,128)S(1)} %get-tuple-element.202), channel_id=1, replica_groups={{0,32,64,96},{128,160,192,224},{256,288,320,352},{384,416,448,480},{2,3..., dimensions={0} | all-to-all | bytes 1048576 | tf_op jit(solution)/shard_map/all_to_all | solution.py:235
  76.9 0.0 copy-start.2
  76.9 12.5 %all_to_all.62.parts_ref = f32[4,64,512]{2,1,0:T(8,128)S(1)} all-to-all(f32[4,64,512]{2,1,0:T(8,128)S(1)} %add_row.1), channel_id=1, replica_groups={{0,128,256,384},{32,160,288,416},{64,192,320,448},{96,224,352,480},{2,1..., dimensions={0} | all-to-all | bytes 1048576 | tf_op jit(solution)/shard_map/all_to_all | solution.py:244
  89.3 0.0 copy-done.2
  89.3 0.7 weights_step.1
  (2 shorter events, 0.0 us)
Async XLA Ops:
  0.6 3.9 %copy-start.5 = (s32[32]{0:T(128)S(1)}, s32[32]{0:T(128)}, u32[]{:S(2)}) copy-start(s32[32]{0:T(128)} %counts_ref.1) | copy-start | bytes 388
  0.6 22.8 %copy-start.1 = (f32[1,64,512]{2,1,0:T(8,128)S(1)}, f32[1,64,512]{2,1,0:T(8,128)}, u32[]{:S(2)}) copy-start(f32[1,64,512]{2,1,0:T(8,128)} %momentum_ref.1) | copy-start | bytes 393220
  0.7 5.8 %all-to-all-start.8 = ((f32[2,32,4096]{2,1,0:T(8,128)}), f32[2,32,4096]{2,1,0:T(8,128)S(1)}, u32[]{:S(2)}, u32[]{:S(2)}) async-start(f32[2,32,4096]{2,1,0:T(8,128)} %bitcast.7), calls=%async_computation.8 | async-start | bytes 2097152 | tf_op jit(solution)/shard_map/all_to_all | solution.py:195
  4.4 19.1 %copy-start = (s32[16,32,512]{2,1,0:T(8,128)S(1)}, s32[16,32,512]{2,1,0:T(8,128)}, u32[]{:S(2)}) copy-start(s32[16,32,512]{2,1,0:T(8,128)} %chosen_ref.1) | copy-start | bytes 3145732
  6.5 17.0 %copy-start.3 = (f32[64,64]{1,0:T(8,128)S(1)}, f32[64,64]{1,0:T(8,128)}, u32[]{:S(2)}) copy-start(f32[64,64]{1,0:T(8,128)} %constant.35.clone.table_ref) | copy-start | bytes 49156
  6.5 17.8 %collective-permute-start = (f32[8,4096]{1,0:T(8,128)S(1)}, f32[8,4096]{1,0:T(8,128)S(1)}, u32[]{:S(2)}, u32[]{:S(2)}) collective-permute-start(f32[8,4096]{1,0:T(8,128)S(1)} %get-tuple-element.196), channel_id=1, source_target_pairs={{0,2},{1,31},{2,0},{3,5},{4,6},{5,3},{6,4},{7,9},{8,10},{9,7},{10,... | collective-permute-start | bytes 393224 | tf_op jit(solution)/shard_map/ppermute | solution.py:223
  10.4 13.9 %collective-permute-start.1 = (f32[8,4096]{1,0:T(8,128)S(1)}, f32[8,4096]{1,0:T(8,128)S(1)}, u32[]{:S(2)}, u32[]{:S(2)}) collective-permute-start(f32[8,4096]{1,0:T(8,128)S(1)} %get-tuple-element.197), channel_id=1, source_target_pairs={{0,30},{1,3},{2,4},{3,1},{4,2},{5,7},{6,8},{7,5},{8,6},{9,11},{10,... | collective-permute-start | bytes 393224 | tf_op jit(solution)/shard_map/ppermute | solution.py:223
  20.9 7.8 %collective-permute-start.2 = (f32[8,4096]{1,0:T(8,128)S(1)}, f32[8,4096]{1,0:T(8,128)S(1)}, u32[]{:S(2)}, u32[]{:S(2)}) collective-permute-start(f32[8,4096]{1,0:T(8,128)S(1)} %get-tuple-element.198), channel_id=1, source_target_pairs={{0,4},{1,29},{2,6},{3,31},{4,0},{5,9},{6,2},{7,11},{8,12},{9,5},{1... | collective-permute-start | bytes 393224 | tf_op jit(solution)/shard_map/ppermute | solution.py:223
  54.5 11.2 %copy-start.4 = (f32[64,64]{1,0:T(8,128)S(1)}, f32[64,64]{1,0:T(8,128)}, u32[]{:S(2)}) copy-start(f32[64,64]{1,0:T(8,128)} %constant.36.clone.back_ref) | copy-start | bytes 49156
  76.9 12.5 %copy-start.2 = (f32[64,512]{1,0:T(8,128)S(1)}, f32[64,512]{1,0:T(8,128)}, u32[]{:S(2)}) copy-start(f32[64,512]{1,0:T(8,128)} %weights_ref.1) | copy-start | bytes 393220

commit v8 on v7

--- a/solution.py
+++ b/solution.py
@@ -67,38 +67,42 @@
         tile_ref[...] = parts_ref[0, rows, :] + parts_ref[1, rows, :]
 
 
-def plan_kernel(where_ref, counts_ref, plan_ref, branch_ref):
+def plan_kernel(where_ref, counts_ref, plan_ref, branch_ref, offsets_ref):
     plan_ref[0] = where_ref[0]
     plan_ref[1] = counts_ref[where_ref[1]]
+    far = where_ref[1] // NEAR
+    lane = lax.broadcasted_iota(jnp.int32, (8, 128), 1)
+    offsets = jnp.zeros((8, 128), jnp.int32)
     start = jnp.int32(0)
     reach = jnp.int32(0)
     first = jnp.int32(0)
     for i in range(OWNERS):
         if i % NEAR == 0:
             first = start - start % 128
-        plan_ref[2 + i] = start
+            offsets = jnp.where(lane == i // NEAR, first, offsets)
+        here = (lane == FAR + i % NEAR) & (far == i // NEAR)
+        offsets = jnp.where(here, start - first, offsets)
         start = start + counts_ref[i]
         reach = jnp.maximum(reach, start - first)
     branch_ref[0] = sum((reach > width).astype(jnp.int32) for width in WIDTHS[:-1])
-
-
-def spread_kernel(width, plan_ref, after_ref, own_ref, next_ref, other_ref, across_ref, out_ref, total_ref):
+    offsets_ref[...] = offsets
+
+
+def spread_kernel(width, offsets_ref, after_ref, own_ref, next_ref, other_ref, across_ref, out_ref, total_ref):
     del after_ref
     total_ref[:, :BLOCKS] = (own_ref[...] + next_ref[...]) + (other_ref[...] + across_ref[...])
     total_ref[:, BLOCKS:] = jnp.zeros((ROWS, width), jnp.float32)
     for a in range(FAR):
-        base = pl.multiple_of((plan_ref[2 + NEAR * a] // 128) * 128, 128)
+        base = pl.multiple_of(offsets_ref[0, a], 128)
         out_ref[a] = total_ref[:, pl.ds(base, width)]
 
 
-def window_kernel(width, plan_ref, far_ref, parts_ref, out_ref, total_ref):
+def window_kernel(width, offsets_ref, parts_ref, out_ref, total_ref):
     total_ref[:, :width] = jnp.sum(parts_ref[...], axis=0)
     total_ref[:, width:] = jnp.zeros((ROWS, MOST + 128), jnp.float32)
     lane = lax.broadcasted_iota(jnp.int32, (ROWS, 128), 1)
-    owner = far_ref[0] * NEAR
-    first = (plan_ref[2 + owner] // 128) * 128
     for i in range(NEAR):
-        start = plan_ref[2 + owner + i] - first
+        start = offsets_ref[0, FAR + i]
         base = pl.multiple_of((start // 128) * 128, 128)
         shift = start % 128
         tiles = [
@@ -109,29 +113,28 @@
             out_ref[i, :, 128 * t : 128 * (t + 1)] = jnp.where(lane < 128 - shift, tiles[t], tiles[t + 1])
 
 
-def deliver(width, plan, far, after, *near):
-    smem = pl.BlockSpec(memory_space=pltpu.SMEM)
+def deliver(width, offsets, after, *near):
     whole = pl.BlockSpec(memory_space=pltpu.VMEM)
     small = pltpu.CompilerParams(vmem_limit_bytes=8 << 20)
     spread = pl.pallas_call(
         functools.partial(spread_kernel, width),
         out_shape=jax.ShapeDtypeStruct((FAR, ROWS, width), jnp.float32),
-        in_specs=[smem, pl.BlockSpec(memory_space=pl.ANY)] + [whole] * CHIPS,
+        in_specs=[whole, pl.BlockSpec(memory_space=pl.ANY)] + [whole] * CHIPS,
         out_specs=whole,
         scratch_shapes=[pltpu.VMEM((ROWS, BLOCKS + width), jnp.float32)],
         compiler_params=small,
         name=f"spread_{width}",
-    )(plan, after, *near)
+    )(offsets, after, *near)
     met = lax.all_to_all(spread, "zh", 0, 0, tiled=False)
     return pl.pallas_call(
         functools.partial(window_kernel, width),
         out_shape=jax.ShapeDtypeStruct((NEAR, ROWS, MOST), jnp.float32),
-        in_specs=[smem, smem, whole],
+        in_specs=[whole, whole],
         out_specs=whole,
         scratch_shapes=[pltpu.VMEM((ROWS, width + MOST + 128), jnp.float32)],
         compiler_params=small,
         name=f"windows_{width}",
-    )(plan, far, met)
+    )(offsets, met)
 
 
 def prepare_kernel(place_ref, after_ref, momentum_ref, chosen_ref, table_ref, decayed_ref, listed_ref, sparse_ref, live_ref):
@@ -179,19 +182,17 @@
 def body(partials, owner_blocks, momentum, weights, selected):
     owner = lax.axis_index(FSDP)
     group = lax.axis_index(REP)
-    far = lax.axis_index("zh").reshape(1)
     smem = pl.BlockSpec(memory_space=pltpu.SMEM)
-    place, branch = pl.pallas_call(
+    whole = pl.BlockSpec(memory_space=pltpu.VMEM)
+    small = pltpu.CompilerParams(vmem_limit_bytes=8 << 20)
+    place, branch, offsets = pl.pallas_call(
         plan_kernel,
-        out_shape=(jax.ShapeDtypeStruct((2 + OWNERS,), jnp.int32), jax.ShapeDtypeStruct((1,), jnp.int32)),
+        out_shape=tuple(jax.ShapeDtypeStruct(shape, jnp.int32) for shape in ((2,), (1,), (8, 128))),
         in_specs=[smem, smem],
-        out_specs=(smem, smem),
+        out_specs=(smem, smem, whole),
         compiler_params=pltpu.CompilerParams(vmem_limit_bytes=1 << 20),
         name="plan",
     )(jnp.stack([group, owner]).astype(jnp.int32), owner_blocks)
-    whole = pl.BlockSpec(memory_space=pltpu.VMEM)
-    small = pltpu.CompilerParams(vmem_limit_bytes=8 << 20)
-
     halves = lax.all_to_all(partials.reshape(2, BLOCK // 2, BLOCKS), "core", 0, 0, tiled=False)
     tiles = pl.pallas_call(
         add_cores_kernel,
@@ -221,7 +222,7 @@
         name="prepare",
     )(place, tiles[0], momentum, selected, table)
     near = [tiles[0]] + [lax.ppermute(tiles[1 + kind], FSDP, near_pairs(kind)) for kind in range(3)]
-    windows = lax.switch(branch[0], [functools.partial(deliver, width) for width in WIDTHS], place, far, sparse, *near)
+    windows = lax.switch(branch[0], [functools.partial(deliver, width) for width in WIDTHS], offsets, sparse, *near)
     blocks = lax.all_to_all(windows, ("zl", "core"), 0, 0, tiled=False).reshape(CHIPS, 2, ROWS, MOST)
 
     left, copies = pl.pallas_call(

time: 91.3 us -> 88.7 us (0.972)
  blocking collectives: 58.8 us -> 57 us
    all_to_all x1, blocking collectives: 24.5 us -> 22.9 us  [deliver(): met = lax.all_to_all(spread, 'zh', 0, 0, tiled=False)]
where the time goes in v8:
time: 88.7 us; the launch traced here: 87.5 us
  blocking collectives  57 us (64%)
  starting transfers between devices  20 us (23%)
  waiting for transfers between devices  5.13 us (6%)
  Pallas kernels  3.77 us (4%)
  between operations  1.45 us (2%)
    all_to_all x1, blocking collectives, deliver(): met = lax.all_to_all(spread, 'zh', 0, 0, tiled=False)  22.9 us
    ppermute x3, starting transfers between devices, body(): lax.ppermute(tiles[1 + kind], FSDP, near_pairs(kind))  16.2 us
    all_to_all x1, blocking collectives, body(): lax.all_to_all(copies, REP + FSDP, 0, 0, axis_index_groups=rep_groups(1),...  12.5 us
    all_to_all x1, blocking collectives, body(): lax.all_to_all(windows, ('zl', 'core'), 0, 0, tiled=False)  11 us
    all_to_all x1, blocking collectives, body(): lax.all_to_all(copies, REP + FSDP, 0, 0, axis_index_groups=rep_groups(0),...  10.6 us
    ppermute x3, waiting for transfers between devices, body(): lax.ppermute(tiles[1 + kind], FSDP, near_pairs(kind))  4.33 us
    all_to_all x1, starting transfers between devices, body(): lax.all_to_all(partials.reshape(2, BLOCK // 2, BLOCKS), 'core', 0, 0, til...  3.72 us
  transfers between devices with their start and end apart: 4, of which 2 were waited for; matrix products, arithmetic and copies ran while one was open for 0% of the time, Pallas kernels for 2%

profile of v8, /device:TPU:6, one launch (start us, length us, event | category | flops | bytes accessed | tf_op | source)
XLA Modules:
  0.0 87.5 jit_solution(6449181338053411408)
XLA Ops:
  0.6 0.0 copy-start.5
  0.6 0.0 copy-start.1
  0.7 3.7 %all-to-all-start.8 = ((f32[2,32,4096]{2,1,0:T(8,128)}), f32[2,32,4096]{2,1,0:T(8,128)S(1)}, u32[]{:S(2)}, u32[]{:S(2)}) async-start(f32[2,32,4096]{2,1,0:T(8,128)} %bitcast.6), calls=%async_computation.8 | async-start | bytes 2097152 | tf_op jit(solution)/shard_map/all_to_all | solution.py:196
  4.4 0.0 copy-start
  4.4 0.1 pad_add_fusion.where_ref
  4.5 0.0 copy-done.5
  4.5 1.2 %plan.1 = (s32[2]{0:T(128)S(1)}, s32[1]{0:T(128)}, s32[8,128]{1,0:T(8,128)S(1)}) custom-call(s32[2]{0:T(128)S(1)} %pad_add_fusion.where_ref, s32[32]{0:T(128)S(1)} %copy-done.5), custom_call_target="tpu_custom_call" | custom-call | tf_op jit(solution)/shard_map/plan/pallas_call | solution.py:188
  5.7 0.8 all-to-all-done.8.parts_ref
  6.5 0.1 add_cores.1
  6.5 3.8 %collective-permute-start = (f32[8,4096]{1,0:T(8,128)S(1)}, f32[8,4096]{1,0:T(8,128)S(1)}, u32[]{:S(2)}, u32[]{:S(2)}) collective-permute-start(f32[8,4096]{1,0:T(8,128)S(1)} %get-tuple-element.174), channel_id=1, source_target_pairs={{0,2},{1,31},{2,0},{3,5},{4,6},{5,3},{6,4},{7,9},{8,10},{9,7},{10,... | collective-permute-start | bytes 393224 | tf_op jit(solution)/shard_map/ppermute | solution.py:224
  10.4 10.5 %collective-permute-start.1 = (f32[8,4096]{1,0:T(8,128)S(1)}, f32[8,4096]{1,0:T(8,128)S(1)}, u32[]{:S(2)}, u32[]{:S(2)}) collective-permute-start(f32[8,4096]{1,0:T(8,128)S(1)} %get-tuple-element.175), channel_id=1, source_target_pairs={{0,30},{1,3},{2,4},{3,1},{4,2},{5,7},{6,8},{7,5},{8,6},{9,11},{10,... | collective-permute-start | bytes 393224 | tf_op jit(solution)/shard_map/ppermute | solution.py:224
  20.9 1.9 %collective-permute-start.2 = (f32[8,4096]{1,0:T(8,128)S(1)}, f32[8,4096]{1,0:T(8,128)S(1)}, u32[]{:S(2)}, u32[]{:S(2)}) collective-permute-start(f32[8,4096]{1,0:T(8,128)S(1)} %get-tuple-element.176), channel_id=1, source_target_pairs={{0,4},{1,29},{2,6},{3,31},{4,0},{5,9},{6,2},{7,11},{8,12},{9,5},{1... | collective-permute-start | bytes 393224 | tf_op jit(solution)/shard_map/ppermute | solution.py:224
  23.5 0.0 copy-done.1
  23.5 0.0 copy-done
  23.5 0.0 copy-done.3
  23.5 0.8 prepare.1
  24.3 0.0 collective-permute-done
  24.3 0.0 collective-permute-done.1
  24.3 4.3 %collective-permute-done.2 = f32[8,4096]{1,0:T(8,128)S(1)} collective-permute-done((f32[8,4096]{1,0:T(8,128)S(1)}, f32[8,4096]{1,0:T(8,128)S(1)}, u32[]{:S(2)}, u32[]{:S(2)}) %collective-permute-start.2) | collective-permute-done | bytes 131104 | tf_op jit(solution)/shard_map/ppermute | solution.py:224
  28.6 23.4 %conditional.1 = (f32[8,8,512]{2,1,0:T(8,128)S(1)}) conditional(s32[]{:T(128)} %bitcast.3, (s32[8,128]{1,0:T(8,128)S(1)}, f32[64,512]{1,0:T(8,128)S(1)}, f32[8,4096]{1,0:T(8,128)S(1)}, f32[8,4096]{1,0:T(8,128)S(1)}, f32[8,4096]{1,0:T(8,128)S(1)}, /*index=5*/f32[8,4096]{1,0:T(8,128)S(1)}) %tuple.31, ...), branch_computations={%region_0.0_spmd, %region_1.0_spmd, %region_2.0_spmd, %region_3.0_... | conditional | bytes 1048584 | solution.py:225
  28.6 0.1 spread_1280.1
  28.8 22.9 %all_to_all.52.parts_ref = f32[4,8,1280]{2,1,0:T(8,128)S(1)} all-to-all(f32[4,8,1280]{2,1,0:T(8,128)S(1)} %spread_1280.1), channel_id=1, replica_groups=mesh['y'=4,'x'=4,'zh'=4,'zl'=4,'core'=2] {'zh'}, dimensions={0} | all-to-all | bytes 327680 | tf_op jit(solution)/shard_map/cond/branch_0_fun/all_to_all | solution.py:128
  51.7 0.3 windows_1280.1
  52.0 0.0 copy-start.4
  52.0 11.0 %all_to_all.60 = f32[8,8,512]{2,1,0:T(8,128)S(1)} all-to-all(f32[8,8,512]{2,1,0:T(8,128)S(1)} %get-tuple-element.181), channel_id=1, replica_groups=mesh['y'=4,'x'=4,'zh'=4,'zl'=4,'core'=2] {'zl','core'}, dimensions={0} | all-to-all | bytes 262144 | tf_op jit(solution)/shard_map/all_to_all | solution.py:226
  63.1 0.0 copy-done.4
  63.1 0.5 owner_step.1
  63.6 10.6 %all_to_all.61.parts_ref = f32[4,64,512]{2,1,0:T(8,128)S(1)} all-to-all(f32[4,64,512]{2,1,0:T(8,128)S(1)} %get-tuple-element.180), channel_id=1, replica_groups={{0,32,64,96},{128,160,192,224},{256,288,320,352},{384,416,448,480},{2,3..., dimensions={0} | all-to-all | bytes 1048576 | tf_op jit(solution)/shard_map/all_to_all | solution.py:236
  74.3 0.0 copy-start.2
  74.3 12.5 %all_to_all.62.parts_ref = f32[4,64,512]{2,1,0:T(8,128)S(1)} all-to-all(f32[4,64,512]{2,1,0:T(8,128)S(1)} %add_row.1), channel_id=1, replica_groups={{0,128,256,384},{32,160,288,416},{64,192,320,448},{96,224,352,480},{2,1..., dimensions={0} | all-to-all | bytes 1048576 | tf_op jit(solution)/shard_map/all_to_all | solution.py:245
  86.7 0.0 copy-done.2
  86.7 0.7 weights_step.1
  (2 shorter events, 0.0 us)
Async XLA Ops:
  0.6 3.8 %copy-start.5 = (s32[32]{0:T(128)S(1)}, s32[32]{0:T(128)}, u32[]{:S(2)}) copy-start(s32[32]{0:T(128)} %counts_ref.1) | copy-start | bytes 388
  0.6 22.8 %copy-start.1 = (f32[1,64,512]{2,1,0:T(8,128)S(1)}, f32[1,64,512]{2,1,0:T(8,128)}, u32[]{:S(2)}) copy-start(f32[1,64,512]{2,1,0:T(8,128)} %momentum_ref.1) | copy-start | bytes 393220
  0.7 5.8 %all-to-all-start.8 = ((f32[2,32,4096]{2,1,0:T(8,128)}), f32[2,32,4096]{2,1,0:T(8,128)S(1)}, u32[]{:S(2)}, u32[]{:S(2)}) async-start(f32[2,32,4096]{2,1,0:T(8,128)} %bitcast.6), calls=%async_computation.8 | async-start | bytes 2097152 | tf_op jit(solution)/shard_map/all_to_all | solution.py:196
  4.4 19.1 %copy-start = (s32[16,32,512]{2,1,0:T(8,128)S(1)}, s32[16,32,512]{2,1,0:T(8,128)}, u32[]{:S(2)}) copy-start(s32[16,32,512]{2,1,0:T(8,128)} %chosen_ref.1) | copy-start | bytes 3145732
  6.5 17.0 %copy-start.3 = (f32[64,64]{1,0:T(8,128)S(1)}, f32[64,64]{1,0:T(8,128)}, u32[]{:S(2)}) copy-start(f32[64,64]{1,0:T(8,128)} %constant.35.clone.table_ref) | copy-start | bytes 49156
  6.5 17.8 %collective-permute-start = (f32[8,4096]{1,0:T(8,128)S(1)}, f32[8,4096]{1,0:T(8,128)S(1)}, u32[]{:S(2)}, u32[]{:S(2)}) collective-permute-start(f32[8,4096]{1,0:T(8,128)S(1)} %get-tuple-element.174), channel_id=1, source_target_pairs={{0,2},{1,31},{2,0},{3,5},{4,6},{5,3},{6,4},{7,9},{8,10},{9,7},{10,... | collective-permute-start | bytes 393224 | tf_op jit(solution)/shard_map/ppermute | solution.py:224
  10.4 13.9 %collective-permute-start.1 = (f32[8,4096]{1,0:T(8,128)S(1)}, f32[8,4096]{1,0:T(8,128)S(1)}, u32[]{:S(2)}, u32[]{:S(2)}) collective-permute-start(f32[8,4096]{1,0:T(8,128)S(1)} %get-tuple-element.175), channel_id=1, source_target_pairs={{0,30},{1,3},{2,4},{3,1},{4,2},{5,7},{6,8},{7,5},{8,6},{9,11},{10,... | collective-permute-start | bytes 393224 | tf_op jit(solution)/shard_map/ppermute | solution.py:224
  20.9 7.8 %collective-permute-start.2 = (f32[8,4096]{1,0:T(8,128)S(1)}, f32[8,4096]{1,0:T(8,128)S(1)}, u32[]{:S(2)}, u32[]{:S(2)}) collective-permute-start(f32[8,4096]{1,0:T(8,128)S(1)} %get-tuple-element.176), channel_id=1, source_target_pairs={{0,4},{1,29},{2,6},{3,31},{4,0},{5,9},{6,2},{7,11},{8,12},{9,5},{1... | collective-permute-start | bytes 393224 | tf_op jit(solution)/shard_map/ppermute | solution.py:224
  52.0 11.0 %copy-start.4 = (f32[64,64]{1,0:T(8,128)S(1)}, f32[64,64]{1,0:T(8,128)}, u32[]{:S(2)}) copy-start(f32[64,64]{1,0:T(8,128)} %constant.36.clone.back_ref) | copy-start | bytes 49156
  74.3 12.5 %copy-start.2 = (f32[64,512]{1,0:T(8,128)S(1)}, f32[64,512]{1,0:T(8,128)}, u32[]{:S(2)}) copy-start(f32[64,512]{1,0:T(8,128)} %weights_ref.1) | copy-start | bytes 393220

commit v9 on v8

--- a/solution.py
+++ b/solution.py
@@ -17,7 +17,7 @@
 NEAR = 8
 CHIPS = NEAR // 2
 SIDE = 4
-WIDTHS = (1280, 1408, 1536, 1664, 1792, 2048, 2560, 4096)
+WIDTHS = (1280, 1408, 1536, 1664, 1792, 1920, 2048, 2304, 2560, 4096)
 FAR = OWNERS // NEAR
 ROWS = BLOCK // NEAR
 
@@ -58,13 +58,22 @@
     return groups
 
 
-def add_cores_kernel(plan_ref, parts_ref, *tile_refs):
+def other_half_kernel(partials_ref, out_ref, done):
+    rows = pl.ds(pl.multiple_of((1 - lax.axis_index("core")) * (BLOCK // 2), BLOCK // 2), BLOCK // 2)
+    copy = pltpu.make_async_copy(partials_ref.at[rows, :], out_ref, done)
+    copy.start()
+    copy.wait()
+
+
+def add_cores_kernel(plan_ref, partials_ref, received_ref, *tile_refs):
     del plan_ref
     place = lax.axis_index("zl")
-    up = 1 + 2 * ((place + lax.axis_index("core")) % 2)
+    core = lax.axis_index("core")
+    up = 1 + 2 * ((place + core) % 2)
     for hop, tile_ref in zip((0, up, 4 - up, 2), tile_refs):
-        rows = pl.ds(pl.multiple_of((place + hop) % CHIPS * ROWS, ROWS), ROWS)
-        tile_ref[...] = parts_ref[0, rows, :] + parts_ref[1, rows, :]
+        row = (place + hop) % CHIPS * ROWS
+        here = pl.ds(pl.multiple_of(core * (BLOCK // 2) + row, ROWS), ROWS)
+        tile_ref[...] = partials_ref[here, :] + received_ref[pl.ds(pl.multiple_of(row, ROWS), ROWS), :]
 
 
 def plan_kernel(where_ref, counts_ref, plan_ref, branch_ref, offsets_ref):
@@ -193,15 +202,25 @@
         compiler_params=pltpu.CompilerParams(vmem_limit_bytes=1 << 20),
         name="plan",
     )(jnp.stack([group, owner]).astype(jnp.int32), owner_blocks)
-    halves = lax.all_to_all(partials.reshape(2, BLOCK // 2, BLOCKS), "core", 0, 0, tiled=False)
+    partials = partials.reshape(BLOCK, BLOCKS)
+    leaving = pl.pallas_call(
+        other_half_kernel,
+        out_shape=jax.ShapeDtypeStruct((BLOCK // 2, BLOCKS), jnp.float32),
+        in_specs=[pl.BlockSpec(memory_space=pl.ANY)],
+        out_specs=whole,
+        scratch_shapes=[pltpu.SemaphoreType.DMA],
+        compiler_params=small,
+        name="other_half",
+    )(partials)
+    received = lax.ppermute(leaving, "core", [(0, 1), (1, 0)])
     tiles = pl.pallas_call(
         add_cores_kernel,
         out_shape=[jax.ShapeDtypeStruct((ROWS, BLOCKS), jnp.float32)] * CHIPS,
-        in_specs=[pl.BlockSpec(memory_space=pl.ANY), whole],
+        in_specs=[pl.BlockSpec(memory_space=pl.ANY), whole, whole],
         out_specs=[whole] * CHIPS,
         compiler_params=pltpu.CompilerParams(vmem_limit_bytes=8 << 20),
         name="add_cores",
-    )(place, halves)
+    )(place, partials, received)
     table, back = jnp.asarray(dct_matrix()), jnp.asarray(dct_matrix().T)
     square = jax.ShapeDtypeStruct((BLOCK, MOST), jnp.float32)
     decayed, listed, sparse, live = pl.pallas_call(

time: 88.7 us -> 89.8 us (1.012)
  blocking collectives: 57 us -> 58.7 us
  starting transfers between devices: 20 us -> 18.4 us
  local copies, waits for them, and re-layouts: 0.03 us -> 1.25 us
    all_to_all x1 -> x0, starting transfers between devices: 3.72 us -> none  [body(): lax.all_to_all(partials.reshape(2, BLOCK // 2, BLOCKS), 'core', 0, 0, til...]
    ppermute x0 -> x1, starting transfers between devices: none -> 2.05 us  [body(): received = lax.ppermute(leaving, 'core', [(0, 1), (1, 0)])]
    all_to_all x1, blocking collectives: 22.9 us -> 24.5 us  [deliver(): met = lax.all_to_all(spread, 'zh', 0, 0, tiled=False)]
    unnamed x12 -> x16, local copies, waits for them, and re-layouts: 0.03 us -> 1.25 us
where the time goes in v9:
time: 89.8 us; the launch traced here: 88.7 us
  blocking collectives  58.7 us (65%)
  starting transfers between devices  18.4 us (20%)
  waiting for transfers between devices  4.91 us (5%)
  Pallas kernels  3.81 us (4%)
  between operations  1.45 us (2%)
  local copies, waits for them, and re-layouts  1.25 us (1%)
    all_to_all x1, blocking collectives, deliver(): met = lax.all_to_all(spread, 'zh', 0, 0, tiled=False)  24.5 us
    ppermute x3, starting transfers between devices, body(): lax.ppermute(tiles[1 + kind], FSDP, near_pairs(kind))  16.4 us
    all_to_all x1, blocking collectives, body(): lax.all_to_all(copies, REP + FSDP, 0, 0, axis_index_groups=rep_groups(1),...  12.5 us
    all_to_all x1, blocking collectives, body(): lax.all_to_all(windows, ('zl', 'core'), 0, 0, tiled=False)  11.2 us
    all_to_all x1, blocking collectives, body(): lax.all_to_all(copies, REP + FSDP, 0, 0, axis_index_groups=rep_groups(0),...  10.6 us
    ppermute x3, waiting for transfers between devices, body(): lax.ppermute(tiles[1 + kind], FSDP, near_pairs(kind))  4.33 us
    ppermute x1, starting transfers between devices, body(): received = lax.ppermute(leaving, 'core', [(0, 1), (1, 0)])  2.05 us
  transfers between devices with their start and end apart: 4, of which 2 were waited for; matrix products, arithmetic and copies ran while one was open for 0% of the time, Pallas kernels for 2%

profile of v9, /device:TPU:6, one launch (start us, length us, event | category | flops | bytes accessed | tf_op | source)
XLA Modules:
  0.0 88.7 jit_solution(3407815931272485857)
XLA Ops:
  0.6 0.0 copy-start
  0.6 1.2 %copy-done = f32[1,1,64,4096]{3,2,1,0:T(8,128)S(1)} copy-done((f32[1,1,64,4096]{3,2,1,0:T(8,128)S(1)}, f32[1,1,64,4096]{3,2,1,0:T(8,128)}, u32[]{:S(2)}) %copy-start) | copy-done | bytes 1048600
  1.9 0.0 copy-start.2
  1.9 2.1 %collective-permute-start = (f32[32,4096]{1,0:T(8,128)S(1)}, f32[32,4096]{1,0:T(8,128)S(1)}, u32[]{:S(2)}, u32[]{:S(2)}) collective-permute-start(f32[32,4096]{1,0:T(8,128)S(1)} %other_half.1), channel_id=1, source_target_pairs={{0,1},{1,0},{2,3},{3,2},{4,5},{5,4},{6,7},{7,6},{8,9},{9,8},{10,11... | collective-permute-start | bytes 1572872 | tf_op jit(solution)/shard_map/ppermute | solution.py:215
  4.0 0.1 pad_add_fusion.where_ref
  4.1 0.0 copy-done.7
  4.1 1.2 %plan.1 = (s32[2]{0:T(128)S(1)}, s32[1]{0:T(128)}, s32[8,128]{1,0:T(8,128)S(1)}) custom-call(s32[2]{0:T(128)S(1)} %pad_add_fusion.where_ref, s32[32]{0:T(128)S(1)} %copy-done.7), custom_call_target="tpu_custom_call" | custom-call | tf_op jit(solution)/shard_map/plan/pallas_call | solution.py:197
  5.3 0.6 collective-permute-done.received_ref
  5.9 0.0 copy-done.1
  5.9 0.1 add_cores.1
  5.9 4.0 %collective-permute-start.1 = (f32[8,4096]{1,0:T(8,128)S(1)}, f32[8,4096]{1,0:T(8,128)S(1)}, u32[]{:S(2)}, u32[]{:S(2)}) collective-permute-start(f32[8,4096]{1,0:T(8,128)S(1)} %get-tuple-element.212), channel_id=1, source_target_pairs={{0,2},{1,31},{2,0},{3,5},{4,6},{5,3},{6,4},{7,9},{8,10},{9,7},{10,... | collective-permute-start | bytes 393224 | tf_op jit(solution)/shard_map/ppermute | solution.py:243
  9.9 10.5 %collective-permute-start.2 = (f32[8,4096]{1,0:T(8,128)S(1)}, f32[8,4096]{1,0:T(8,128)S(1)}, u32[]{:S(2)}, u32[]{:S(2)}) collective-permute-start(f32[8,4096]{1,0:T(8,128)S(1)} %get-tuple-element.213), channel_id=1, source_target_pairs={{0,30},{1,3},{2,4},{3,1},{4,2},{5,7},{6,8},{7,5},{8,6},{9,11},{10,... | collective-permute-start | bytes 393224 | tf_op jit(solution)/shard_map/ppermute | solution.py:243
  20.4 1.9 %collective-permute-start.3 = (f32[8,4096]{1,0:T(8,128)S(1)}, f32[8,4096]{1,0:T(8,128)S(1)}, u32[]{:S(2)}, u32[]{:S(2)}) collective-permute-start(f32[8,4096]{1,0:T(8,128)S(1)} %get-tuple-element.214), channel_id=1, source_target_pairs={{0,4},{1,29},{2,6},{3,31},{4,0},{5,9},{6,2},{7,11},{8,12},{9,5},{1... | collective-permute-start | bytes 393224 | tf_op jit(solution)/shard_map/ppermute | solution.py:243
  23.0 0.0 copy-done.2
  23.0 0.0 copy-done.3
  23.0 0.0 copy-done.5
  23.0 0.8 prepare.1
  23.8 0.0 collective-permute-done.1
  23.8 0.0 collective-permute-done.2
  23.8 4.3 %collective-permute-done.3 = f32[8,4096]{1,0:T(8,128)S(1)} collective-permute-done((f32[8,4096]{1,0:T(8,128)S(1)}, f32[8,4096]{1,0:T(8,128)S(1)}, u32[]{:S(2)}, u32[]{:S(2)}) %collective-permute-start.3) | collective-permute-done | bytes 131104 | tf_op jit(solution)/shard_map/ppermute | solution.py:243
  28.2 24.9 %conditional.1 = (f32[8,8,512]{2,1,0:T(8,128)S(1)}) conditional(s32[]{:T(128)} %bitcast.3, (s32[8,128]{1,0:T(8,128)S(1)}, f32[64,512]{1,0:T(8,128)S(1)}, f32[8,4096]{1,0:T(8,128)S(1)}, f32[8,4096]{1,0:T(8,128)S(1)}, f32[8,4096]{1,0:T(8,128)S(1)}, /*index=5*/f32[8,4096]{1,0:T(8,128)S(1)}) %tuple.37, ...), branch_computations={%region_0.0_spmd, %region_1.0_spmd, %region_2.0_spmd, %region_3.0_... | conditional | bytes 1048584 | solution.py:244
  28.2 0.1 spread_1664.1
  28.3 24.5 %all_to_all.58.parts_ref = f32[4,8,1664]{2,1,0:T(8,128)S(1)} all-to-all(f32[4,8,1664]{2,1,0:T(8,128)S(1)} %spread_1664.1), channel_id=1, replica_groups=mesh['y'=4,'x'=4,'zh'=4,'zl'=4,'core'=2] {'zh'}, dimensions={0} | all-to-all | bytes 425984 | tf_op jit(solution)/shard_map/cond/branch_3_fun/all_to_all | solution.py:137
  52.8 0.3 windows_1664.1
  53.1 0.0 copy-start.6
  53.1 11.2 %all_to_all.65 = f32[8,8,512]{2,1,0:T(8,128)S(1)} all-to-all(f32[8,8,512]{2,1,0:T(8,128)S(1)} %get-tuple-element.219), channel_id=1, replica_groups=mesh['y'=4,'x'=4,'zh'=4,'zl'=4,'core'=2] {'zl','core'}, dimensions={0} | all-to-all | bytes 262144 | tf_op jit(solution)/shard_map/all_to_all | solution.py:245
  64.3 0.0 copy-done.6
  64.3 0.5 owner_step.1
  64.8 10.6 %all_to_all.66.parts_ref = f32[4,64,512]{2,1,0:T(8,128)S(1)} all-to-all(f32[4,64,512]{2,1,0:T(8,128)S(1)} %get-tuple-element.218), channel_id=1, replica_groups={{0,32,64,96},{128,160,192,224},{256,288,320,352},{384,416,448,480},{2,3..., dimensions={0} | all-to-all | bytes 1048576 | tf_op jit(solution)/shard_map/all_to_all | solution.py:255
  75.5 0.0 copy-start.4
  75.5 12.5 %all_to_all.67.parts_ref = f32[4,64,512]{2,1,0:T(8,128)S(1)} all-to-all(f32[4,64,512]{2,1,0:T(8,128)S(1)} %add_row.1), channel_id=1, replica_groups={{0,128,256,384},{32,160,288,416},{64,192,320,448},{96,224,352,480},{2,1..., dimensions={0} | all-to-all | bytes 1048576 | tf_op jit(solution)/shard_map/all_to_all | solution.py:264
  88.0 0.7 weights_step.1
  (7 shorter events, 0.1 us)
Async XLA Ops:
  0.6 1.2 %copy-start = (f32[1,1,64,4096]{3,2,1,0:T(8,128)S(1)}, f32[1,1,64,4096]{3,2,1,0:T(8,128)}, u32[]{:S(2)}) copy-start(f32[1,1,64,4096]{3,2,1,0:T(8,128)} %param.17) | copy-start | bytes 3145732
  1.9 2.2 %copy-start.7 = (s32[32]{0:T(128)S(1)}, s32[32]{0:T(128)}, u32[]{:S(2)}) copy-start(s32[32]{0:T(128)} %counts_ref.1) | copy-start | bytes 388
  1.9 4.0 %copy-start.1 = (f32[1,1,64,4096]{3,2,1,0:T(8,128)S(1)}, f32[1,1,64,4096]{3,2,1,0:T(8,128)}, u32[]{:S(2)}) copy-start(f32[1,1,64,4096]{3,2,1,0:T(8,128)} %param.17) | copy-start | bytes 3145732
  1.9 21.1 %copy-start.2 = (s32[16,32,512]{2,1,0:T(8,128)S(1)}, s32[16,32,512]{2,1,0:T(8,128)}, u32[]{:S(2)}) copy-start(s32[16,32,512]{2,1,0:T(8,128)} %chosen_ref.1) | copy-start | bytes 3145732
  1.9 3.9 %collective-permute-start = (f32[32,4096]{1,0:T(8,128)S(1)}, f32[32,4096]{1,0:T(8,128)S(1)}, u32[]{:S(2)}, u32[]{:S(2)}) collective-permute-start(f32[32,4096]{1,0:T(8,128)S(1)} %other_half.1), channel_id=1, source_target_pairs={{0,1},{1,0},{2,3},{3,2},{4,5},{5,4},{6,7},{7,6},{8,9},{9,8},{10,11... | collective-permute-start | bytes 1572872 | tf_op jit(solution)/shard_map/ppermute | solution.py:215
  5.9 17.1 %copy-start.3 = (f32[1,64,512]{2,1,0:T(8,128)S(1)}, f32[1,64,512]{2,1,0:T(8,128)}, u32[]{:S(2)}) copy-start(f32[1,64,512]{2,1,0:T(8,128)} %momentum_ref.1) | copy-start | bytes 393220
  5.9 17.1 %copy-start.5 = (f32[64,64]{1,0:T(8,128)S(1)}, f32[64,64]{1,0:T(8,128)}, u32[]{:S(2)}) copy-start(f32[64,64]{1,0:T(8,128)} %constant.35.clone.table_ref) | copy-start | bytes 49156
  5.9 17.9 %collective-permute-start.1 = (f32[8,4096]{1,0:T(8,128)S(1)}, f32[8,4096]{1,0:T(8,128)S(1)}, u32[]{:S(2)}, u32[]{:S(2)}) collective-permute-start(f32[8,4096]{1,0:T(8,128)S(1)} %get-tuple-element.212), channel_id=1, source_target_pairs={{0,2},{1,31},{2,0},{3,5},{4,6},{5,3},{6,4},{7,9},{8,10},{9,7},{10,... | collective-permute-start | bytes 393224 | tf_op jit(solution)/shard_map/ppermute | solution.py:243
  9.9 13.9 %collective-permute-start.2 = (f32[8,4096]{1,0:T(8,128)S(1)}, f32[8,4096]{1,0:T(8,128)S(1)}, u32[]{:S(2)}, u32[]{:S(2)}) collective-permute-start(f32[8,4096]{1,0:T(8,128)S(1)} %get-tuple-element.213), channel_id=1, source_target_pairs={{0,30},{1,3},{2,4},{3,1},{4,2},{5,7},{6,8},{7,5},{8,6},{9,11},{10,... | collective-permute-start | bytes 393224 | tf_op jit(solution)/shard_map/ppermute | solution.py:243
  20.4 7.8 %collective-permute-start.3 = (f32[8,4096]{1,0:T(8,128)S(1)}, f32[8,4096]{1,0:T(8,128)S(1)}, u32[]{:S(2)}, u32[]{:S(2)}) collective-permute-start(f32[8,4096]{1,0:T(8,128)S(1)} %get-tuple-element.214), channel_id=1, source_target_pairs={{0,4},{1,29},{2,6},{3,31},{4,0},{5,9},{6,2},{7,11},{8,12},{9,5},{1... | collective-permute-start | bytes 393224 | tf_op jit(solution)/shard_map/ppermute | solution.py:243
  53.1 11.2 %copy-start.6 = (f32[64,64]{1,0:T(8,128)S(1)}, f32[64,64]{1,0:T(8,128)}, u32[]{:S(2)}) copy-start(f32[64,64]{1,0:T(8,128)} %constant.36.clone.back_ref) | copy-start | bytes 49156
  75.5 12.5 %copy-start.4 = (f32[64,512]{1,0:T(8,128)S(1)}, f32[64,512]{1,0:T(8,128)}, u32[]{:S(2)}) copy-start(f32[64,512]{1,0:T(8,128)} %weights_ref.1) | copy-start | bytes 393220

commit v10 on v9

--- a/solution.py
+++ b/solution.py
@@ -48,6 +48,21 @@
     return pairs
 
 
+def far_hop(group, core, kind):
+    if kind == 0:
+        return (group + 2) % FAR
+    turned = (core + kind + 1) % 2
+    return (((group + FAR - turned) % FAR ^ 1) + turned) % FAR
+
+
+def far_pairs(kind):
+    pairs = []
+    for group in range(FAR):
+        for f in range(NEAR):
+            pairs.append((group * NEAR + f, far_hop(group, f % 2, kind) * NEAR + f))
+    return pairs
+
+
 def rep_groups(turn):
     groups = []
     for core in range(2):
@@ -80,6 +95,7 @@
     plan_ref[0] = where_ref[0]
     plan_ref[1] = counts_ref[where_ref[1]]
     far = where_ref[1] // NEAR
+    hops = [far] + [far_hop(far, where_ref[1] % 2, kind) for kind in range(FAR - 1)]
     lane = lax.broadcasted_iota(jnp.int32, (8, 128), 1)
     offsets = jnp.zeros((8, 128), jnp.int32)
     start = jnp.int32(0)
@@ -88,7 +104,8 @@
     for i in range(OWNERS):
         if i % NEAR == 0:
             first = start - start % 128
-            offsets = jnp.where(lane == i // NEAR, first, offsets)
+            for k, hop in enumerate(hops):
+                offsets = jnp.where((lane == k) & (hop == i // NEAR), first, offsets)
         here = (lane == FAR + i % NEAR) & (far == i // NEAR)
         offsets = jnp.where(here, start - first, offsets)
         start = start + counts_ref[i]
@@ -97,17 +114,18 @@
     offsets_ref[...] = offsets
 
 
-def spread_kernel(width, offsets_ref, after_ref, own_ref, next_ref, other_ref, across_ref, out_ref, total_ref):
+def spread_kernel(width, offsets_ref, after_ref, own_ref, next_ref, other_ref, across_ref, *refs):
     del after_ref
+    *out_refs, total_ref = refs
     total_ref[:, :BLOCKS] = (own_ref[...] + next_ref[...]) + (other_ref[...] + across_ref[...])
     total_ref[:, BLOCKS:] = jnp.zeros((ROWS, width), jnp.float32)
-    for a in range(FAR):
-        base = pl.multiple_of(offsets_ref[0, a], 128)
-        out_ref[a] = total_ref[:, pl.ds(base, width)]
-
-
-def window_kernel(width, offsets_ref, parts_ref, out_ref, total_ref):
-    total_ref[:, :width] = jnp.sum(parts_ref[...], axis=0)
+    for k, out_ref in enumerate(out_refs):
+        base = pl.multiple_of(offsets_ref[0, k], 128)
+        out_ref[...] = total_ref[:, pl.ds(base, width)]
+
+
+def window_kernel(width, offsets_ref, own_ref, across_ref, next_ref, other_ref, out_ref, total_ref):
+    total_ref[:, :width] = (own_ref[...] + across_ref[...]) + (next_ref[...] + other_ref[...])
     total_ref[:, width:] = jnp.zeros((ROWS, MOST + 128), jnp.float32)
     lane = lax.broadcasted_iota(jnp.int32, (ROWS, 128), 1)
     for i in range(NEAR):
@@ -127,23 +145,23 @@
     small = pltpu.CompilerParams(vmem_limit_bytes=8 << 20)
     spread = pl.pallas_call(
         functools.partial(spread_kernel, width),
-        out_shape=jax.ShapeDtypeStruct((FAR, ROWS, width), jnp.float32),
+        out_shape=[jax.ShapeDtypeStruct((ROWS, width), jnp.float32)] * FAR,
         in_specs=[whole, pl.BlockSpec(memory_space=pl.ANY)] + [whole] * CHIPS,
-        out_specs=whole,
+        out_specs=[whole] * FAR,
         scratch_shapes=[pltpu.VMEM((ROWS, BLOCKS + width), jnp.float32)],
         compiler_params=small,
         name=f"spread_{width}",
     )(offsets, after, *near)
-    met = lax.all_to_all(spread, "zh", 0, 0, tiled=False)
+    met = [spread[0]] + [lax.ppermute(spread[1 + kind], FSDP, far_pairs(kind)) for kind in range(FAR - 1)]
     return pl.pallas_call(
         functools.partial(window_kernel, width),
         out_shape=jax.ShapeDtypeStruct((NEAR, ROWS, MOST), jnp.float32),
-        in_specs=[whole, whole],
+        in_specs=[whole] * (1 + FAR),
         out_specs=whole,
         scratch_shapes=[pltpu.VMEM((ROWS, width + MOST + 128), jnp.float32)],
         compiler_params=small,
         name=f"windows_{width}",
-    )(offsets, met)
+    )(offsets, *met)
 
 
 def prepare_kernel(place_ref, after_ref, momentum_ref, chosen_ref, table_ref, decayed_ref, listed_ref, sparse_ref, live_ref):

time: 89.8 us -> 87.5 us (0.974)
  blocking collectives: 58.7 us -> 32.2 us
  starting transfers between devices: 18.4 us -> 35.5 us
  waiting for transfers between devices: 4.91 us -> 11.9 us
    all_to_all x1 -> x0, blocking collectives: 24.5 us -> none  [deliver(): met = lax.all_to_all(spread, 'zh', 0, 0, tiled=False)]
    ppermute x0 -> x3, starting transfers between devices: none -> 17 us  [deliver(): lax.ppermute(spread[1 + kind], FSDP, far_pairs(kind))]
    ppermute x0 -> x3, waiting for transfers between devices: none -> 6.99 us  [deliver(): lax.ppermute(spread[1 + kind], FSDP, far_pairs(kind))]
    all_to_all x1, blocking collectives: 11.2 us -> 9.17 us  [body(): lax.all_to_all(windows, ('zl', 'core'), 0, 0, tiled=False)]
  transfers between devices with their start and end apart: 4 -> 7, of which waited for: 2 -> 3; matrix products, arithmetic and copies ran while one was open for 0% -> 0% of each run, Pallas kernels for 2% -> 2%
where the time goes in v10:
time: 87.5 us; the launch traced here: 86.2 us
  starting transfers between devices  35.5 us (41%)
  blocking collectives  32.2 us (37%)
  waiting for transfers between devices  11.9 us (14%)
  Pallas kernels  3.84 us (4%)
  between operations  1.45 us (2%)
  local copies, waits for them, and re-layouts  1.25 us (1%)
    ppermute x3, starting transfers between devices, deliver(): lax.ppermute(spread[1 + kind], FSDP, far_pairs(kind))  17 us
    ppermute x3, starting transfers between devices, body(): lax.ppermute(tiles[1 + kind], FSDP, near_pairs(kind))  16.4 us
    all_to_all x1, blocking collectives, body(): lax.all_to_all(copies, REP + FSDP, 0, 0, axis_index_groups=rep_groups(1),...  12.5 us
    all_to_all x1, blocking collectives, body(): lax.all_to_all(copies, REP + FSDP, 0, 0, axis_index_groups=rep_groups(0),...  10.6 us
    all_to_all x1, blocking collectives, body(): lax.all_to_all(windows, ('zl', 'core'), 0, 0, tiled=False)  9.17 us
    ppermute x3, waiting for transfers between devices, deliver(): lax.ppermute(spread[1 + kind], FSDP, far_pairs(kind))  6.99 us
    ppermute x3, waiting for transfers between devices, body(): lax.ppermute(tiles[1 + kind], FSDP, near_pairs(kind))  4.33 us
    ppermute x1, starting transfers between devices, body(): received = lax.ppermute(leaving, 'core', [(0, 1), (1, 0)])  2.05 us
  transfers between devices with their start and end apart: 7, of which 3 were waited for; matrix products, arithmetic and copies ran while one was open for 0% of the time, Pallas kernels for 2%

profile of v10, /device:TPU:6, one launch (start us, length us, event | category | flops | bytes accessed | tf_op | source)
XLA Modules:
  0.0 86.2 jit_solution(10145774239001150977)
XLA Ops:
  0.6 0.0 copy-start
  0.6 1.2 %copy-done = f32[1,1,64,4096]{3,2,1,0:T(8,128)S(1)} copy-done((f32[1,1,64,4096]{3,2,1,0:T(8,128)S(1)}, f32[1,1,64,4096]{3,2,1,0:T(8,128)}, u32[]{:S(2)}) %copy-start) | copy-done | bytes 1048600
  1.9 0.0 copy-start.2
  1.9 2.1 %collective-permute-start.30 = (f32[32,4096]{1,0:T(8,128)S(1)}, f32[32,4096]{1,0:T(8,128)S(1)}, u32[]{:S(2)}, u32[]{:S(2)}) collective-permute-start(f32[32,4096]{1,0:T(8,128)S(1)} %other_half.1), channel_id=1, source_target_pairs={{0,1},{1,0},{2,3},{3,2},{4,5},{5,4},{6,7},{7,6},{8,9},{9,8},{10,11... | collective-permute-start | bytes 1572872 | tf_op jit(solution)/shard_map/ppermute | solution.py:233
  4.0 0.1 pad_add_fusion.where_ref
  4.1 1.2 %plan.1 = (s32[2]{0:T(128)S(1)}, s32[1]{0:T(128)}, s32[8,128]{1,0:T(8,128)S(1)}) custom-call(s32[2]{0:T(128)S(1)} %pad_add_fusion.where_ref, s32[32]{0:T(128)S(1)} %copy-done.7), custom_call_target="tpu_custom_call" | custom-call | tf_op jit(solution)/shard_map/plan/pallas_call | solution.py:215
  5.3 0.6 collective-permute-done.30.received_ref
  5.9 0.0 copy-done.1
  5.9 0.1 add_cores.1
  5.9 4.0 %collective-permute-start.31 = (f32[8,4096]{1,0:T(8,128)S(1)}, f32[8,4096]{1,0:T(8,128)S(1)}, u32[]{:S(2)}, u32[]{:S(2)}) collective-permute-start(f32[8,4096]{1,0:T(8,128)S(1)} %get-tuple-element.252), channel_id=1, source_target_pairs={{0,2},{1,31},{2,0},{3,5},{4,6},{5,3},{6,4},{7,9},{8,10},{9,7},{10,... | collective-permute-start | bytes 393224 | tf_op jit(solution)/shard_map/ppermute | solution.py:261
  9.9 10.5 %collective-permute-start.32 = (f32[8,4096]{1,0:T(8,128)S(1)}, f32[8,4096]{1,0:T(8,128)S(1)}, u32[]{:S(2)}, u32[]{:S(2)}) collective-permute-start(f32[8,4096]{1,0:T(8,128)S(1)} %get-tuple-element.253), channel_id=1, source_target_pairs={{0,30},{1,3},{2,4},{3,1},{4,2},{5,7},{6,8},{7,5},{8,6},{9,11},{10,... | collective-permute-start | bytes 393224 | tf_op jit(solution)/shard_map/ppermute | solution.py:261
  20.4 1.9 %collective-permute-start.33 = (f32[8,4096]{1,0:T(8,128)S(1)}, f32[8,4096]{1,0:T(8,128)S(1)}, u32[]{:S(2)}, u32[]{:S(2)}) collective-permute-start(f32[8,4096]{1,0:T(8,128)S(1)} %get-tuple-element.254), channel_id=1, source_target_pairs={{0,4},{1,29},{2,6},{3,31},{4,0},{5,9},{6,2},{7,11},{8,12},{9,5},{1... | collective-permute-start | bytes 393224 | tf_op jit(solution)/shard_map/ppermute | solution.py:261
  23.0 0.8 prepare.1
  23.8 0.0 collective-permute-done.31
  23.8 0.0 collective-permute-done.32
  23.8 4.3 %collective-permute-done.33 = f32[8,4096]{1,0:T(8,128)S(1)} collective-permute-done((f32[8,4096]{1,0:T(8,128)S(1)}, f32[8,4096]{1,0:T(8,128)S(1)}, u32[]{:S(2)}, u32[]{:S(2)}) %collective-permute-start.33) | collective-permute-done | bytes 131104 | tf_op jit(solution)/shard_map/ppermute | solution.py:261
  28.2 24.5 %conditional.1 = (f32[8,8,512]{2,1,0:T(8,128)S(1)}) conditional(s32[]{:T(128)} %bitcast.3, (s32[8,128]{1,0:T(8,128)S(1)}, f32[64,512]{1,0:T(8,128)S(1)}, f32[8,4096]{1,0:T(8,128)S(1)}, f32[8,4096]{1,0:T(8,128)S(1)}, f32[8,4096]{1,0:T(8,128)S(1)}, /*index=5*/f32[8,4096]{1,0:T(8,128)S(1)}) %tuple.37, ...), branch_computations={%region_0.0_spmd, %region_1.0_spmd, %region_2.0_spmd, %region_3.0_... | conditional | bytes 1572992 | solution.py:262
  28.2 0.1 spread_1408.1
  28.3 6.4 %collective-permute-start.3 = (f32[8,1408]{1,0:T(8,128)S(1)}, f32[8,1408]{1,0:T(8,128)S(1)}, u32[]{:S(2)}, u32[]{:S(2)}) collective-permute-start(f32[8,1408]{1,0:T(8,128)S(1)} %get-tuple-element.148), channel_id=1, source_target_pairs={{0,16},{1,17},{2,18},{3,19},{4,20},{5,21},{6,22},{7,23},{8,24},{9,... | collective-permute-start | bytes 135176 | tf_op jit(solution)/shard_map/cond/branch_1_fun/ppermute | solution.py:155
  34.6 7.7 %collective-permute-start.4 = (f32[8,1408]{1,0:T(8,128)S(1)}, f32[8,1408]{1,0:T(8,128)S(1)}, u32[]{:S(2)}, u32[]{:S(2)}) collective-permute-start(f32[8,1408]{1,0:T(8,128)S(1)} %get-tuple-element.149), channel_id=1, source_target_pairs={{0,8},{1,25},{2,10},{3,27},{4,12},{5,29},{6,14},{7,31},{8,0},{9,17... | collective-permute-start | bytes 135176 | tf_op jit(solution)/shard_map/cond/branch_1_fun/ppermute | solution.py:155
  42.4 3.0 %collective-permute-start.5 = (f32[8,1408]{1,0:T(8,128)S(1)}, f32[8,1408]{1,0:T(8,128)S(1)}, u32[]{:S(2)}, u32[]{:S(2)}) collective-permute-start(f32[8,1408]{1,0:T(8,128)S(1)} %get-tuple-element.150), channel_id=1, source_target_pairs={{0,24},{1,9},{2,26},{3,11},{4,28},{5,13},{6,30},{7,15},{8,16},{9,1... | collective-permute-start | bytes 135176 | tf_op jit(solution)/shard_map/cond/branch_1_fun/ppermute | solution.py:155
  45.3 0.0 collective-permute-done.3.across_ref
  45.3 0.0 collective-permute-done.4.next_ref
  45.3 7.0 %collective-permute-done.5.other_ref = f32[8,1408]{1,0:T(8,128)S(1)} collective-permute-done((f32[8,1408]{1,0:T(8,128)S(1)}, f32[8,1408]{1,0:T(8,128)S(1)}, u32[]{:S(2)}, u32[]{:S(2)}) %collective-permute-start.5) | collective-permute-done | bytes 45088 | tf_op jit(solution)/shard_map/cond/branch_1_fun/ppermute | solution.py:155
  52.3 0.3 windows_1408.1
  52.6 0.0 copy-start.6
  52.6 9.2 %all_to_all.15 = f32[8,8,512]{2,1,0:T(8,128)S(1)} all-to-all(f32[8,8,512]{2,1,0:T(8,128)S(1)} %get-tuple-element.259), channel_id=1, replica_groups=mesh['y'=4,'x'=4,'zh'=4,'zl'=4,'core'=2] {'zl','core'}, dimensions={0} | all-to-all | bytes 262144 | tf_op jit(solution)/shard_map/all_to_all | solution.py:263
  61.8 0.6 owner_step.1
  62.4 10.6 %all_to_all.16.parts_ref = f32[4,64,512]{2,1,0:T(8,128)S(1)} all-to-all(f32[4,64,512]{2,1,0:T(8,128)S(1)} %get-tuple-element.258), channel_id=1, replica_groups={{0,32,64,96},{128,160,192,224},{256,288,320,352},{384,416,448,480},{2,3..., dimensions={0} | all-to-all | bytes 1048576 | tf_op jit(solution)/shard_map/all_to_all | solution.py:273
  73.0 0.0 copy-start.4
  73.0 12.5 %all_to_all.17.parts_ref = f32[4,64,512]{2,1,0:T(8,128)S(1)} all-to-all(f32[4,64,512]{2,1,0:T(8,128)S(1)} %add_row.1), channel_id=1, replica_groups={{0,128,256,384},{32,160,288,416},{64,192,320,448},{96,224,352,480},{2,1..., dimensions={0} | all-to-all | bytes 1048576 | tf_op jit(solution)/shard_map/all_to_all | solution.py:282
  85.5 0.7 weights_step.1
  (12 shorter events, 0.1 us)
Async XLA Ops:
  0.6 1.2 %copy-start = (f32[1,1,64,4096]{3,2,1,0:T(8,128)S(1)}, f32[1,1,64,4096]{3,2,1,0:T(8,128)}, u32[]{:S(2)}) copy-start(f32[1,1,64,4096]{3,2,1,0:T(8,128)} %param.17) | copy-start | bytes 3145732
  1.9 2.2 %copy-start.7 = (s32[32]{0:T(128)S(1)}, s32[32]{0:T(128)}, u32[]{:S(2)}) copy-start(s32[32]{0:T(128)} %counts_ref.1) | copy-start | bytes 388
  1.9 4.0 %copy-start.1 = (f32[1,1,64,4096]{3,2,1,0:T(8,128)S(1)}, f32[1,1,64,4096]{3,2,1,0:T(8,128)}, u32[]{:S(2)}) copy-start(f32[1,1,64,4096]{3,2,1,0:T(8,128)} %param.17) | copy-start | bytes 3145732
  1.9 21.1 %copy-start.2 = (s32[16,32,512]{2,1,0:T(8,128)S(1)}, s32[16,32,512]{2,1,0:T(8,128)}, u32[]{:S(2)}) copy-start(s32[16,32,512]{2,1,0:T(8,128)} %chosen_ref.1) | copy-start | bytes 3145732
  1.9 3.9 %collective-permute-start.30 = (f32[32,4096]{1,0:T(8,128)S(1)}, f32[32,4096]{1,0:T(8,128)S(1)}, u32[]{:S(2)}, u32[]{:S(2)}) collective-permute-start(f32[32,4096]{1,0:T(8,128)S(1)} %other_half.1), channel_id=1, source_target_pairs={{0,1},{1,0},{2,3},{3,2},{4,5},{5,4},{6,7},{7,6},{8,9},{9,8},{10,11... | collective-permute-start | bytes 1572872 | tf_op jit(solution)/shard_map/ppermute | solution.py:233
  5.9 17.1 %copy-start.3 = (f32[1,64,512]{2,1,0:T(8,128)S(1)}, f32[1,64,512]{2,1,0:T(8,128)}, u32[]{:S(2)}) copy-start(f32[1,64,512]{2,1,0:T(8,128)} %momentum_ref.1) | copy-start | bytes 393220
  5.9 17.1 %copy-start.5 = (f32[64,64]{1,0:T(8,128)S(1)}, f32[64,64]{1,0:T(8,128)}, u32[]{:S(2)}) copy-start(f32[64,64]{1,0:T(8,128)} %constant.35.clone.table_ref) | copy-start | bytes 49156
  5.9 17.9 %collective-permute-start.31 = (f32[8,4096]{1,0:T(8,128)S(1)}, f32[8,4096]{1,0:T(8,128)S(1)}, u32[]{:S(2)}, u32[]{:S(2)}) collective-permute-start(f32[8,4096]{1,0:T(8,128)S(1)} %get-tuple-element.252), channel_id=1, source_target_pairs={{0,2},{1,31},{2,0},{3,5},{4,6},{5,3},{6,4},{7,9},{8,10},{9,7},{10,... | collective-permute-start | bytes 393224 | tf_op jit(solution)/shard_map/ppermute | solution.py:261
  9.9 13.9 %collective-permute-start.32 = (f32[8,4096]{1,0:T(8,128)S(1)}, f32[8,4096]{1,0:T(8,128)S(1)}, u32[]{:S(2)}, u32[]{:S(2)}) collective-permute-start(f32[8,4096]{1,0:T(8,128)S(1)} %get-tuple-element.253), channel_id=1, source_target_pairs={{0,30},{1,3},{2,4},{3,1},{4,2},{5,7},{6,8},{7,5},{8,6},{9,11},{10,... | collective-permute-start | bytes 393224 | tf_op jit(solution)/shard_map/ppermute | solution.py:261
  20.4 7.8 %collective-permute-start.33 = (f32[8,4096]{1,0:T(8,128)S(1)}, f32[8,4096]{1,0:T(8,128)S(1)}, u32[]{:S(2)}, u32[]{:S(2)}) collective-permute-start(f32[8,4096]{1,0:T(8,128)S(1)} %get-tuple-element.254), channel_id=1, source_target_pairs={{0,4},{1,29},{2,6},{3,31},{4,0},{5,9},{6,2},{7,11},{8,12},{9,5},{1... | collective-permute-start | bytes 393224 | tf_op jit(solution)/shard_map/ppermute | solution.py:261
  28.3 17.1 %collective-permute-start.3 = (f32[8,1408]{1,0:T(8,128)S(1)}, f32[8,1408]{1,0:T(8,128)S(1)}, u32[]{:S(2)}, u32[]{:S(2)}) collective-permute-start(f32[8,1408]{1,0:T(8,128)S(1)} %get-tuple-element.148), channel_id=1, source_target_pairs={{0,16},{1,17},{2,18},{3,19},{4,20},{5,21},{6,22},{7,23},{8,24},{9,... | collective-permute-start | bytes 135176 | tf_op jit(solution)/shard_map/cond/branch_1_fun/ppermute | solution.py:155
  34.6 10.7 %collective-permute-start.4 = (f32[8,1408]{1,0:T(8,128)S(1)}, f32[8,1408]{1,0:T(8,128)S(1)}, u32[]{:S(2)}, u32[]{:S(2)}) collective-permute-start(f32[8,1408]{1,0:T(8,128)S(1)} %get-tuple-element.149), channel_id=1, source_target_pairs={{0,8},{1,25},{2,10},{3,27},{4,12},{5,29},{6,14},{7,31},{8,0},{9,17... | collective-permute-start | bytes 135176 | tf_op jit(solution)/shard_map/cond/branch_1_fun/ppermute | solution.py:155
  42.4 10.0 %collective-permute-start.5 = (f32[8,1408]{1,0:T(8,128)S(1)}, f32[8,1408]{1,0:T(8,128)S(1)}, u32[]{:S(2)}, u32[]{:S(2)}) collective-permute-start(f32[8,1408]{1,0:T(8,128)S(1)} %get-tuple-element.150), channel_id=1, source_target_pairs={{0,24},{1,9},{2,26},{3,11},{4,28},{5,13},{6,30},{7,15},{8,16},{9,1... | collective-permute-start | bytes 135176 | tf_op jit(solution)/shard_map/cond/branch_1_fun/ppermute | solution.py:155
  52.6 9.2 %copy-start.6 = (f32[64,64]{1,0:T(8,128)S(1)}, f32[64,64]{1,0:T(8,128)}, u32[]{:S(2)}) copy-start(f32[64,64]{1,0:T(8,128)} %constant.36.clone.back_ref) | copy-start | bytes 49156
  73.0 12.5 %copy-start.4 = (f32[64,512]{1,0:T(8,128)S(1)}, f32[64,512]{1,0:T(8,128)}, u32[]{:S(2)}) copy-start(f32[64,512]{1,0:T(8,128)} %weights_ref.1) | copy-start | bytes 393220
